TPU v7x, 128 devices: a whole 4x4x4 slice. The times are simulated.
128 devices in a mesh: wide: 16 (over y, x_lo, core), narrow: 8 (over x_hi, z).
Axes of the slice: x: 4 (x_hi: 2, x_lo: 2; x = x_hi * 2 + x_lo), y: 4, z: 4, core: 2. Of those that a mesh axis runs over, the one named last changes fastest.
Arguments:
- inputs: bfloat16 [1024, 8192], P('wide', 'narrow'), may hold values from -6 to 6
- grad_out: bfloat16 [1024, 8192], P('wide', 'narrow'), may hold values from -6 to 6
- w_gate: bfloat16 [8192, 29568], P('narrow', 'wide'), may hold values from -0.0625 to 0.0625
- w_up: bfloat16 [8192, 29568], P('narrow', 'wide'), may hold values from -0.0625 to 0.0625
- w_down: bfloat16 [29568, 8192], P('wide', 'narrow'), may hold values from -0.03125 to 0.03125
Outputs:
- grad_input: bfloat16 [1024, 8192], P('wide', 'narrow')
- grad_gate: bfloat16 [8192, 29568], P('narrow', 'wide')
- grad_up: bfloat16 [8192, 29568], P('narrow', 'wide')
- grad_down: bfloat16 [29568, 8192], P('wide', 'narrow')
All inputs are finite; a program needn't handle non-finite values.
Results may differ from a plain program's by a relative error of at most 0.033.
Values may be sent and summed in bfloat16 or wider, within the bound.
No kernel may reach another device: no remote copies, remote signals or barrier semaphores. Data moves between devices by JAX's collectives and lax.ppermute only.
A program may use at most 128 MiB of HBM per device.

v0:
```python
import jax
import jax.numpy as jnp
from jax import lax
from jax.sharding import PartitionSpec as P


def swiglu_backward(gate_sum, up_sum, hidden_grad):
    sigmoid_gate = jax.nn.sigmoid(gate_sum)
    hidden = (gate_sum * sigmoid_gate * up_sum).astype(jnp.bfloat16)
    gate_grad = (
        hidden_grad * up_sum * sigmoid_gate * (1.0 + gate_sum * (1.0 - sigmoid_gate))
    ).astype(jnp.bfloat16)
    up_grad = (hidden_grad * gate_sum * sigmoid_gate).astype(jnp.bfloat16)
    return (hidden, gate_grad, up_grad)


def body(inputs, grad_out, w_gate, w_up, w_down):
    whole_input, whole_grad = (
        lax.all_gather(inputs, "wide", axis=0, tiled=True),
        lax.all_gather(grad_out, "wide", axis=0, tiled=True),
    )
    last_contract = (((1,), (1,)), ((), ()))
    row_contract = (((0,), (0,)), ((), ()))
    hidden_width = w_gate.shape[1]
    row_block = whole_input
    joined = lax.psum_scatter(
        jnp.concatenate(
            [
                jnp.dot(row_block, w_gate, preferred_element_type=jnp.float32),
                jnp.dot(row_block, w_up, preferred_element_type=jnp.float32),
            ],
            1,
        ).astype(jnp.bfloat16),
        "narrow",
        scatter_dimension=0,
        tiled=True,
    ).astype(jnp.float32)
    gate_sum = joined[:, :hidden_width]
    up_sum = joined[:, hidden_width:]
    row_block = whole_grad
    hidden_grad = lax.psum_scatter(
        lax.dot_general(
            row_block, w_down, last_contract, preferred_element_type=jnp.float32
        ).astype(jnp.bfloat16),
        "narrow",
        scatter_dimension=0,
        tiled=True,
    ).astype(jnp.float32)
    hidden, gate_grad, up_grad = swiglu_backward(gate_sum, up_sum, hidden_grad)
    hidden_all, gate_all, up_all = (
        lax.all_gather(hidden, "narrow", axis=0, tiled=True),
        lax.all_gather(gate_grad, "narrow", axis=0, tiled=True),
        lax.all_gather(up_grad, "narrow", axis=0, tiled=True),
    )
    grad_input = lax.psum_scatter(
        (
            lax.dot_general(gate_all, w_gate, last_contract, preferred_element_type=jnp.float32)
            + lax.dot_general(up_all, w_up, last_contract, preferred_element_type=jnp.float32)
        ).astype(jnp.bfloat16),
        "wide",
        scatter_dimension=0,
        tiled=True,
    )
    grad_gate = lax.dot_general(
        whole_input, gate_all, row_contract, preferred_element_type=jnp.float32
    ).astype(jnp.bfloat16)
    grad_up = lax.dot_general(
        whole_input, up_all, row_contract, preferred_element_type=jnp.float32
    ).astype(jnp.bfloat16)
    grad_down = lax.dot_general(
        hidden_all, whole_grad, row_contract, preferred_element_type=jnp.float32
    ).astype(jnp.bfloat16)
    return (grad_input, grad_gate, grad_up, grad_down)


def solution(mesh):
    return jax.shard_map(
        body,
        mesh=mesh,
        in_specs=(
            P("wide", "narrow"),
            P("wide", "narrow"),
            P("narrow", "wide"),
            P("narrow", "wide"),
            P("wide", "narrow"),
        ),
        out_specs=(
            P("wide", "narrow"),
            P("narrow", "wide"),
            P("narrow", "wide"),
            P("wide", "narrow"),
        ),
        check_vma=False,
    )
```

profile of v0, /device:TPU:1, one launch (start us, length us, event | category | flops | bytes accessed | tf_op | source)
XLA Modules:
  0.0 564.3 jit_solution(5933361544348469252)
XLA Ops:
  7.2 0.0 all-gather.6.cloned.1.call-start
  7.2 0.7 all-gather.6.cloned.1.call-update
  7.9 0.0 all-gather.8.cloned.1.call-start
  7.9 0.7 all-gather.8.cloned.1.call-update
  8.6 0.0 reduce-scatter.10.cloned.1.call-start
  8.7 38.7 %all-gather.6.cloned.1.call-done = bf16[1024,1024]{1,0:T(8,128)(2,1)} async-done(((bf16[64,1024]{1,0:T(8,128)(2,1)}), bf16[1024,1024]{1,0:T(8,128)(2,1)}) %all-gather.6.cloned.1.call-update) | async-done | bytes 2097168 | tf_op jit(solution)/shard_map/all_gather | solution.py:20
  47.4 8.7 %convolution_convert_fusion.3 = bf16[1024,1848]{0,1:T(8,128)(2,1)} fusion(bf16[1024,1024]{1,0:T(8,128)(2,1)} %all-gather.6.cloned.1.call-done, bf16[1848,1024]{1,0:T(8,128)(2,1)} %param.9), kind=kOutput, calls=%fused_computation.7 | convolution fusion | flops 3877429248 | bytes 9666560 | tf_op jit(solution)/shard_map/dot_general | solution.py:42
  56.1 6.1 %copy.9 = bf16[1024,1848]{1,0:T(8,128)(2,1)} copy(bf16[1024,1848]{0,1:T(8,128)(2,1)} %convolution_convert_fusion.3) | data formatting | bytes 7569408
  62.2 0.0 reduce-scatter.10.cloned.1.call-update
  62.3 0.0 reduce-scatter.12.cloned.1.call-start
  62.3 20.8 %all-gather.8.cloned.1.call-done = bf16[1024,1024]{1,0:T(8,128)(2,1)} async-done(((bf16[64,1024]{1,0:T(8,128)(2,1)}), bf16[1024,1024]{1,0:T(8,128)(2,1)}) %all-gather.8.cloned.1.call-update) | async-done | bytes 2097168 | tf_op jit(solution)/shard_map/all_gather | solution.py:19
  83.1 0.0 copy-start
  83.1 0.0 copy-start.3
  83.1 8.9 %convolution_convert_fusion.1 = bf16[1024,1848]{0,1:T(8,128)(2,1)} fusion(bf16[1024,1024]{1,0:T(8,128)(2,1)} %all-gather.8.cloned.1.call-done, bf16[1024,1848]{0,1:T(8,128)(2,1)} %param.8), kind=kOutput, calls=%fused_computation.5 | convolution fusion | flops 3877429248 | bytes 9666560 | tf_op jit(solution)/shard_map/dot_general | solution.py:30
  92.0 0.0 copy-done
  92.0 0.0 copy-done.3
  92.0 5.7 %convolution_convert_fusion.2 = bf16[1024,1848]{0,1:T(8,128)(2,1)} fusion(bf16[1024,1024]{1,0:T(8,128)(2,1)S(1)} %copy-done.3, bf16[1024,1848]{0,1:T(8,128)(2,1)S(1)} %copy-done), kind=kOutput, calls=%fused_computation.6 | convolution fusion | flops 3877429248 | bytes 9666560 | tf_op jit(solution)/shard_map/dot_general | solution.py:29
  97.7 7.2 %pad_maximum_fusion = bf16[1024,3696]{0,1:T(8,128)(2,1)} fusion(bf16[1024,1848]{0,1:T(8,128)(2,1)} %convolution_convert_fusion.1, bf16[1024,1848]{0,1:T(8,128)(2,1)} %convolution_convert_fusion.2), kind=kLoop, calls=%fused_computation | loop fusion | flops 15138816 | bytes 15138816 | tf_op jit(solution)/shard_map/concatenate | solution.py:27
  104.9 10.4 %copy.11 = bf16[1024,3696]{1,0:T(8,128)(2,1)} copy(bf16[1024,3696]{0,1:T(8,128)(2,1)} %pad_maximum_fusion) | data formatting | bytes 15138816
  115.2 0.0 reduce-scatter.12.cloned.1.call-update
  115.3 0.2 all-gather.10.cloned.1.call-start
  115.5 53.6 %reduce-scatter.10.cloned.1.call-done = bf16[128,1848]{1,0:T(8,128)(2,1)} async-done(((bf16[1024,1848]{1,0:T(8,128)(2,1)}), bf16[128,1848]{1,0:T(8,128)(2,1)}) %reduce-scatter.10.cloned.1.call-update) | async-done | bytes 473104
  169.1 1.3 copy.10
  170.3 112.2 %reduce-scatter.12.cloned.1.call-done = bf16[128,3696]{1,0:T(8,128)(2,1)} async-done(((bf16[1024,3696]{1,0:T(8,128)(2,1)}), bf16[128,3696]{1,0:T(8,128)(2,1)}) %reduce-scatter.12.cloned.1.call-update) | async-done | bytes 946192
  282.5 2.0 copy.12
  284.6 0.1 convert_element_type.39
  284.7 1.7 fusion.4
  286.4 0.0 all-gather.10.cloned.1.call-update
  286.4 0.0 all-gather.12.cloned.1.call-start
  286.4 0.5 all-gather.12.cloned.1.call-update
  287.0 0.0 all-gather.14.cloned.1.call-start
  287.0 0.7 all-gather.14.cloned.1.call-update
  287.7 0.0 reduce-scatter.8.cloned.1.call-start
  287.8 66.7 %all-gather.10.cloned.1.call-done = bf16[1024,1848]{0,1:T(8,128)(2,1)} async-done(((bf16[128,1848]{0,1:T(8,128)(2,1)}), bf16[1024,1848]{0,1:T(8,128)(2,1)}) %all-gather.10.cloned.1.call-update) | async-done | bytes 3784720 | tf_op jit(solution)/shard_map/all_gather | solution.py:52
  354.5 9.7 %fusion.5 = f32[1024,1024]{1,0:T(8,128)} fusion(bf16[1024,1848]{0,1:T(8,128)(2,1)} %all-gather.10.cloned.1.call-done, bf16[1024,1848]{0,1:T(8,128)(2,1)} %param.7), kind=kOutput, calls=%fused_computation.17 | convolution fusion | flops 3875536896 | bytes 11763712 | tf_op jit(solution)/shard_map/dot_general | solution.py:57
  364.2 60.7 %all-gather.12.cloned.1.call-done = bf16[1024,1848]{0,1:T(8,128)(2,1)} async-done(((bf16[128,1848]{0,1:T(8,128)(2,1)}), bf16[1024,1848]{0,1:T(8,128)(2,1)}) %all-gather.12.cloned.1.call-update) | async-done | bytes 3784720 | tf_op jit(solution)/shard_map/all_gather | solution.py:53
  424.9 10.3 %add_convert_fusion = bf16[1024,1024]{1,0:T(8,128)(2,1)} fusion(f32[1024,1024]{1,0:T(8,128)} %fusion.5, bf16[1024,1848]{0,1:T(8,128)(2,1)} %all-gather.12.cloned.1.call-done, bf16[1024,1848]{0,1:T(8,128)(2,1)} %param.8), kind=kOutput, calls=%fused_computation.1 | convolution fusion | flops 3877634048 | bytes 13860864 | tf_op jit(solution)/shard_map/dot_general | solution.py:58
  435.2 0.0 reduce-scatter.8.cloned.1.call-update
  435.3 0.0 copy-start.1
  435.3 0.0 copy-start.4
  435.3 8.2 %convert_bitcast_fusion = bf16[1024,1848]{0,1:T(8,128)(2,1)} fusion(bf16[1024,1848]{0,1:T(8,128)(2,1)} %all-gather.12.cloned.1.call-done, bf16[1024,1024]{1,0:T(8,128)(2,1)S(1)} %copy-done.3), kind=kOutput, calls=%fused_computation.2 | convolution fusion | flops 3877429248 | bytes 9666560 | tf_op jit(solution)/shard_map/dot_general | solution.py:67
  443.5 0.0 copy-done.1
  443.5 0.0 copy-done.4
  443.5 5.6 convert_bitcast_fusion.1
  449.1 45.9 %all-gather.14.cloned.1.call-done = bf16[1024,1848]{0,1:T(8,128)(2,1)} async-done(((bf16[128,1848]{0,1:T(8,128)(2,1)}), bf16[1024,1848]{0,1:T(8,128)(2,1)}) %all-gather.14.cloned.1.call-update) | async-done | bytes 3784720 | tf_op jit(solution)/shard_map/all_gather | solution.py:51
  494.9 0.0 copy-done.2
  494.9 7.6 %convolution_convert_fusion = bf16[1848,1024]{1,0:T(8,128)(2,1)} fusion(bf16[1024,1848]{0,1:T(8,128)(2,1)} %all-gather.14.cloned.1.call-done, bf16[1024,1024]{1,0:T(8,128)(2,1)S(1)} %copy-done.2), kind=kOutput, calls=%fused_computation.4 | convolution fusion | flops 3877429248 | bytes 9666560 | tf_op jit(solution)/shard_map/dot_general | solution.py:70
  502.5 54.9 %reduce-scatter.8.cloned.1.call-done = bf16[64,1024]{1,0:T(8,128)(2,1)} async-done(((bf16[1024,1024]{1,0:T(8,128)(2,1)}), bf16[64,1024]{1,0:T(8,128)(2,1)}) %reduce-scatter.8.cloned.1.call-update) | async-done | bytes 131088 | tf_op jit(solution)/shard_map/reduce_scatter | solution.py:55
  (1 shorter events, 0.0 us)
Async XLA Ops:
  7.2 40.2 %all-gather.6.cloned.1.call-start = ((), (), s32[]{:S(2)}) async-start(), calls=%async_computation.3 | async-start | bytes 2228224 | tf_op jit(solution)/shard_map/all_gather | solution.py:20
  7.9 75.2 %all-gather.8.cloned.1.call-start = ((), (), s32[]{:S(2)}) async-start(), calls=%async_computation.4 | async-start | bytes 2228224 | tf_op jit(solution)/shard_map/all_gather | solution.py:19
  8.6 160.4 %reduce-scatter.10.cloned.1.call-start = ((), (), s32[]{:S(2)}) async-start(), calls=%async_computation.9 | async-start | bytes 4423680
  62.3 220.2 %reduce-scatter.12.cloned.1.call-start = ((), (), s32[]{:S(2)}) async-start(), calls=%async_computation.10 | async-start | bytes 8552448
  83.1 8.9 %copy-start = (bf16[1024,1848]{0,1:T(8,128)(2,1)S(1)}, bf16[1024,1848]{0,1:T(8,128)(2,1)}, u32[]{:S(2)}) copy-start(bf16[1024,1848]{0,1:T(8,128)(2,1)} %param.7) | copy-start | bytes 11354116
  83.1 8.9 %copy-start.3 = (bf16[1024,1024]{1,0:T(8,128)(2,1)S(1)}, bf16[1024,1024]{1,0:T(8,128)(2,1)}, u32[]{:S(2)}) copy-start(bf16[1024,1024]{1,0:T(8,128)(2,1)} %all-gather.8.cloned.1.call-done) | copy-start | bytes 6291460
  115.3 239.2 %all-gather.10.cloned.1.call-start = ((), (), s32[]{:S(2)}) async-start(), calls=%async_computation.5 | async-start | bytes 4257792 | tf_op jit(solution)/shard_map/all_gather | solution.py:52
  286.4 138.5 %all-gather.12.cloned.1.call-start = ((), (), s32[]{:S(2)}) async-start(), calls=%async_computation.6 | async-start | bytes 4257792 | tf_op jit(solution)/shard_map/all_gather | solution.py:53
  287.0 208.0 %all-gather.14.cloned.1.call-start = ((), (), s32[]{:S(2)}) async-start(), calls=%async_computation.8 | async-start | bytes 4257792 | tf_op jit(solution)/shard_map/all_gather | solution.py:51
  287.7 269.7 %reduce-scatter.8.cloned.1.call-start = ((), (), s32[]{:S(2)}) async-start(), calls=%async_computation.7 | async-start | bytes 2228224 | tf_op jit(solution)/shard_map/reduce_scatter | solution.py:55
  435.3 8.2 %copy-start.1 = (bf16[1024,1848]{0,1:T(8,128)(2,1)S(1)}, bf16[1024,1848]{0,1:T(8,128)(2,1)}, u32[]{:S(2)}) copy-start(bf16[1024,1848]{0,1:T(8,128)(2,1)} %all-gather.10.cloned.1.call-done) | copy-start | bytes 11354116
  435.3 8.2 %copy-start.4 = (bf16[1024,1024]{1,0:T(8,128)(2,1)S(1)}, bf16[1024,1024]{1,0:T(8,128)(2,1)}, u32[]{:S(2)}) copy-start(bf16[1024,1024]{1,0:T(8,128)(2,1)} %all-gather.8.cloned.1.call-done) | copy-start | bytes 6291460
  443.5 51.4 %copy-start.2 = (bf16[1024,1024]{1,0:T(8,128)(2,1)S(1)}, bf16[1024,1024]{1,0:T(8,128)(2,1)}, u32[]{:S(2)}) copy-start(bf16[1024,1024]{1,0:T(8,128)(2,1)} %all-gather.6.cloned.1.call-done) | copy-start | bytes 6291460
Sparse Core Ops, SparseCore 0:
  9.7 37.6 all-gather.5
  49.1 33.9 all-gather.7
  87.0 81.9 reduce-scatter.9
  173.3 109.1 reduce-scatter.11
  286.5 67.9 all-gather.9
  357.1 67.7 all-gather.11
  427.1 67.7 all-gather.13
  497.9 59.5 reduce-scatter.7
where the time goes:
time: 567 us; the launch traced here: 564 us
  waiting for transfers between devices  456 us (80%)
  matrix products  64.7 us (11%)
  local copies, waits for them, and re-layouts  19.8 us (3%)
  between operations  14.2 us (3%)
  other arithmetic  8.97 us (2%)
    unnamed x10, waiting for transfers between devices  168 us
    all_gather x1, waiting for transfers between devices, body(): lax.all_gather(gate_grad, 'narrow', axis=0, tiled=True)  66.7 us
    all_gather x1, waiting for transfers between devices, body(): lax.all_gather(up_grad, 'narrow', axis=0, tiled=True)  60.7 us
    reduce_scatter x1, waiting for transfers between devices, body(): lax.psum_scatter((lax.dot_general(gate_all, w_gate, last_contract, prefer...  54.9 us
    all_gather x1, waiting for transfers between devices, body(): lax.all_gather(hidden, 'narrow', axis=0, tiled=True)  45.9 us
    all_gather x1, waiting for transfers between devices, body(): lax.all_gather(grad_out, 'wide', axis=0, tiled=True)  38.7 us
    all_gather x1, waiting for transfers between devices, body(): lax.all_gather(inputs, 'wide', axis=0, tiled=True)  20.8 us
    unnamed x14, local copies, waits for them, and re-layouts  19.8 us
  transfers between devices with their start and end apart: 8, of which 8 were waited for; matrix products, arithmetic and copies ran while one was open for 16% of the time, Pallas kernels for 0%

commit v1 on v0

v1 whole, which is shorter than its diff:
```python
import functools

import jax
import jax.numpy as jnp
from jax import lax
from jax.experimental import pallas as pl
from jax.experimental.pallas import tpu as pltpu
from jax.sharding import PartitionSpec as P

BF = jnp.bfloat16
F32 = jnp.float32
D = 1024
T = 1024
HALF = T // 2
B = 128
FF = 1848
R = 464
Q = 4
N_BLOCK = 256
VMEM = 48 * 1024 * 1024

NT = (((1,), (1,)), ((), ()))
NN = (((1,), (0,)), ((), ()))
TN = (((0,), (0,)), ((), ()))


def dot(a, b, dims):
    return lax.dot_general(a, b, dims, preferred_element_type=F32)


def shape(*dims, dtype=BF):
    return jax.ShapeDtypeStruct(dims, dtype)


def params():
    return pltpu.CompilerParams(vmem_limit_bytes=VMEM)


def cost(flops, nbytes):
    return pl.CostEstimate(flops=int(flops), bytes_accessed=int(nbytes), transcendentals=0)


def narrow_move(value, dxh, dz):
    pairs = [
        (xh * 4 + z, ((xh + dxh) % 2) * 4 + (z + dz) % 4) for xh in range(2) for z in range(4)
    ]
    return lax.ppermute(value, "narrow", pairs)


def wide_move(value, dy, dxl, dc):
    pairs = [
        (y * 4 + xl * 2 + c, ((y + dy) % 4) * 4 + ((xl + dxl) % 2) * 2 + (c + dc) % 2)
        for y in range(4)
        for xl in range(2)
        for c in range(2)
    ]
    return lax.ppermute(value, "wide", pairs)


def first_kernel(is_x, at, xo, xt, go, gt, wg, wu, wd, *rest):
    outs, (xs, gs) = rest[:-2], rest[-2:]
    step = pl.program_id(0)
    xh = at[0]
    own = pl.multiple_of(xh * B, B)
    other = pl.multiple_of((1 - xh) * B, B)
    xs[pl.ds(own, B), :] = xo[0]
    xs[pl.ds(other, B), :] = xt[0]
    gs[pl.ds(own, B), :] = go[0]
    gs[pl.ds(other, B), :] = gt[0]
    for i, (w, src) in enumerate(((wg, xs), (wu, xs), (wd, gs))):
        res = dot(w[...], src[...], NT).astype(BF)
        near, far = res[:, :B], res[:, B:]
        if is_x:
            send, keep = outs
            keep[0, i] = near
            send[0, i] = far
        else:
            own_out, mid1, mid3, a2, b2 = outs
            for k, out in ((0, own_out), (1, mid1), (3, mid3)):

                @pl.when(step == k)
                def _(out=out):
                    out[0, i] = near
                    out[1, i] = far

            @pl.when(step == 2)
            def _():
                a2[i] = near
                b2[i] = far


def first(q, is_x, at, xg_o, xg_t, wg, wu, wd):
    def tokens(which):
        return pl.BlockSpec((1, B, D), lambda s, at: (which, lax.rem(at[1] + s, 4), 0))

    weight = pl.BlockSpec((R, D), lambda s, at: (q, 0))
    if is_x:
        out_shape = [shape(4, 3, R, B)] * 2
        out_specs = [pl.BlockSpec((1, 3, R, B), lambda s, at: (s, 0, 0, 0))] * 2
    else:
        out_shape = [shape(2, 3, R, B)] * 3 + [shape(3, R, B)] * 2
        out_specs = [pl.BlockSpec((2, 3, R, B), lambda s, at: (0, 0, 0, 0))] * 3 + [
            pl.BlockSpec((3, R, B), lambda s, at: (0, 0, 0))
        ] * 2
    return pl.pallas_call(
        functools.partial(first_kernel, is_x),
        out_shape=out_shape,
        grid_spec=pltpu.PrefetchScalarGridSpec(
            num_scalar_prefetch=1,
            grid=(4,),
            in_specs=[tokens(0), tokens(0), tokens(1), tokens(1), weight, weight, weight],
            out_specs=out_specs,
            scratch_shapes=[pltpu.VMEM((2 * B, D), BF)] * 2,
        ),
        compiler_params=params(),
        cost_estimate=cost(3 * 2 * R * T * D, 3 * R * D * 2 + 4 * T * D + 3 * R * T * 2),
        name=f"first{q}",
    )(at, xg_o, xg_t, xg_o, xg_t, wg, wu, wd)


def x_sum_kernel(keep, recv, s1, s2, s3):
    for k, out in ((1, s1), (2, s2), (3, s3)):
        out[0] = (keep[k, 0].astype(F32) + recv[k, 0].astype(F32)).astype(BF)


def x_sum(keep, recv):
    block = pl.BlockSpec((4, 1, R, B), lambda i: (0, i, 0, 0))
    return pl.pallas_call(
        x_sum_kernel,
        out_shape=[shape(3, R, B)] * 3,
        grid=(3,),
        in_specs=[block] * 2,
        out_specs=[pl.BlockSpec((1, R, B), lambda i: (i, 0, 0))] * 3,
        compiler_params=params(),
        cost_estimate=cost(3 * 3 * R * B, 11 * 3 * R * B * 2),
        name="x_sum",
    )(keep, recv)


def z_mid_kernel(mid1, ra, mid3, rb, out1, out3):
    out1[0, 0] = (mid1[0, 0].astype(F32) + ra[0].astype(F32)).astype(BF)
    out3[0, 0] = (mid3[0, 0].astype(F32) + rb[0].astype(F32)).astype(BF)


def z_mid(mid1, ra, mid3, rb):
    first_half = pl.BlockSpec((1, 1, R, B), lambda i: (0, i, 0, 0))
    second_half = pl.BlockSpec((1, 1, R, B), lambda i: (1, i, 0, 0))
    one = pl.BlockSpec((1, R, B), lambda i: (i, 0, 0))
    return pl.pallas_call(
        z_mid_kernel,
        out_shape=[shape(2, 3, R, B)] * 2,
        grid=(3,),
        in_specs=[first_half, one, second_half, one],
        out_specs=[first_half, second_half],
        input_output_aliases={0: 0, 2: 1},
        compiler_params=params(),
        cost_estimate=cost(2 * 3 * R * B, 6 * 3 * R * B * 2),
        name="z_mid",
    )(mid1, ra, mid3, rb)


def z_far_kernel(a, b, c, out):
    out[0] = (a[0, 0].astype(F32) + b[0, 0].astype(F32) + c[0, 0].astype(F32)).astype(BF)


def z_far(own, u, v):
    half = pl.BlockSpec((1, 1, R, B), lambda i: (1, i, 0, 0))
    return pl.pallas_call(
        z_far_kernel,
        out_shape=shape(3, R, B),
        grid=(3,),
        in_specs=[half] * 3,
        out_specs=pl.BlockSpec((1, R, B), lambda i: (i, 0, 0)),
        compiler_params=params(),
        cost_estimate=cost(2 * 3 * R * B, 4 * 3 * R * B * 2),
        name="z_far",
    )(own, u, v)


def swiglu_kernel(*refs):
    ins, (gu, hid) = refs[:-2], refs[-2:]

    def total(i):
        acc = None
        for ref in ins:
            term = (ref[0, i] if len(ref.shape) == 4 else ref[i]).astype(F32)
            acc = term if acc is None else acc + term
        return acc

    gate, up, grad = total(0), total(1), total(2)
    sig = jax.nn.sigmoid(gate)
    silu = gate * sig
    hid[...] = (silu * up).astype(BF)
    gu[0] = (grad * up * sig * (1.0 + gate * (1.0 - sig))).astype(BF)
    gu[1] = (grad * silu).astype(BF)


def swiglu(terms):
    specs = [
        pl.BlockSpec((1, 3, R, B), lambda i: (0, 0, 0, 0))
        if t.ndim == 4
        else pl.BlockSpec((3, R, B), lambda i: (0, 0, 0))
        for t in terms
    ]
    return pl.pallas_call(
        swiglu_kernel,
        out_shape=[shape(2, R, B), shape(R, B)],
        grid=(1,),
        in_specs=specs,
        out_specs=[
            pl.BlockSpec((2, R, B), lambda i: (0, 0, 0)),
            pl.BlockSpec((R, B), lambda i: (0, 0)),
        ],
        compiler_params=params(),
        cost_estimate=cost(40 * R * B, (len(terms) + 1) * 3 * R * B * 2),
        name="swiglu",
    )(*terms)


def scatter_x(send, keep):
    recv = narrow_move(send, 1, 0)
    s1, s2, s3 = x_sum(keep, recv)
    terms = [narrow_move(s1, 0, 1), narrow_move(s3, 0, 3), narrow_move(s2, 0, 2)]
    return [keep, recv, *terms]


def scatter_z(own, mid1, mid3, a2, b2):
    ra = narrow_move(a2, 0, 1)
    rb = narrow_move(b2, 0, 3)
    mid1, mid3 = z_mid(mid1, ra, mid3, rb)
    u = narrow_move(mid1, 0, 1)
    v = narrow_move(mid3, 0, 3)
    far = narrow_move(z_far(own, u, v), 1, 0)
    return [own, u, v, far]


def gather_x(block):
    before = narrow_move(block, 0, 1)
    after = narrow_move(block, 0, 3)
    across = narrow_move(block, 0, 2)
    far = narrow_move(jnp.stack([block, after, across, before]), 1, 0)
    near = [(block, None, 0, 0), (after, None, 0, 1), (across, None, 0, 2), (before, None, 0, 3)]
    return near + [(far, k, 1, k) for k in range(4)]


def gather_z(block):
    pair = jnp.stack([block, narrow_move(block, 1, 0)])
    before = narrow_move(pair, 0, 1)
    after = narrow_move(pair, 0, 3)
    near = narrow_move(before[0], 0, 1)
    far = narrow_move(after[1], 0, 3)
    blocks = [(near, None, 0, 2), (far, None, 1, 2)]
    for dz, source in ((0, pair), (1, after), (3, before)):
        blocks += [(source, k, k, dz) for k in range(2)]
    return blocks


def distinct(blocks):
    arrays, places = [], []
    for array, lead, dxh, dz in blocks:
        for n, seen in enumerate(arrays):
            if seen is array:
                break
        else:
            n = len(arrays)
            arrays.append(array)
        places.append((n, lead, dxh, dz))
    return arrays, places


def place(at, refs, places, i, target, rows):
    for n, lead, dxh, dz in places:
        value = refs[n][i] if lead is None else refs[n][lead, i]
        if rows is not None:
            value = jnp.where(rows, value, jnp.zeros_like(value))
        column = (lax.rem(at[0] + dxh, 2) * 4 + lax.rem(at[1] + dz, 4)) * B
        target[:, pl.ds(pl.multiple_of(column, B), B)] = value


def valid_rows(q, width):
    valid = FF - q * R
    if valid >= R:
        return None
    return lax.broadcasted_iota(jnp.int32, (R, width), 0) < valid


def whole(array):
    rank = array.ndim
    return pl.BlockSpec(array.shape, lambda *_: (0,) * rank)


def last_kernel(q, places, n_arrays, has_prev, is_end, at, *refs):
    refs = list(refs)
    arrays = [refs.pop(0) for _ in range(n_arrays)]
    xo, xt, wg, wu = [refs.pop(0) for _ in range(4)]
    if has_prev:
        acc_o, acc_t = refs.pop(0), refs.pop(0)
        refs.pop(0), refs.pop(0)
    gg, gu, out_o, out_t, ag, au = refs

    @pl.when(pl.program_id(0) == 0)
    def _():
        rows = valid_rows(q, B)
        place(at, arrays, places, 0, ag, rows)
        place(at, arrays, places, 1, au, rows)

    for out, act in ((gg, ag), (gu, au)):
        out[...] = (dot(act[:, :HALF], xo[0], NN) + dot(act[:, HALF:], xt[0], NN)).astype(BF)
    rows = valid_rows(q, N_BLOCK)
    vg, vu = wg[...], wu[...]
    if rows is not None:
        vg = jnp.where(rows, vg, jnp.zeros_like(vg))
        vu = jnp.where(rows, vu, jnp.zeros_like(vu))
    for k, out in enumerate((out_o, out_t)):
        part = slice(k * HALF, (k + 1) * HALF)
        total = dot(ag[:, part], vg, TN) + dot(au[:, part], vu, TN)
        if has_prev:
            total = total + (acc_o, acc_t)[k][...]
        out[...] = total.astype(out.dtype)


def last(q, is_end, at, blocks, xg_o, xg_t, wg, wu, prev):
    arrays, places = distinct(blocks)
    tokens = pl.BlockSpec((1, HALF, N_BLOCK), lambda n, at: (0, 0, n))
    weight = pl.BlockSpec((R, N_BLOCK), lambda n, at: (q, n))
    acc = pl.BlockSpec((HALF, N_BLOCK), lambda n, at: (0, n))
    operands = [*arrays, xg_o, xg_t, wg, wu]
    in_specs = [whole(a) for a in arrays] + [tokens, tokens, weight, weight]
    aliases = {}
    if prev is not None:
        n = len(operands) + 1
        gg, gu, acc_o, acc_t = prev
        operands += [acc_o, acc_t, gg, gu]
        in_specs += [acc, acc, pl.BlockSpec(memory_space=pl.ANY), pl.BlockSpec(memory_space=pl.ANY)]
        aliases = {n + 2: 0, n + 3: 1}
    acc_shape = shape(HALF, D, dtype=BF if is_end else F32)
    return pl.pallas_call(
        functools.partial(last_kernel, q, places, len(arrays), prev is not None, is_end),
        out_shape=[shape(FF, D), shape(FF, D), acc_shape, acc_shape],
        grid_spec=pltpu.PrefetchScalarGridSpec(
            num_scalar_prefetch=1,
            grid=(D // N_BLOCK,),
            in_specs=in_specs,
            out_specs=[weight, weight, acc, acc],
            scratch_shapes=[pltpu.VMEM((R, T), BF)] * 2,
        ),
        input_output_aliases=aliases,
        compiler_params=params(),
        cost_estimate=cost(4 * 2 * R * T * D, 2 * R * T * 2 + 4 * R * D * 2 + T * D * 10),
        name=f"last{q}",
    )(at, *operands)


def down_kernel(quarters, places, n_arrays, has_prev, at, *refs):
    refs = list(refs)
    arrays = [refs.pop(0) for _ in range(n_arrays)]
    go, gt = refs.pop(0), refs.pop(0)
    if has_prev:
        refs.pop(0)
    out, act = refs
    for i in range(len(quarters)):

        @pl.when((pl.program_id(0) == i) & (pl.program_id(1) == 0))
        def _(i=i):
            place(at, arrays, places, i, act, None)

    out[...] = (dot(act[:, :HALF], go[0], NN) + dot(act[:, HALF:], gt[0], NN)).astype(BF)


def down(quarters, at, blocks, xg_o, xg_t, prev):
    arrays, places = distinct(blocks)
    tokens = pl.BlockSpec((1, HALF, N_BLOCK), lambda i, n, at: (1, 0, n))
    stride = quarters[1] - quarters[0]
    out = pl.BlockSpec((R, N_BLOCK), lambda i, n, at: (quarters[0] + stride * i, n))
    operands = [*arrays, xg_o, xg_t]
    in_specs = [whole(a) for a in arrays] + [tokens, tokens]
    aliases = {}
    if prev is not None:
        aliases = {len(operands) + 1: 0}
        operands.append(prev)
        in_specs.append(pl.BlockSpec(memory_space=pl.ANY))
    return pl.pallas_call(
        functools.partial(down_kernel, quarters, places, len(arrays), prev is not None),
        out_shape=shape(FF, D),
        grid_spec=pltpu.PrefetchScalarGridSpec(
            num_scalar_prefetch=1,
            grid=(len(quarters), D // N_BLOCK),
            in_specs=in_specs,
            out_specs=out,
            scratch_shapes=[pltpu.VMEM((R, T), BF)],
        ),
        input_output_aliases=aliases,
        compiler_params=params(),
        cost_estimate=cost(len(quarters) * 2 * R * T * D, len(quarters) * 4 * R * T + T * D * 4),
        name=f"down{quarters[0]}",
    )(at, *operands)


def gather_tokens(inputs, grad_out):
    mine = jnp.stack([inputs, grad_out])
    pair = jnp.concatenate([mine, wide_move(mine, 0, 1, 0)], 1)
    around = [wide_move(pair, -dy, 0, 0) for dy in (1, 2, 3)]
    xg_o = jnp.concatenate([pair, *around], 1)
    return xg_o, wide_move(xg_o, 0, 0, 1)


def scatter_tokens(keep, send):
    recv = wide_move(send, 0, 0, 1)
    total = keep.astype(F32) + recv.astype(F32)
    parts = [total[dy * B : (dy + 1) * B] for dy in range(4)]
    acc = parts[0]
    for dy in (1, 3, 2):
        acc = acc + wide_move(parts[dy].astype(BF), dy, 0, 0).astype(F32)
    far = wide_move(acc[B // 2 :].astype(BF), 0, 1, 0)
    return (acc[: B // 2] + far.astype(F32)).astype(BF)


def body(inputs, grad_out, w_gate, w_up, w_down):
    narrow = lax.axis_index("narrow")
    at = jnp.stack([narrow // 4, narrow % 4]).astype(jnp.int32)
    xg_o, xg_t = gather_tokens(inputs, grad_out)
    wg, wu, wd = w_gate.T, w_up.T, w_down
    gu, hid = [], []
    for q in range(Q):
        is_x = q % 2 == 0
        products = first(q, is_x, at, xg_o, xg_t, wg, wu, wd)
        terms = scatter_x(*products) if is_x else scatter_z(*products)
        a, b = swiglu(terms)
        gu.append(a)
        hid.append(b)
    prev = None
    for q in range(Q):
        blocks = (gather_x if q % 2 == 0 else gather_z)(gu[q])
        prev = last(q, q == Q - 1, at, blocks, xg_o, xg_t, wg, wu, prev)
    grad_gate, grad_up, keep, send = prev
    grad_input = scatter_tokens(keep, send)
    grad_down = None
    for q in range(2):
        blocks = (gather_x if q == 0 else gather_z)(jnp.stack([hid[q], hid[q + 2]]))
        grad_down = down((q, q + 2), at, blocks, xg_o, xg_t, grad_down)
    return grad_input, grad_gate.T, grad_up.T, grad_down


def solution(mesh):
    return jax.shard_map(
        body,
        mesh=mesh,
        in_specs=(
            P("wide", "narrow"),
            P("wide", "narrow"),
            P("narrow", "wide"),
            P("narrow", "wide"),
            P("wide", "narrow"),
        ),
        out_specs=(
            P("wide", "narrow"),
            P("narrow", "wide"),
            P("narrow", "wide"),
            P("wide", "narrow"),
        ),
        check_vma=False,
    )
```

time: 567 us -> 343 us (0.60)
  waiting for transfers between devices: 456 us -> 158 us
  Pallas kernels: 0 us -> 88.9 us
  starting transfers between devices: 0.5 us -> 81.3 us
  matrix products: 64.7 us -> 0 us
  between operations: 14.2 us -> 0.99 us
  local copies, waits for them, and re-layouts: 19.8 us -> 8.42 us
    all_gather x5 -> x0, waiting for transfers between devices: 233 us -> none  [the longest x1 66.7 us: body(): lax.all_gather(gate_grad, 'narrow', axis=0, tiled=True)]
    unnamed x10 -> x0, waiting for transfers between devices: 168 us -> none
    ppermute x0 -> x55, waiting for transfers between devices: none -> 158 us  [the longest x45 124 us: narrow_move(): return lax.ppermute(value, 'narrow', pairs)]
    pallas_call x0 -> x20, Pallas kernels: none -> 88.9 us  [the longest x4 35.8 us: first(): pl.pallas_call(functools.partial(first_kernel, is_x), out_shape=out_shape...]
    ppermute x0 -> x55, starting transfers between devices: none -> 81.3 us  [the longest x45 49.6 us: narrow_move(): return lax.ppermute(value, 'narrow', pairs)]
    dot_general x8 -> x0, matrix products: 64.7 us -> none  [the longest x1 10.3 us: body(): lax.dot_general(up_all, w_up, last_contract, preferred_element_type=jnp.f...]
    reduce_scatter x1 -> x0, waiting for transfers between devices: 54.9 us -> none  [body(): lax.psum_scatter((lax.dot_general(gate_all, w_gate, last_contract, prefer...]
    unnamed x14 -> x19, local copies, waits for them, and re-layouts: 19.8 us -> 8.22 us
  transfers between devices with their start and end apart: 8 -> 55, of which waited for: 8 -> 24; matrix products, arithmetic and copies ran while one was open for 16% -> 0% of each run, Pallas kernels for 0% -> 23%
where the time goes in v1:
time: 343 us; the launch traced here: 342 us
  waiting for transfers between devices  158 us (46%)
  Pallas kernels  88.9 us (26%)
  starting transfers between devices  81.3 us (24%)
  local copies, waits for them, and re-layouts  8.42 us (2%)
  other arithmetic  3.93 us (1%)
    ppermute x45, waiting for transfers between devices, narrow_move(): return lax.ppermute(value, 'narrow', pairs)  124 us
    ppermute x45, starting transfers between devices, narrow_move(): return lax.ppermute(value, 'narrow', pairs)  49.6 us
    pallas_call x4, Pallas kernels, first(): pl.pallas_call(functools.partial(first_kernel, is_x), out_shape=out_shape...  35.8 us
    ppermute x10, waiting for transfers between devices, wide_move(): return lax.ppermute(value, 'wide', pairs)  34.8 us
    pallas_call x4, Pallas kernels, last(): pl.pallas_call(functools.partial(last_kernel, q, places, len(arrays), pre...  33.5 us
    ppermute x10, starting transfers between devices, wide_move(): return lax.ppermute(value, 'wide', pairs)  31.7 us
    pallas_call x2, Pallas kernels, down(): pl.pallas_call(functools.partial(down_kernel, quarters, places, len(array...  16.6 us
    unnamed x19, local copies, waits for them, and re-layouts  8.22 us
  transfers between devices with their start and end apart: 55, of which 24 were waited for; matrix products, arithmetic and copies ran while one was open for 0% of the time, Pallas kernels for 23%

profile of v1, /device:TPU:1, one launch (start us, length us, event | category | flops | bytes accessed | tf_op | source)
XLA Modules:
  0.0 342.0 jit_solution(3153476711005473053)
XLA Ops:
  1.6 2.1 collective-permute-start
  3.8 5.5 %collective-permute-done = bf16[2,64,1024]{2,1,0:T(8,128)(2,1)S(1)} collective-permute-done((bf16[2,64,1024]{2,1,0:T(8,128)(2,1)S(1)}, bf16[2,64,1024]{2,1,0:T(8,128)(2,1)S(1)}, u32[]{:S(2)}, u32[]{:S(2)}) %collective-permute-start) | collective-permute-done | bytes 262176 | tf_op jit(solution)/shard_map/ppermute | solution.py:57
  10.3 3.2 collective-permute-start.1
  14.6 9.7 %collective-permute-done.1 = bf16[2,128,1024]{2,1,0:T(8,128)(2,1)S(1)} collective-permute-done((bf16[2,128,1024]{2,1,0:T(8,128)(2,1)S(1)}, bf16[2,128,1024]{2,1,0:T(8,128)(2,1)S(1)}, u32[]{:S(2)}, u32[]{:S(2)}) %collective-permute-start.1) | collective-permute-done | bytes 524320 | tf_op jit(solution)/shard_map/ppermute | solution.py:57
  24.4 2.3 collective-permute-done.2
  26.8 13.4 %collective-permute-done.3 = bf16[2,128,1024]{2,1,0:T(8,128)(2,1)S(1)} collective-permute-done((bf16[2,128,1024]{2,1,0:T(8,128)(2,1)S(1)}, bf16[2,128,1024]{2,1,0:T(8,128)(2,1)S(1)}, u32[]{:S(2)}, u32[]{:S(2)}) %collective-permute-start.3) | collective-permute-done | bytes 524320 | tf_op jit(solution)/shard_map/ppermute | solution.py:57
  40.8 3.8 %collective-permute-done.4.xt.gt.refs_6_ = bf16[2,512,1024]{2,1,0:T(8,128)(2,1)} collective-permute-done((bf16[2,512,1024]{2,1,0:T(8,128)(2,1)S(1)}, bf16[2,512,1024]{2,1,0:T(8,128)(2,1)}, u32[]{:S(2)}, u32[]{:S(2)}) %collective-permute-start.4) | collective-permute-done | bytes 2097184 | tf_op jit(solution)/shard_map/ppermute | solution.py:57
  44.7 10.4 %first1.1 = (bf16[2,3,464,128]{3,2,1,0:T(8,128)(2,1)S(1)}, bf16[2,3,464,128]{3,2,1,0:T(8,128)(2,1)S(1)}, bf16[2,3,464,128]{3,2,1,0:T(8,128)(2,1)S(1)}, bf16[3,46...) custom-call(s32[2]{0:T(128)S(1)} %pad_add_fusion.at, ...), custom_call_target="tpu_custom_call" | custom-call | flops 2919235584 | bytes 9895936 | tf_op jit(solution)/shard_map/first1/pallas_call | solution.py:105
  56.8 2.2 collective-permute-start.24
  59.0 7.5 %first0.1 = (bf16[4,3,464,128]{3,2,1,0:T(8,128)(2,1)}, bf16[4,3,464,128]{3,2,1,0:T(8,128)(2,1)S(1)}) custom-call(s32[2]{0:T(128)S(1)} %pad_add_fusion.at, bf16[2,512,1024]{2,1,0:T(8,128)(2,1)S(1)} %constant_dynamic-update-slice_fusion.xo.go.refs_5_, bf16[2,512,1024]{2,1,0:T(8,128)(2,1)} %collective-permute-done.4.xt.gt.refs_6_, ...), custom_call_target="tpu_custom_call" | custom-call | flops 2919235584 | bytes 9895936 | tf_op jit(solution)/shard_map/first0/pallas_call | solution.py:105
  66.4 2.7 collective-permute-start.33
  69.2 7.5 %first2.1 = (bf16[4,3,464,128]{3,2,1,0:T(8,128)(2,1)}, bf16[4,3,464,128]{3,2,1,0:T(8,128)(2,1)S(1)}) custom-call(s32[2]{0:T(128)S(1)} %pad_add_fusion.at, bf16[2,512,1024]{2,1,0:T(8,128)(2,1)S(1)} %constant_dynamic-update-slice_fusion.xo.go.refs_5_, bf16[2,512,1024]{2,1,0:T(8,128)(2,1)} %collective-permute-done.4.xt.gt.refs_6_, ...), custom_call_target="tpu_custom_call" | custom-call | flops 2919235584 | bytes 9895936 | tf_op jit(solution)/shard_map/first2/pallas_call | solution.py:105
  77.2 10.4 %first3.1 = (bf16[2,3,464,128]{3,2,1,0:T(8,128)(2,1)S(1)}, bf16[2,3,464,128]{3,2,1,0:T(8,128)(2,1)S(1)}, bf16[2,3,464,128]{3,2,1,0:T(8,128)(2,1)S(1)}, bf16[3,46...) custom-call(s32[2]{0:T(128)S(1)} %pad_add_fusion.at, ...), custom_call_target="tpu_custom_call" | custom-call | flops 2919235584 | bytes 9895936 | tf_op jit(solution)/shard_map/first3/pallas_call | solution.py:105
  88.6 1.8 collective-permute-start.6
  90.4 11.8 %collective-permute-done.5.ra = bf16[3,464,128]{2,1,0:T(8,128)(2,1)S(1)} collective-permute-done((bf16[3,464,128]{2,1,0:T(8,128)(2,1)S(1)}, bf16[3,464,128]{2,1,0:T(8,128)(2,1)S(1)}, u32[]{:S(2)}, u32[]{:S(2)}) %collective-permute-start.5) | collective-permute-done | bytes 356384 | tf_op jit(solution)/shard_map/ppermute | solution.py:47
  105.2 12.3 %collective-permute-done.26.c.refs_2_ = bf16[2,3,464,128]{3,2,1,0:T(8,128)(2,1)S(1)} collective-permute-done((bf16[2,3,464,128]{3,2,1,0:T(8,128)(2,1)S(1)}, bf16[2,3,464,128]{3,2,1,0:T(8,128)(2,1)S(1)}, u32[]{:S(2)}, u32[]{:S(2)}) %collective-permute-start.26) | collective-permute-done | bytes 712736 | tf_op jit(solution)/shard_map/ppermute | solution.py:47
  117.7 2.9 collective-permute-start.27
  120.6 12.2 %collective-permute-done.8.c.refs_2_ = bf16[2,3,464,128]{3,2,1,0:T(8,128)(2,1)S(1)} collective-permute-done((bf16[2,3,464,128]{3,2,1,0:T(8,128)(2,1)S(1)}, bf16[2,3,464,128]{3,2,1,0:T(8,128)(2,1)S(1)}, u32[]{:S(2)}, u32[]{:S(2)}) %collective-permute-start.8) | collective-permute-done | bytes 712736 | tf_op jit(solution)/shard_map/ppermute | solution.py:47
  132.9 2.9 collective-permute-start.9
  136.5 2.7 collective-permute-start.35
  140.6 5.4 %collective-permute-done.9.refs_3_ = bf16[3,464,128]{2,1,0:T(8,128)(2,1)S(1)} collective-permute-done((bf16[3,464,128]{2,1,0:T(8,128)(2,1)S(1)}, bf16[3,464,128]{2,1,0:T(8,128)(2,1)S(1)}, u32[]{:S(2)}, u32[]{:S(2)}) %collective-permute-start.9) | collective-permute-done | bytes 356384 | tf_op jit(solution)/shard_map/ppermute | solution.py:47
  146.0 2.7 collective-permute-start.28
  151.2 1.9 collective-permute-done.28
  154.1 6.5 %collective-permute-done.16.refs_2_ = bf16[3,464,128]{2,1,0:T(8,128)(2,1)S(1)} collective-permute-done((bf16[3,464,128]{2,1,0:T(8,128)(2,1)S(1)}, bf16[3,464,128]{2,1,0:T(8,128)(2,1)S(1)}, u32[]{:S(2)}, u32[]{:S(2)}) %collective-permute-start.16) | collective-permute-done | bytes 356384 | tf_op jit(solution)/shard_map/ppermute | solution.py:47
  160.9 3.0 collective-permute-done.17.refs_3_
  163.8 2.6 collective-permute-done.18.refs_4_
  167.7 1.8 collective-permute-start.19
  169.6 3.1 collective-permute-done.37.refs_1_
  173.0 4.2 %collective-permute-start.21 = (bf16[2,464,128]{2,1,0:T(8,128)(2,1)S(1)}, bf16[2,464,128]{2,1,0:T(8,128)(2,1)S(1)}, u32[]{:S(2)}, u32[]{:S(2)}) collective-permute-start(bf16[2,464,128]{2,1,0:T(8,128)(2,1)S(1)} %get-tuple-element.65.refs_0_), channel_id=1, source_target_pairs={{0,1},{1,2},{2,3},{3,0},{4,5},{5,6},{6,7},{7,4},{8,9},{9,10},{10,1... | collective-permute-start | bytes 712712 | tf_op jit(solution)/shard_map/ppermute | solution.py:47
  177.3 11.7 %collective-permute-done.39.refs_3_ = bf16[2,464,128]{2,1,0:T(8,128)(2,1)S(1)} collective-permute-done((bf16[2,464,128]{2,1,0:T(8,128)(2,1)S(1)}, bf16[2,464,128]{2,1,0:T(8,128)(2,1)S(1)}, u32[]{:S(2)}, u32[]{:S(2)}) %collective-permute-start.39) | collective-permute-done | bytes 237600 | tf_op jit(solution)/shard_map/ppermute | solution.py:47
  190.8 3.3 collective-permute-done.21.refs_3_
  195.1 4.1 %collective-permute-done.31.refs_3_ = bf16[2,2,464,128]{3,2,1,0:T(8,128)(2,1)S(1)} collective-permute-done((bf16[2,2,464,128]{3,2,1,0:T(8,128)(2,1)S(1)}, bf16[2,2,464,128]{3,2,1,0:T(8,128)(2,1)S(1)}, u32[]{:S(2)}, u32[]{:S(2)}) %collective-permute-start.31) | collective-permute-done | bytes 475168 | tf_op jit(solution)/shard_map/ppermute | solution.py:47
  199.3 7.3 %collective-permute-done.11.refs_4_ = bf16[2,2,464,128]{3,2,1,0:T(8,128)(2,1)S(1)} collective-permute-done((bf16[2,2,464,128]{3,2,1,0:T(8,128)(2,1)S(1)}, bf16[2,2,464,128]{3,2,1,0:T(8,128)(2,1)S(1)}, u32[]{:S(2)}, u32[]{:S(2)}) %collective-permute-start.11) | collective-permute-done | bytes 475168 | tf_op jit(solution)/shard_map/ppermute | solution.py:47
  206.6 2.7 collective-permute-start.32
  210.7 7.8 %last0.1 = (bf16[1848,1024]{1,0:T(8,128)(2,1)}, bf16[1848,1024]{1,0:T(8,128)(2,1)}, f32[512,1024]{1,0:T(8,128)S(1)}, f32[512,1024]{1,0:T(8,128)S(1)}) custom-call(s32[2]{0:T(128)S(1)} %pad_add_fusion.at, bf16[2,464,128]{2,1,0:T(8,128)(2,1)S(1)} %get-tuple-element.79.refs_0_, bf16[2,464,128]{2,1,0:T(8,128)(2,1)S(1)} %collective-permute-done.37.refs_1_, ...), custom_call_target="tpu_custom_call" | custom-call | flops 3892314112 | bytes 16187392 | tf_op jit(solution)/shard_map/last0/pallas_call | solution.py:337
  221.2 2.7 collective-permute-start.14
  223.9 8.3 %last1.1 = (bf16[1848,1024]{1,0:T(8,128)(2,1)}, bf16[1848,1024]{1,0:T(8,128)(2,1)}, f32[512,1024]{1,0:T(8,128)S(1)}, f32[512,1024]{1,0:T(8,128)S(1)}) custom-call(s32[2]{0:T(128)S(1)} %pad_add_fusion.at, bf16[2,464,128]{2,1,0:T(8,128)(2,1)S(1)} %collective-permute-done.30.refs_0_, ...), custom_call_target="tpu_custom_call", output_to_operand_aliasing={{0}: (12, {}), {1}: (13, {})} | custom-call | flops 3892314112 | bytes 16187392 | tf_op jit(solution)/shard_map/last1/pallas_call | solution.py:337
  235.0 8.4 %last2.1 = (bf16[1848,1024]{1,0:T(8,128)(2,1)}, bf16[1848,1024]{1,0:T(8,128)(2,1)}, f32[512,1024]{1,0:T(8,128)S(1)}, f32[512,1024]{1,0:T(8,128)S(1)}) custom-call(s32[2]{0:T(128)S(1)} %pad_add_fusion.at, bf16[2,464,128]{2,1,0:T(8,128)(2,1)S(1)} %get-tuple-element.65.refs_0_, ...), custom_call_target="tpu_custom_call", output_to_operand_aliasing={{0}: (12, {}), {1}: (13, {})} | custom-call | flops 3892314112 | bytes 16187392 | tf_op jit(solution)/shard_map/last2/pallas_call | solution.py:337
  246.1 9.0 %last3.1 = (bf16[1848,1024]{1,0:T(8,128)(2,1)}, bf16[1848,1024]{1,0:T(8,128)(2,1)}, bf16[512,1024]{1,0:T(8,128)(2,1)S(1)}, bf16[512,1024]{1,0:T(8,128)(2,1)S(1)}) custom-call(s32[2]{0:T(128)S(1)} %pad_add_fusion.at, bf16[2,464,128]{2,1,0:T(8,128)(2,1)S(1)} %collective-permute-done.12.refs_0_, ...), custom_call_target="tpu_custom_call", output_to_operand_aliasing={{0}: (12, {}), {1}: (13, {})} | custom-call | flops 3892314112 | bytes 16187392 | tf_op jit(solution)/shard_map/last3/pallas_call | solution.py:337
  255.1 21.6 %collective-permute-start.41 = (bf16[512,1024]{1,0:T(8,128)(2,1)S(1)}, bf16[512,1024]{1,0:T(8,128)(2,1)S(1)}, u32[]{:S(2)}, u32[]{:S(2)}) collective-permute-start(bf16[512,1024]{1,0:T(8,128)(2,1)S(1)} %get-tuple-element.93), channel_id=1, source_target_pairs={{0,8},{8,0},{16,24},{24,16},{32,40},{40,32},{48,56},{56,48},{64,72... | collective-permute-start | bytes 3145736 | tf_op jit(solution)/shard_map/ppermute | solution.py:57
  276.9 2.7 collective-permute-start.51
  280.3 9.2 %collective-permute-done.51.refs_1_ = bf16[2,464,128]{2,1,0:T(8,128)(2,1)S(1)} collective-permute-done((bf16[2,464,128]{2,1,0:T(8,128)(2,1)S(1)}, bf16[2,464,128]{2,1,0:T(8,128)(2,1)S(1)}, u32[]{:S(2)}, u32[]{:S(2)}) %collective-permute-start.51) | collective-permute-done | bytes 237600 | tf_op jit(solution)/shard_map/ppermute | solution.py:47
  289.4 3.6 %collective-permute-start.49 = (bf16[2,2,464,128]{3,2,1,0:T(8,128)(2,1)S(1)}, bf16[2,2,464,128]{3,2,1,0:T(8,128)(2,1)S(1)}, u32[]{:S(2)}, u32[]{:S(2)}) collective-permute-start(bf16[2,2,464,128]{3,2,1,0:T(8,128)(2,1)S(1)} %pad_maximum_fusion.6.refs_2_), channel_id=1, source_target_pairs={{0,3},{1,0},{2,1},{3,2},{4,7},{5,4},{6,5},{7,6},{8,11},{9,8},{10,9... | collective-permute-start | bytes 1425416 | tf_op jit(solution)/shard_map/ppermute | solution.py:47
  293.9 6.8 %collective-permute-done.53.refs_3_ = bf16[2,464,128]{2,1,0:T(8,128)(2,1)S(1)} collective-permute-done((bf16[2,464,128]{2,1,0:T(8,128)(2,1)S(1)}, bf16[2,464,128]{2,1,0:T(8,128)(2,1)S(1)}, u32[]{:S(2)}, u32[]{:S(2)}) %collective-permute-start.53) | collective-permute-done | bytes 237600 | tf_op jit(solution)/shard_map/ppermute | solution.py:47
  301.7 2.7 collective-permute-start.43
  304.4 19.8 %collective-permute-done.54.refs_4_ = bf16[4,2,464,128]{3,2,1,0:T(8,128)(2,1)S(1)} collective-permute-done((bf16[4,2,464,128]{3,2,1,0:T(8,128)(2,1)S(1)}, bf16[4,2,464,128]{3,2,1,0:T(8,128)(2,1)S(1)}, u32[]{:S(2)}, u32[]{:S(2)}) %collective-permute-start.54) | collective-permute-done | bytes 950304 | tf_op jit(solution)/shard_map/ppermute | solution.py:47
  324.2 8.3 %down0.1.refs_7_ = bf16[1848,1024]{1,0:T(8,128)(2,1)} custom-call(s32[2]{0:T(128)S(1)} %pad_add_fusion.at, bf16[2,464,128]{2,1,0:T(8,128)(2,1)S(1)} %get-tuple-element.108.refs_0_, bf16[2,464,128]{2,1,0:T(8,128)(2,1)S(1)} %collective-permute-done.51.refs_1_, bf16[2,464,128]{2,1,0:T(8,128)(2,1)S(1)} %collective-permute-done.52.refs_2_, ...), custom_call_target="tpu_custom_call" | custom-call | flops 1946157056 | bytes 7995392 | tf_op jit(solution)/shard_map/down0/pallas_call | solution.py:382
  333.0 8.3 %down1.1 = bf16[1848,1024]{1,0:T(8,128)(2,1)} custom-call(s32[2]{0:T(128)S(1)} %pad_add_fusion.at, bf16[2,464,128]{2,1,0:T(8,128)(2,1)S(1)} %collective-permute-done.48.refs_0_, bf16[2,464,128]{2,1,0:T(8,128)(2,1)S(1)} %collective-permute-done.50.refs_1_, bf16[2,2,464,128]{3,2,1,0:T(8,128)(2,1)S(1)} %pad_maximum_fusion.6.refs_2_, ...), custom_call_target="tpu_custom_call", output_to_operand_aliasing={{}: (8, {})} | custom-call | flops 1946157056 | bytes 7995392 | tf_op jit(solution)/shard_map/down1/pallas_call | solution.py:382
  (124 shorter events, 34.2 us)
Async XLA Ops:
  10.3 14.0 %collective-permute-start.1 = (bf16[2,128,1024]{2,1,0:T(8,128)(2,1)S(1)}, bf16[2,128,1024]{2,1,0:T(8,128)(2,1)S(1)}, u32[]{:S(2)}, u32[]{:S(2)}) collective-permute-start(bf16[2,128,1024]{2,1,0:T(8,128)(2,1)S(1)} %pad_maximum_fusion.3), channel_id=1, source_target_pairs={{0,96},{8,104},{16,112},{24,120},{32,0},{40,8},{48,16},{56,24},{64... | collective-permute-start | bytes 1572872 | tf_op jit(solution)/shard_map/ppermute | solution.py:57
  13.5 13.2 %collective-permute-start.2 = (bf16[2,128,1024]{2,1,0:T(8,128)(2,1)S(1)}, bf16[2,128,1024]{2,1,0:T(8,128)(2,1)S(1)}, u32[]{:S(2)}, u32[]{:S(2)}) collective-permute-start(bf16[2,128,1024]{2,1,0:T(8,128)(2,1)S(1)} %pad_maximum_fusion.3), channel_id=1, source_target_pairs={{0,64},{8,72},{16,80},{24,88},{32,96},{40,104},{48,112},{56,120},{... | collective-permute-start | bytes 1572872 | tf_op jit(solution)/shard_map/ppermute | solution.py:57
  13.9 26.2 %collective-permute-start.3 = (bf16[2,128,1024]{2,1,0:T(8,128)(2,1)S(1)}, bf16[2,128,1024]{2,1,0:T(8,128)(2,1)S(1)}, u32[]{:S(2)}, u32[]{:S(2)}) collective-permute-start(bf16[2,128,1024]{2,1,0:T(8,128)(2,1)S(1)} %pad_maximum_fusion.3), channel_id=1, source_target_pairs={{0,32},{8,40},{16,48},{24,56},{32,64},{40,72},{48,80},{56,88},{64,... | collective-permute-start | bytes 1572872 | tf_op jit(solution)/shard_map/ppermute | solution.py:57
  55.1 21.8 %collective-permute-start.23 = (bf16[3,464,128]{2,1,0:T(8,128)(2,1)S(1)}, bf16[3,464,128]{2,1,0:T(8,128)(2,1)S(1)}, u32[]{:S(2)}, u32[]{:S(2)}) collective-permute-start(bf16[3,464,128]{2,1,0:T(8,128)(2,1)S(1)} %get-tuple-element.68), channel_id=1, source_target_pairs={{0,1},{1,2},{2,3},{3,0},{4,5},{5,6},{6,7},{7,4},{8,9},{9,10},{10,1... | collective-permute-start | bytes 1069064 | tf_op jit(solution)/shard_map/ppermute | solution.py:47
  56.8 20.1 %collective-permute-start.24 = (bf16[3,464,128]{2,1,0:T(8,128)(2,1)S(1)}, bf16[3,464,128]{2,1,0:T(8,128)(2,1)S(1)}, u32[]{:S(2)}, u32[]{:S(2)}) collective-permute-start(bf16[3,464,128]{2,1,0:T(8,128)(2,1)S(1)} %get-tuple-element.70), channel_id=1, source_target_pairs={{0,3},{1,0},{2,1},{3,2},{4,7},{5,4},{6,5},{7,6},{8,11},{9,8},{10,9... | collective-permute-start | bytes 1069064 | tf_op jit(solution)/shard_map/ppermute | solution.py:47
  66.4 69.4 %collective-permute-start.33 = (bf16[4,3,464,128]{3,2,1,0:T(8,128)(2,1)}, bf16[4,3,464,128]{3,2,1,0:T(8,128)(2,1)S(1)}, u32[]{:S(2)}, u32[]{:S(2)}) collective-permute-start(bf16[4,3,464,128]{3,2,1,0:T(8,128)(2,1)} %get-tuple-element.75), channel_id=1, source_target_pairs={{0,4},{1,5},{2,6},{3,7},{4,0},{5,1},{6,2},{7,3},{8,12},{9,13},{10,... | collective-permute-start | bytes 4276232 | tf_op jit(solution)/shard_map/ppermute | solution.py:47
  76.7 62.5 %collective-permute-start.15 = (bf16[4,3,464,128]{3,2,1,0:T(8,128)(2,1)}, bf16[4,3,464,128]{3,2,1,0:T(8,128)(2,1)S(1)}, u32[]{:S(2)}, u32[]{:S(2)}) collective-permute-start(bf16[4,3,464,128]{3,2,1,0:T(8,128)(2,1)} %get-tuple-element.61), channel_id=1, source_target_pairs={{0,4},{1,5},{2,6},{3,7},{4,0},{5,1},{6,2},{7,3},{8,12},{9,13},{10,... | collective-permute-start | bytes 4276232 | tf_op jit(solution)/shard_map/ppermute | solution.py:47
  77.1 26.9 %collective-permute-start.25 = (bf16[2,3,464,128]{3,2,1,0:T(8,128)(2,1)S(1)}, bf16[2,3,464,128]{3,2,1,0:T(8,128)(2,1)S(1)}, u32[]{:S(2)}, u32[]{:S(2)}) collective-permute-start(bf16[2,3,464,128]{3,2,1,0:T(8,128)(2,1)S(1)} %get-tuple-element.71), channel_id=1, source_target_pairs={{0,1},{1,2},{2,3},{3,0},{4,5},{5,6},{6,7},{7,4},{8,9},{9,10},{10,1... | collective-permute-start | bytes 2138120 | tf_op jit(solution)/shard_map/ppermute | solution.py:47
  87.6 14.6 %collective-permute-start.5 = (bf16[3,464,128]{2,1,0:T(8,128)(2,1)S(1)}, bf16[3,464,128]{2,1,0:T(8,128)(2,1)S(1)}, u32[]{:S(2)}, u32[]{:S(2)}) collective-permute-start(bf16[3,464,128]{2,1,0:T(8,128)(2,1)S(1)} %get-tuple-element.54), channel_id=1, source_target_pairs={{0,1},{1,2},{2,3},{3,0},{4,5},{5,6},{6,7},{7,4},{8,9},{9,10},{10,1... | collective-permute-start | bytes 1069064 | tf_op jit(solution)/shard_map/ppermute | solution.py:47
  88.6 13.6 %collective-permute-start.6 = (bf16[3,464,128]{2,1,0:T(8,128)(2,1)S(1)}, bf16[3,464,128]{2,1,0:T(8,128)(2,1)S(1)}, u32[]{:S(2)}, u32[]{:S(2)}) collective-permute-start(bf16[3,464,128]{2,1,0:T(8,128)(2,1)S(1)} %get-tuple-element.56), channel_id=1, source_target_pairs={{0,3},{1,0},{2,1},{3,2},{4,7},{5,4},{6,5},{7,6},{8,11},{9,8},{10,9... | collective-permute-start | bytes 1069064 | tf_op jit(solution)/shard_map/ppermute | solution.py:47
  102.2 15.3 %collective-permute-start.26 = (bf16[2,3,464,128]{3,2,1,0:T(8,128)(2,1)S(1)}, bf16[2,3,464,128]{3,2,1,0:T(8,128)(2,1)S(1)}, u32[]{:S(2)}, u32[]{:S(2)}) collective-permute-start(bf16[2,3,464,128]{3,2,1,0:T(8,128)(2,1)S(1)} %get-tuple-element.72), channel_id=1, source_target_pairs={{0,3},{1,0},{2,1},{3,2},{4,7},{5,4},{6,5},{7,6},{8,11},{9,8},{10,9... | collective-permute-start | bytes 2138120 | tf_op jit(solution)/shard_map/ppermute | solution.py:47
  102.4 18.2 %collective-permute-start.7 = (bf16[2,3,464,128]{3,2,1,0:T(8,128)(2,1)S(1)}, bf16[2,3,464,128]{3,2,1,0:T(8,128)(2,1)S(1)}, u32[]{:S(2)}, u32[]{:S(2)}) collective-permute-start(bf16[2,3,464,128]{3,2,1,0:T(8,128)(2,1)S(1)} %get-tuple-element.57), channel_id=1, source_target_pairs={{0,1},{1,2},{2,3},{3,0},{4,5},{5,6},{6,7},{7,4},{8,9},{9,10},{10,1... | collective-permute-start | bytes 2138120 | tf_op jit(solution)/shard_map/ppermute | solution.py:47
  104.0 28.8 %collective-permute-start.8 = (bf16[2,3,464,128]{3,2,1,0:T(8,128)(2,1)S(1)}, bf16[2,3,464,128]{3,2,1,0:T(8,128)(2,1)S(1)}, u32[]{:S(2)}, u32[]{:S(2)}) collective-permute-start(bf16[2,3,464,128]{3,2,1,0:T(8,128)(2,1)S(1)} %get-tuple-element.58), channel_id=1, source_target_pairs={{0,3},{1,0},{2,1},{3,2},{4,7},{5,4},{6,5},{7,6},{8,11},{9,8},{10,9... | collective-permute-start | bytes 2138120 | tf_op jit(solution)/shard_map/ppermute | solution.py:47
  117.7 22.0 %collective-permute-start.27 = (bf16[3,464,128]{2,1,0:T(8,128)(2,1)S(1)}, bf16[3,464,128]{2,1,0:T(8,128)(2,1)S(1)}, u32[]{:S(2)}, u32[]{:S(2)}) collective-permute-start(bf16[3,464,128]{2,1,0:T(8,128)(2,1)S(1)} %z_far.3), channel_id=1, source_target_pairs={{0,4},{1,5},{2,6},{3,7},{4,0},{5,1},{6,2},{7,3},{8,12},{9,13},{10,... | collective-permute-start | bytes 1069064 | tf_op jit(solution)/shard_map/ppermute | solution.py:47
  132.9 13.1 %collective-permute-start.9 = (bf16[3,464,128]{2,1,0:T(8,128)(2,1)S(1)}, bf16[3,464,128]{2,1,0:T(8,128)(2,1)S(1)}, u32[]{:S(2)}, u32[]{:S(2)}) collective-permute-start(bf16[3,464,128]{2,1,0:T(8,128)(2,1)S(1)} %z_far.2), channel_id=1, source_target_pairs={{0,4},{1,5},{2,6},{3,7},{4,0},{5,1},{6,2},{7,3},{8,12},{9,13},{10,... | collective-permute-start | bytes 1069064 | tf_op jit(solution)/shard_map/ppermute | solution.py:47
  136.4 12.3 %collective-permute-start.34 = (bf16[3,464,128]{2,1,0:T(8,128)(2,1)S(1)}, bf16[3,464,128]{2,1,0:T(8,128)(2,1)S(1)}, u32[]{:S(2)}, u32[]{:S(2)}) collective-permute-start(bf16[3,464,128]{2,1,0:T(8,128)(2,1)S(1)} %get-tuple-element.76), channel_id=1, source_target_pairs={{0,1},{1,2},{2,3},{3,0},{4,5},{5,6},{6,7},{7,4},{8,9},{9,10},{10,1... | collective-permute-start | bytes 1069064 | tf_op jit(solution)/shard_map/ppermute | solution.py:47
  136.5 13.5 %collective-permute-start.35 = (bf16[3,464,128]{2,1,0:T(8,128)(2,1)S(1)}, bf16[3,464,128]{2,1,0:T(8,128)(2,1)S(1)}, u32[]{:S(2)}, u32[]{:S(2)}) collective-permute-start(bf16[3,464,128]{2,1,0:T(8,128)(2,1)S(1)} %get-tuple-element.77), channel_id=1, source_target_pairs={{0,3},{1,0},{2,1},{3,2},{4,7},{5,4},{6,5},{7,6},{8,11},{9,8},{10,9... | collective-permute-start | bytes 1069064 | tf_op jit(solution)/shard_map/ppermute | solution.py:47
  139.7 21.0 %collective-permute-start.16 = (bf16[3,464,128]{2,1,0:T(8,128)(2,1)S(1)}, bf16[3,464,128]{2,1,0:T(8,128)(2,1)S(1)}, u32[]{:S(2)}, u32[]{:S(2)}) collective-permute-start(bf16[3,464,128]{2,1,0:T(8,128)(2,1)S(1)} %get-tuple-element.62), channel_id=1, source_target_pairs={{0,1},{1,2},{2,3},{3,0},{4,5},{5,6},{6,7},{7,4},{8,9},{9,10},{10,1... | collective-permute-start | bytes 1069064 | tf_op jit(solution)/shard_map/ppermute | solution.py:47
  148.6 15.2 %collective-permute-start.17 = (bf16[3,464,128]{2,1,0:T(8,128)(2,1)S(1)}, bf16[3,464,128]{2,1,0:T(8,128)(2,1)S(1)}, u32[]{:S(2)}, u32[]{:S(2)}) collective-permute-start(bf16[3,464,128]{2,1,0:T(8,128)(2,1)S(1)} %get-tuple-element.63), channel_id=1, source_target_pairs={{0,3},{1,0},{2,1},{3,2},{4,7},{5,4},{6,5},{7,6},{8,11},{9,8},{10,9... | collective-permute-start | bytes 1069064 | tf_op jit(solution)/shard_map/ppermute | solution.py:47
  149.9 16.5 %collective-permute-start.18 = (bf16[3,464,128]{2,1,0:T(8,128)(2,1)S(1)}, bf16[3,464,128]{2,1,0:T(8,128)(2,1)S(1)}, u32[]{:S(2)}, u32[]{:S(2)}) collective-permute-start(bf16[3,464,128]{2,1,0:T(8,128)(2,1)S(1)} %get-tuple-element.64), channel_id=1, source_target_pairs={{0,2},{1,3},{2,0},{3,1},{4,6},{5,7},{6,4},{7,5},{8,10},{9,11},{10,... | collective-permute-start | bytes 1069064 | tf_op jit(solution)/shard_map/ppermute | solution.py:47
  150.9 16.9 %collective-permute-start.10 = (bf16[2,464,128]{2,1,0:T(8,128)(2,1)S(1)}, bf16[2,464,128]{2,1,0:T(8,128)(2,1)S(1)}, u32[]{:S(2)}, u32[]{:S(2)}) collective-permute-start(bf16[2,464,128]{2,1,0:T(8,128)(2,1)S(1)} %get-tuple-element.59), channel_id=1, source_target_pairs={{0,4},{1,5},{2,6},{3,7},{4,0},{5,1},{6,2},{7,3},{8,12},{9,13},{10,... | collective-permute-start | bytes 712712 | tf_op jit(solution)/shard_map/ppermute | solution.py:47
  153.1 19.5 %collective-permute-start.37 = (bf16[2,464,128]{2,1,0:T(8,128)(2,1)S(1)}, bf16[2,464,128]{2,1,0:T(8,128)(2,1)S(1)}, u32[]{:S(2)}, u32[]{:S(2)}) collective-permute-start(bf16[2,464,128]{2,1,0:T(8,128)(2,1)S(1)} %get-tuple-element.79.refs_0_), channel_id=1, source_target_pairs={{0,3},{1,0},{2,1},{3,2},{4,7},{5,4},{6,5},{7,6},{8,11},{9,8},{10,9... | collective-permute-start | bytes 712712 | tf_op jit(solution)/shard_map/ppermute | solution.py:47
  160.7 12.4 %collective-permute-start.38 = (bf16[2,464,128]{2,1,0:T(8,128)(2,1)S(1)}, bf16[2,464,128]{2,1,0:T(8,128)(2,1)S(1)}, u32[]{:S(2)}, u32[]{:S(2)}) collective-permute-start(bf16[2,464,128]{2,1,0:T(8,128)(2,1)S(1)} %get-tuple-element.79.refs_0_), channel_id=1, source_target_pairs={{0,2},{1,3},{2,0},{3,1},{4,6},{5,7},{6,4},{7,5},{8,10},{9,11},{10,... | collective-permute-start | bytes 712712 | tf_op jit(solution)/shard_map/ppermute | solution.py:47
  163.8 30.5 %collective-permute-start.29 = (bf16[2,2,464,128]{3,2,1,0:T(8,128)(2,1)S(1)}, bf16[2,2,464,128]{3,2,1,0:T(8,128)(2,1)S(1)}, u32[]{:S(2)}, u32[]{:S(2)}) collective-permute-start(bf16[2,2,464,128]{3,2,1,0:T(8,128)(2,1)S(1)} %pad_maximum_fusion.5.refs_2_), channel_id=1, source_target_pairs={{0,1},{1,2},{2,3},{3,0},{4,5},{5,6},{6,7},{7,4},{8,9},{9,10},{10,1... | collective-permute-start | bytes 1425416 | tf_op jit(solution)/shard_map/ppermute | solution.py:47
  166.4 22.6 %collective-permute-start.39 = (bf16[2,464,128]{2,1,0:T(8,128)(2,1)S(1)}, bf16[2,464,128]{2,1,0:T(8,128)(2,1)S(1)}, u32[]{:S(2)}, u32[]{:S(2)}) collective-permute-start(bf16[2,464,128]{2,1,0:T(8,128)(2,1)S(1)} %get-tuple-element.79.refs_0_), channel_id=1, source_target_pairs={{0,1},{1,2},{2,3},{3,0},{4,5},{5,6},{6,7},{7,4},{8,9},{9,10},{10,1... | collective-permute-start | bytes 712712 | tf_op jit(solution)/shard_map/ppermute | solution.py:47
  167.7 21.4 %collective-permute-start.19 = (bf16[2,464,128]{2,1,0:T(8,128)(2,1)S(1)}, bf16[2,464,128]{2,1,0:T(8,128)(2,1)S(1)}, u32[]{:S(2)}, u32[]{:S(2)}) collective-permute-start(bf16[2,464,128]{2,1,0:T(8,128)(2,1)S(1)} %get-tuple-element.65.refs_0_), channel_id=1, source_target_pairs={{0,3},{1,0},{2,1},{3,2},{4,7},{5,4},{6,5},{7,6},{8,11},{9,8},{10,9... | collective-permute-start | bytes 712712 | tf_op jit(solution)/shard_map/ppermute | solution.py:47
  172.6 16.7 %collective-permute-start.20 = (bf16[2,464,128]{2,1,0:T(8,128)(2,1)S(1)}, bf16[2,464,128]{2,1,0:T(8,128)(2,1)S(1)}, u32[]{:S(2)}, u32[]{:S(2)}) collective-permute-start(bf16[2,464,128]{2,1,0:T(8,128)(2,1)S(1)} %get-tuple-element.65.refs_0_), channel_id=1, source_target_pairs={{0,2},{1,3},{2,0},{3,1},{4,6},{5,7},{6,4},{7,5},{8,10},{9,11},{10,... | collective-permute-start | bytes 712712 | tf_op jit(solution)/shard_map/ppermute | solution.py:47
  173.0 21.0 %collective-permute-start.21 = (bf16[2,464,128]{2,1,0:T(8,128)(2,1)S(1)}, bf16[2,464,128]{2,1,0:T(8,128)(2,1)S(1)}, u32[]{:S(2)}, u32[]{:S(2)}) collective-permute-start(bf16[2,464,128]{2,1,0:T(8,128)(2,1)S(1)} %get-tuple-element.65.refs_0_), channel_id=1, source_target_pairs={{0,1},{1,2},{2,3},{3,0},{4,5},{5,6},{6,7},{7,4},{8,9},{9,10},{10,1... | collective-permute-start | bytes 712712 | tf_op jit(solution)/shard_map/ppermute | solution.py:47
  189.1 87.6 %collective-permute-start.46 = (bf16[2,464,128]{2,1,0:T(8,128)(2,1)S(1)}, bf16[2,464,128]{2,1,0:T(8,128)(2,1)S(1)}, u32[]{:S(2)}, u32[]{:S(2)}) collective-permute-start(bf16[2,464,128]{2,1,0:T(8,128)(2,1)S(1)} %get-tuple-element.110), channel_id=1, source_target_pairs={{0,4},{1,5},{2,6},{3,7},{4,0},{5,1},{6,2},{7,3},{8,12},{9,13},{10,... | collective-permute-start | bytes 712712 | tf_op jit(solution)/shard_map/ppermute | solution.py:47
  189.3 17.2 %collective-permute-start.11 = (bf16[2,2,464,128]{3,2,1,0:T(8,128)(2,1)S(1)}, bf16[2,2,464,128]{3,2,1,0:T(8,128)(2,1)S(1)}, u32[]{:S(2)}, u32[]{:S(2)}) collective-permute-start(bf16[2,2,464,128]{3,2,1,0:T(8,128)(2,1)S(1)} %pad_maximum_fusion.4.refs_2_), channel_id=1, source_target_pairs={{0,1},{1,2},{2,3},{3,0},{4,5},{5,6},{6,7},{7,4},{8,9},{9,10},{10,1... | collective-permute-start | bytes 1425416 | tf_op jit(solution)/shard_map/ppermute | solution.py:47
  194.1 16.6 %collective-permute-start.40 = (bf16[4,2,464,128]{3,2,1,0:T(8,128)(2,1)S(1)}, bf16[4,2,464,128]{3,2,1,0:T(8,128)(2,1)S(1)}, u32[]{:S(2)}, u32[]{:S(2)}) collective-permute-start(bf16[4,2,464,128]{3,2,1,0:T(8,128)(2,1)S(1)} %pad_maximum_fusion.1), channel_id=1, source_target_pairs={{0,4},{1,5},{2,6},{3,7},{4,0},{5,1},{6,2},{7,3},{8,12},{9,13},{10,... | collective-permute-start | bytes 2850824 | tf_op jit(solution)/shard_map/ppermute | solution.py:47
  194.3 12.2 %collective-permute-start.13 = (bf16[2,2,464,128]{3,2,1,0:T(8,128)(2,1)S(1)}, bf16[2,2,464,128]{3,2,1,0:T(8,128)(2,1)S(1)}, u32[]{:S(2)}, u32[]{:S(2)}) collective-permute-start(bf16[2,2,464,128]{3,2,1,0:T(8,128)(2,1)S(1)} %pad_maximum_fusion.4.refs_2_), channel_id=1, source_target_pairs={{0,3},{1,0},{2,1},{3,2},{4,7},{5,4},{6,5},{7,6},{8,11},{9,8},{10,9... | collective-permute-start | bytes 1425416 | tf_op jit(solution)/shard_map/ppermute | solution.py:47
  199.1 35.8 %collective-permute-start.22 = (bf16[4,2,464,128]{3,2,1,0:T(8,128)(2,1)S(1)}, bf16[4,2,464,128]{3,2,1,0:T(8,128)(2,1)S(1)}, u32[]{:S(2)}, u32[]{:S(2)}) collective-permute-start(bf16[4,2,464,128]{3,2,1,0:T(8,128)(2,1)S(1)} %pad_maximum_fusion), channel_id=1, source_target_pairs={{0,4},{1,5},{2,6},{3,7},{4,0},{5,1},{6,2},{7,3},{8,12},{9,13},{10,... | collective-permute-start | bytes 2850824 | tf_op jit(solution)/shard_map/ppermute | solution.py:47
  206.5 14.7 %collective-permute-start.30 = (bf16[2,464,128]{2,1,0:T(8,128)(2,1)S(1)}, bf16[2,464,128]{2,1,0:T(8,128)(2,1)S(1)}, u32[]{:S(2)}, u32[]{:S(2)}) collective-permute-start(bf16[2,464,128]{2,1,0:T(8,128)(2,1)S(1)} %slice_bitcast_fusion.3), channel_id=1, source_target_pairs={{0,1},{1,2},{2,3},{3,0},{4,5},{5,6},{6,7},{7,4},{8,9},{9,10},{10,1... | collective-permute-start | bytes 712712 | tf_op jit(solution)/shard_map/ppermute | solution.py:47
  206.6 17.3 %collective-permute-start.32 = (bf16[2,464,128]{2,1,0:T(8,128)(2,1)S(1)}, bf16[2,464,128]{2,1,0:T(8,128)(2,1)S(1)}, u32[]{:S(2)}, u32[]{:S(2)}) collective-permute-start(bf16[2,464,128]{2,1,0:T(8,128)(2,1)S(1)} %slice_bitcast_fusion.2), channel_id=1, source_target_pairs={{0,3},{1,0},{2,1},{3,2},{4,7},{5,4},{6,5},{7,6},{8,11},{9,8},{10,9... | collective-permute-start | bytes 712712 | tf_op jit(solution)/shard_map/ppermute | solution.py:47
  210.7 35.4 %collective-permute-start.12 = (bf16[2,464,128]{2,1,0:T(8,128)(2,1)S(1)}, bf16[2,464,128]{2,1,0:T(8,128)(2,1)S(1)}, u32[]{:S(2)}, u32[]{:S(2)}) collective-permute-start(bf16[2,464,128]{2,1,0:T(8,128)(2,1)S(1)} %slice_bitcast_fusion.5), channel_id=1, source_target_pairs={{0,1},{1,2},{2,3},{3,0},{4,5},{5,6},{6,7},{7,4},{8,9},{9,10},{10,1... | collective-permute-start | bytes 712712 | tf_op jit(solution)/shard_map/ppermute | solution.py:47
  221.2 24.9 %collective-permute-start.14 = (bf16[2,464,128]{2,1,0:T(8,128)(2,1)S(1)}, bf16[2,464,128]{2,1,0:T(8,128)(2,1)S(1)}, u32[]{:S(2)}, u32[]{:S(2)}) collective-permute-start(bf16[2,464,128]{2,1,0:T(8,128)(2,1)S(1)} %slice_bitcast_fusion.4), channel_id=1, source_target_pairs={{0,3},{1,0},{2,1},{3,2},{4,7},{5,4},{6,5},{7,6},{8,11},{9,8},{10,9... | collective-permute-start | bytes 712712 | tf_op jit(solution)/shard_map/ppermute | solution.py:47
  255.1 46.1 %collective-permute-start.41 = (bf16[512,1024]{1,0:T(8,128)(2,1)S(1)}, bf16[512,1024]{1,0:T(8,128)(2,1)S(1)}, u32[]{:S(2)}, u32[]{:S(2)}) collective-permute-start(bf16[512,1024]{1,0:T(8,128)(2,1)S(1)} %get-tuple-element.93), channel_id=1, source_target_pairs={{0,8},{8,0},{16,24},{24,16},{32,40},{40,32},{48,56},{56,48},{64,72... | collective-permute-start | bytes 3145736 | tf_op jit(solution)/shard_map/ppermute | solution.py:57
  276.7 24.3 %collective-permute-start.47 = (bf16[2,2,464,128]{3,2,1,0:T(8,128)(2,1)S(1)}, bf16[2,2,464,128]{3,2,1,0:T(8,128)(2,1)S(1)}, u32[]{:S(2)}, u32[]{:S(2)}) collective-permute-start(bf16[2,2,464,128]{3,2,1,0:T(8,128)(2,1)S(1)} %pad_maximum_fusion.6.refs_2_), channel_id=1, source_target_pairs={{0,1},{1,2},{2,3},{3,0},{4,5},{5,6},{6,7},{7,4},{8,9},{9,10},{10,1... | collective-permute-start | bytes 1425416 | tf_op jit(solution)/shard_map/ppermute | solution.py:47
  276.9 12.6 %collective-permute-start.51 = (bf16[2,464,128]{2,1,0:T(8,128)(2,1)S(1)}, bf16[2,464,128]{2,1,0:T(8,128)(2,1)S(1)}, u32[]{:S(2)}, u32[]{:S(2)}) collective-permute-start(bf16[2,464,128]{2,1,0:T(8,128)(2,1)S(1)} %get-tuple-element.108.refs_0_), channel_id=1, source_target_pairs={{0,3},{1,0},{2,1},{3,2},{4,7},{5,4},{6,5},{7,6},{8,11},{9,8},{10,9... | collective-permute-start | bytes 712712 | tf_op jit(solution)/shard_map/ppermute | solution.py:47
  279.6 14.3 %collective-permute-start.52 = (bf16[2,464,128]{2,1,0:T(8,128)(2,1)S(1)}, bf16[2,464,128]{2,1,0:T(8,128)(2,1)S(1)}, u32[]{:S(2)}, u32[]{:S(2)}) collective-permute-start(bf16[2,464,128]{2,1,0:T(8,128)(2,1)S(1)} %get-tuple-element.108.refs_0_), channel_id=1, source_target_pairs={{0,2},{1,3},{2,0},{3,1},{4,6},{5,7},{6,4},{7,5},{8,10},{9,11},{10,... | collective-permute-start | bytes 712712 | tf_op jit(solution)/shard_map/ppermute | solution.py:47
  279.6 21.1 %collective-permute-start.53 = (bf16[2,464,128]{2,1,0:T(8,128)(2,1)S(1)}, bf16[2,464,128]{2,1,0:T(8,128)(2,1)S(1)}, u32[]{:S(2)}, u32[]{:S(2)}) collective-permute-start(bf16[2,464,128]{2,1,0:T(8,128)(2,1)S(1)} %get-tuple-element.108.refs_0_), channel_id=1, source_target_pairs={{0,1},{1,2},{2,3},{3,0},{4,5},{5,6},{6,7},{7,4},{8,9},{9,10},{10,1... | collective-permute-start | bytes 712712 | tf_op jit(solution)/shard_map/ppermute | solution.py:47
  289.4 15.0 %collective-permute-start.49 = (bf16[2,2,464,128]{3,2,1,0:T(8,128)(2,1)S(1)}, bf16[2,2,464,128]{3,2,1,0:T(8,128)(2,1)S(1)}, u32[]{:S(2)}, u32[]{:S(2)}) collective-permute-start(bf16[2,2,464,128]{3,2,1,0:T(8,128)(2,1)S(1)} %pad_maximum_fusion.6.refs_2_), channel_id=1, source_target_pairs={{0,3},{1,0},{2,1},{3,2},{4,7},{5,4},{6,5},{7,6},{8,11},{9,8},{10,9... | collective-permute-start | bytes 1425416 | tf_op jit(solution)/shard_map/ppermute | solution.py:47
  300.8 23.4 %collective-permute-start.54 = (bf16[4,2,464,128]{3,2,1,0:T(8,128)(2,1)S(1)}, bf16[4,2,464,128]{3,2,1,0:T(8,128)(2,1)S(1)}, u32[]{:S(2)}, u32[]{:S(2)}) collective-permute-start(bf16[4,2,464,128]{3,2,1,0:T(8,128)(2,1)S(1)} %pad_maximum_fusion.2), channel_id=1, source_target_pairs={{0,4},{1,5},{2,6},{3,7},{4,0},{5,1},{6,2},{7,3},{8,12},{9,13},{10,... | collective-permute-start | bytes 2850824 | tf_op jit(solution)/shard_map/ppermute | solution.py:47
  301.0 32.0 %collective-permute-start.48 = (bf16[2,464,128]{2,1,0:T(8,128)(2,1)S(1)}, bf16[2,464,128]{2,1,0:T(8,128)(2,1)S(1)}, u32[]{:S(2)}, u32[]{:S(2)}) collective-permute-start(bf16[2,464,128]{2,1,0:T(8,128)(2,1)S(1)} %slice_bitcast_fusion.1), channel_id=1, source_target_pairs={{0,1},{1,2},{2,3},{3,0},{4,5},{5,6},{6,7},{7,4},{8,9},{9,10},{10,1... | collective-permute-start | bytes 712712 | tf_op jit(solution)/shard_map/ppermute | solution.py:47
  301.7 30.9 %collective-permute-start.42 = (bf16[128,1024]{1,0:T(8,128)(2,1)S(1)}, bf16[128,1024]{1,0:T(8,128)(2,1)S(1)}, u32[]{:S(2)}, u32[]{:S(2)}) collective-permute-start(bf16[128,1024]{1,0:T(8,128)(2,1)S(1)} %get-tuple-element.102), channel_id=1, source_target_pairs={{0,32},{8,40},{16,48},{24,56},{32,64},{40,72},{48,80},{56,88},{64,... | collective-permute-start | bytes 786440 | tf_op jit(solution)/shard_map/ppermute | solution.py:57
  301.7 30.8 %collective-permute-start.43 = (bf16[128,1024]{1,0:T(8,128)(2,1)S(1)}, bf16[128,1024]{1,0:T(8,128)(2,1)S(1)}, u32[]{:S(2)}, u32[]{:S(2)}) collective-permute-start(bf16[128,1024]{1,0:T(8,128)(2,1)S(1)} %get-tuple-element.104), channel_id=1, source_target_pairs={{0,96},{8,104},{16,112},{24,120},{32,0},{40,8},{48,16},{56,24},{64... | collective-permute-start | bytes 786440 | tf_op jit(solution)/shard_map/ppermute | solution.py:57
  304.4 28.1 %collective-permute-start.44 = (bf16[128,1024]{1,0:T(8,128)(2,1)S(1)}, bf16[128,1024]{1,0:T(8,128)(2,1)S(1)}, u32[]{:S(2)}, u32[]{:S(2)}) collective-permute-start(bf16[128,1024]{1,0:T(8,128)(2,1)S(1)} %get-tuple-element.103), channel_id=1, source_target_pairs={{0,64},{8,72},{16,80},{24,88},{32,96},{40,104},{48,112},{56,120},{... | collective-permute-start | bytes 786440 | tf_op jit(solution)/shard_map/ppermute | solution.py:57
  (15 other events, 114.9 us)

commit v2 on v0

v2 whole, which is shorter than its diff:
```python
import functools

import jax
import jax.numpy as jnp
from jax import lax
from jax.experimental import pallas as pl
from jax.experimental.pallas import tpu as pltpu
from jax.sharding import PartitionSpec as P

BF = jnp.bfloat16
F32 = jnp.float32
D = 1024
T = 1024
HALF = T // 2
B = 128
FF = 1848
RH = 928
R = RH // 2
N_BLOCK = 512
VMEM = 32 * 1024 * 1024
VMEM_FAR = 44 * 1024 * 1024
VMEM_SUMS = 12 * 1024 * 1024

NT = (((1,), (1,)), ((), ()))
NN = (((1,), (0,)), ((), ()))
TN = (((0,), (0,)), ((), ()))


def dot(a, b, dims):
    return lax.dot_general(a, b, dims, preferred_element_type=F32)


def shape(*dims, dtype=BF):
    return jax.ShapeDtypeStruct(dims, dtype)


def params(limit=VMEM):
    return pltpu.CompilerParams(vmem_limit_bytes=limit)


def cost(flops, nbytes):
    return pl.CostEstimate(flops=int(flops), bytes_accessed=int(nbytes), transcendentals=0)


def narrow_move(value, dxh, dz):
    pairs = [
        (xh * 4 + z, ((xh + dxh) % 2) * 4 + (z + dz) % 4) for xh in range(2) for z in range(4)
    ]
    return lax.ppermute(value, "narrow", pairs)


def wide_move(value, dy, dxl, dc):
    pairs = [
        (y * 4 + xl * 2 + c, ((y + dy) % 4) * 4 + ((xl + dxl) % 2) * 2 + (c + dc) % 2)
        for y in range(4)
        for xl in range(2)
        for c in range(2)
    ]
    return lax.ppermute(value, "wide", pairs)


def first_kernel(which, slots, layout, n_outs, at, *refs):
    sources = sorted({w // 2 for w in which})
    own, other, *refs = refs
    weights, refs = refs[: len(which)], refs[len(which) :]
    outs, refs = refs[:n_outs], refs[n_outs:]
    *targets, sems = refs

    @pl.when(pl.program_id(0) == 0)
    def _():
        copies = []
        for s, (dxh, dz) in enumerate(slots):
            row = pl.ds(pl.multiple_of(lax.rem(at[1] + dz, 4) * B, B), B)
            for k, (source, target) in enumerate(zip(sources, targets)):
                place_, sem = target.at[s * B : (s + 1) * B, :], sems.at[k, s]
                near = pltpu.make_async_copy(own.at[source, row, :], place_, sem)
                far = pltpu.make_async_copy(other.at[source, row, :], place_, sem)
                pl.when(at[0] == dxh)(near.start)
                pl.when(at[0] != dxh)(far.start)
                copies.append(near)
        for copy in copies:
            copy.wait()

    for i, w in enumerate(which):
        res = dot(weights[i][...], targets[sources.index(w // 2)][...], NT).astype(BF)

        def store(outs):
            for out, members in zip(outs, layout):
                for k, s in enumerate(members):
                    value = res[:, s * B : (s + 1) * B]
                    if len(members) > 1:
                        out[k, i] = value
                    else:
                        out[i] = value

        if len(outs) == len(layout):
            store(outs)
        else:
            pl.when(pl.program_id(0) < 2)(functools.partial(store, outs[: len(layout)]))
            pl.when(pl.program_id(0) >= 2)(functools.partial(store, outs[len(layout) :]))


def rows_spec(array, lead=None, step=lambda r: r):
    if array.ndim == 3:
        return pl.BlockSpec((array.shape[0], R, B), lambda r, *_: (0, step(r), 0))
    if lead is None:
        return pl.BlockSpec((*array.shape[:2], R, B), lambda r, *_: (0, 0, step(r), 0))
    return pl.BlockSpec((1, array.shape[1], R, B), lambda r, *_: (lead, 0, step(r), 0))


def first(name, half, slots, layout, at, halves, weights):
    which = (0, 1, 2)
    n = len(which)
    base = 0 if half is None else 2 * half
    weight = pl.BlockSpec((R, D), lambda r, at: (base + r, 0))
    out_shape = [shape(len(m), n, RH, B) if len(m) > 1 else shape(n, RH, B) for m in layout]
    out_specs = [rows_spec(o) for o in out_shape]
    if half is None:
        out_specs = [rows_spec(o, step=lambda r: jnp.minimum(r, 1)) for o in out_shape]
        out_specs += [rows_spec(o, step=lambda r: jnp.maximum(r - 2, 0)) for o in out_shape]
        out_shape = out_shape * 2
    width = len(slots) * B
    steps = 4 if half is None else 2
    return pl.pallas_call(
        functools.partial(first_kernel, which, slots, layout, len(out_shape)),
        out_shape=out_shape,
        grid_spec=pltpu.PrefetchScalarGridSpec(
            num_scalar_prefetch=1,
            grid=(steps,),
            in_specs=[pl.BlockSpec(memory_space=pl.ANY)] * 2 + [weight] * n,
            out_specs=out_specs,
            scratch_shapes=[
                *[pltpu.VMEM((width, D), BF)] * 2,
                pltpu.SemaphoreType.DMA((2, len(slots))),
            ],
        ),
        compiler_params=params(VMEM_FAR if half is None else VMEM),
        cost_estimate=cost(n * 2 * steps * R * width * D, n * steps * R * (D + width) * 2),
        name=name,
    )(at, *halves, *[weights[w] for w in which])


def pick(group, lead, i):
    for ref in group:
        rank = len(ref.shape)
        n = ref.shape[rank - 3]
        if i < n:
            return (ref[lead, i] if rank == 4 else ref[i]).astype(F32)
        i -= n


def grouped(refs, sizes):
    refs = list(refs)
    return [[refs.pop(0) for _ in range(size)] for size in sizes]


def on_groups(name, kernel, groups, out_shape, leads=None):
    leads = leads or [None] * len(groups)
    sizes = [len(g) for g in groups]
    n = sum(sizes)
    arrays = [a for g in groups for a in g]

    def run(*refs):
        kernel(grouped(refs[:n], sizes), refs[n:])

    moved = sum(a.size for a in arrays) + sum(o.size for o in out_shape)
    return pl.pallas_call(
        run,
        out_shape=out_shape,
        grid=(2,),
        in_specs=[rows_spec(a, lead) for g, lead in zip(groups, leads) for a in g],
        out_specs=[rows_spec(o) for o in out_shape],
        compiler_params=params(VMEM_SUMS),
        cost_estimate=cost(moved, moved * 2),
        name=name,
    )(*arrays)


def x_sum(keep, recv, first_lead):
    one = recv.ndim == 3
    n = 1 if one else recv.shape[0]

    def kernel(groups, outs):
        for k, out in enumerate(outs):
            for i in range(3):
                out[i] = (pick(groups[0], first_lead + k, i) + pick(groups[1], k, i)).astype(BF)

    return on_groups(f"x_sum{n}", kernel, [(keep,), (recv,)], [shape(3, RH, B)] * n)


def z_mid(mid1, ra, mid3, rb):
    def kernel(groups, outs):
        for i in range(3):
            outs[0][0, i] = (pick(groups[0], 0, i) + pick(groups[1], 0, i)).astype(BF)
            outs[0][1, i] = pick(groups[0], 1, i).astype(BF)
            outs[1][0, i] = pick(groups[2], 0, i).astype(BF)
            outs[1][1, i] = (pick(groups[2], 1, i) + pick(groups[3], 1, i)).astype(BF)

    return on_groups("z_mid", kernel, [mid1, ra, mid3, rb], [shape(2, 3, RH, B)] * 2)


def z_far(own, u, v):
    def kernel(groups, outs):
        for i in range(3):
            total = pick(groups[0], 0, i) + pick(groups[1], 0, i) + pick(groups[2], 0, i)
            outs[0][i] = total.astype(BF)

    groups = [(own,), (u,), (v,)]
    return on_groups("z_far", kernel, groups, [shape(3, RH, B)], leads=[1, 1, 1])[0]


def swiglu(x_terms, z_terms):
    terms = [*x_terms, *z_terms]

    def kernel(groups, outs):
        alone, both = outs
        for k, mine in enumerate((groups[: len(x_terms)], groups[len(x_terms) :])):
            sums = []
            for i in range(3):
                acc = pick(mine[0], 0, i)
                for group in mine[1:]:
                    acc = acc + pick(group, 0, i)
                sums.append(acc)
            gate, up, grad = sums
            sig = jax.nn.sigmoid(gate)
            silu = gate * sig
            gate_grad = grad * up * sig * (1.0 + gate * (1.0 - sig))
            for i, value in enumerate((gate_grad, grad * silu, silu * up)):
                value = value.astype(BF)
                both[k, i] = value
                if k == 0:
                    alone[i] = value

    out_shape = [shape(3, RH, B), shape(2, 3, RH, B)]
    groups, leads = [(t,) for t, _ in terms], [lead for _, lead in terms]
    return on_groups("swiglu", kernel, groups, out_shape, leads=leads)


def distinct(blocks):
    arrays, places = [], []
    for array, lead, base, dxh, dz in blocks:
        for n, seen in enumerate(arrays):
            if seen is array:
                break
        else:
            n = len(arrays)
            arrays.append(array)
        places.append((n, lead, base, dxh, dz))
    return arrays, places


def place_copies(at, refs, places, targets, sems):
    copies = []
    for k, (n, lead, base, dxh, dz) in enumerate(places):
        column = (lax.rem(at[0] + dxh, 2) * 4 + lax.rem(at[1] + dz, 4)) * B
        part = pl.ds(pl.multiple_of(column, B), B)
        for i, target in enumerate(targets):
            source = refs[n].at[base + i] if lead is None else refs[n].at[lead, base + i]
            copies.append(pltpu.make_async_copy(source, target.at[:, part], sems.at[i, k]))
    return copies


def back_kernel(places, counts, at, *refs):
    refs = list(refs)
    arrays = [[refs.pop(0) for _ in range(count)] for count in counts]
    wg, wu, out_o, out_t, *acts, sems = refs
    halves = (slice(0, RH), slice(RH, 2 * RH))

    @pl.when(pl.program_id(0) == 0)
    def _():
        copies = []
        for half in range(2):
            targets = [act.at[halves[half], :] for act in acts]
            copies += place_copies(at, arrays[half], places[half], targets, sems.at[half])
        for copy in copies:
            copy.start()
        for copy in copies:
            copy.wait()
        last = slice(2 * RH - 16, 2 * RH)
        rows = lax.broadcasted_iota(jnp.int32, (16, T), 0) < FF - (2 * RH - 16)
        for act in acts:
            act[last, :] = jnp.where(rows, act[last, :], jnp.zeros((16, T), BF))

    rows = lax.broadcasted_iota(jnp.int32, (2 * RH, N_BLOCK), 0) < FF
    vg = jnp.where(rows, wg[...], jnp.zeros((2 * RH, N_BLOCK), BF))
    vu = jnp.where(rows, wu[...], jnp.zeros((2 * RH, N_BLOCK), BF))
    for k, out in enumerate((out_o, out_t)):
        part = slice(k * HALF, (k + 1) * HALF)
        total = dot(acts[0][:, part], vg, TN) + dot(acts[1][:, part], vu, TN)
        out[...] = total.astype(out.dtype)


def back(at, blocks_x, blocks_z, weights):
    (arrays_x, places_x), (arrays_z, places_z) = distinct(blocks_x), distinct(blocks_z)
    arrays = arrays_x + arrays_z
    weight = pl.BlockSpec((2 * RH, N_BLOCK), lambda n, at: (0, n))
    out = pl.BlockSpec((HALF, N_BLOCK), lambda n, at: (0, n))
    counts = (len(arrays_x), len(arrays_z))
    return pl.pallas_call(
        functools.partial(back_kernel, (places_x, places_z), counts),
        out_shape=[shape(HALF, D)] * 2,
        grid_spec=pltpu.PrefetchScalarGridSpec(
            num_scalar_prefetch=1,
            grid=(D // N_BLOCK,),
            in_specs=[pl.BlockSpec(memory_space=pl.ANY)] * len(arrays) + [weight] * 2,
            out_specs=[out] * 2,
            scratch_shapes=[pltpu.VMEM((2 * RH, T), BF)] * 2 + [pltpu.SemaphoreType.DMA((2, 2, 8))],
        ),
        compiler_params=params(),
        cost_estimate=cost(2 * 2 * FF * T * D, 2 * FF * (T + D) * 2 + T * D * 2),
        name="back",
    )(at, *arrays, *weights[:2])


def grads_kernel(places, counts, n, at, *refs):
    refs = list(refs)
    arrays = [[refs.pop(0) for _ in range(count)] for count in counts]
    own, other, *refs = refs
    outs, acts, tokens, sems = refs[:n], refs[n : 2 * n], refs[2 * n], refs[2 * n + 1]
    halves = (slice(0, RH), slice(RH, 2 * RH))
    copies = []
    for half in range(2):
        targets = [act.at[halves[half], :] for act in acts]
        copies.append(place_copies(at, arrays[half], places[half], targets, sems.at[half]))
    start = pl.program_id(0) == 0

    @pl.when(start)
    def _():
        for copy in copies[0] + copies[1]:
            copy.start()

    tokens[:HALF, :] = own[0]
    tokens[HALF:, :] = other[0]
    for half, rows in enumerate(halves):

        @pl.when(start)
        def _(half=half):
            for copy in copies[half]:
                copy.wait()

        for out, act in zip(outs, acts):
            out[rows, :] = dot(act[rows, :], tokens[...], NN).astype(BF)


def grads(name, n, at, blocks_x, blocks_z, k, halves):
    (arrays_x, places_x), (arrays_z, places_z) = distinct(blocks_x), distinct(blocks_z)
    arrays = arrays_x + arrays_z
    token = pl.BlockSpec((1, HALF, N_BLOCK), lambda n, at: (k, 0, n))
    out = pl.BlockSpec((2 * RH, N_BLOCK), lambda n, at: (0, n))
    counts = (len(arrays_x), len(arrays_z))
    return pl.pallas_call(
        functools.partial(grads_kernel, (places_x, places_z), counts, n),
        out_shape=[shape(FF, D)] * n,
        grid_spec=pltpu.PrefetchScalarGridSpec(
            num_scalar_prefetch=1,
            grid=(D // N_BLOCK,),
            in_specs=[pl.BlockSpec(memory_space=pl.ANY)] * len(arrays) + [token] * 2,
            out_specs=[out] * n,
            scratch_shapes=[
                *[pltpu.VMEM((2 * RH, T), BF)] * n,
                pltpu.VMEM((T, N_BLOCK), BF),
                pltpu.SemaphoreType.DMA((2, n, 8)),
            ],
        ),
        compiler_params=params(),
        cost_estimate=cost(n * 2 * FF * T * D, n * FF * (T + D) * 2 + T * D * 2),
        name=name,
    )(at, *arrays, *halves)


def after(value, *earlier):
    return lax.optimization_barrier((value, *earlier))[0]


def scatter_tokens(keep, recv):
    total = keep.astype(F32) + recv.astype(F32)
    parts = [total[dy * B : (dy + 1) * B] for dy in range(4)]
    acc = parts[0]
    for dy in (1, 3, 2):
        acc = acc + wide_move(parts[dy].astype(BF), dy, 0, 0).astype(F32)
    far = wide_move(acc[B // 2 :].astype(BF), 0, 1, 0)
    return (acc[: B // 2] + far.astype(F32)).astype(BF)


def body(inputs, grad_out, w_gate, w_up, w_down):
    narrow = lax.axis_index("narrow")
    at = jnp.stack([narrow // 4, narrow % 4]).astype(jnp.int32)
    weights = (w_gate.T, w_up.T, w_down)
    wg, wu = weights[:2]

    pair = jnp.concatenate([inputs, wide_move(inputs, 0, 1, 0)])
    grads_y = jnp.stack([grad_out, *[wide_move(grad_out, -dy, 0, 0) for dy in (1, 2, 3)]])
    pairs = [pair, *[wide_move(pair, -dy, 0, 0) for dy in (1, 2, 3)]]
    grads_x = wide_move(grads_y, 0, 1, 0)
    pairs_g = jnp.stack([grads_y, grads_x], 1).reshape(HALF, D)
    tokens = jnp.stack([jnp.concatenate(pairs), pairs_g])
    halves = (tokens, wide_move(tokens, 0, 0, 1))

    keep2, send2, a2, b2 = first("far", None, ((0, 2), (1, 2)), ((0,), (1,)), at, halves, weights)
    recv2 = narrow_move(send2, 1, 0)
    ra, rb = narrow_move(a2, 0, 1), narrow_move(b2, 0, 3)
    (send,) = first("send", 0, ((1, 1), (1, 3)), ((0, 1),), after(at, a2), halves, weights)
    recv = narrow_move(send, 1, 0)
    mid_slots = ((0, 1), (1, 1), (0, 3), (1, 3))
    mid1, mid3 = first("mid", 1, mid_slots, ((0, 1), (2, 3)), after(at, send), halves, weights)
    u, v = z_mid((mid1,), (ra,), (mid3,), (rb,))
    u, v = after(u, recv2), after(v, recv2)
    u, v = narrow_move(u, 0, 1), narrow_move(v, 0, 3)
    (s2,) = x_sum(keep2, recv2, 0)
    s2 = narrow_move(s2, 0, 2)
    keep_slots = ((1, 0), (0, 0), (0, 1), (0, 3))
    send_0, keep = first("keep", 0, keep_slots, ((0,), (1, 2, 3)), after(at, mid1), halves, weights)
    recv_0 = narrow_move(send_0, 1, 0)
    (own,) = first("own", 1, ((0, 0), (1, 0)), ((0, 1),), after(at, keep), halves, weights)
    far = narrow_move(z_far(own, u, v), 1, 0)
    s1, s3 = x_sum(keep, recv, 1)
    s1, s3 = narrow_move(s1, 0, 1), narrow_move(s3, 0, 3)
    alone, both = swiglu(
        [(keep, 0), (recv_0, None), (s1, None), (s2, None), (s3, None)],
        [(own, 0), (u, 0), (v, 0), (far, None)],
    )

    before, after_, across = [narrow_move(alone, 0, dz) for dz in (1, 3, 2)]
    swapped = narrow_move(both, 1, 0)
    ready = (before, after_, across, swapped)

    def far_blocks(part):
        return after(jnp.stack([t[part] for t in (after_, across, before)]), *ready)

    def pair_of(part):
        return after(jnp.stack([both[1, part], swapped[1, part]]), *ready)

    def x_blocks(first, rest):
        near = [(alone, None, 0, 0), (after_, None, 0, 1), (across, None, 0, 2), (before, None, 0, 3)]
        far = [(swapped, 0, 1, 0)] + [(rest, k, 1, k + 1) for k in range(3)]
        return [(a, lead, first if a is not rest else 0, *at_) for a, lead, *at_ in near + far]

    def z_blocks(first, pair, after_, before, near, far):
        blocks = [(near, None, 0, 0, 2), (far, None, 0, 1, 2)]
        for dz, source in ((0, pair), (1, after_), (3, before)):
            blocks += [(source, k, 0, k, dz) for k in range(2)]
        return blocks

    gu, hid = slice(0, 2), slice(2, 3)
    pair = pair_of(gu)
    z_before, z_after = narrow_move(pair, 0, 1), narrow_move(pair, 0, 3)
    rest = narrow_move(far_blocks(gu), 1, 0)
    near, far = narrow_move(z_before[0], 0, 1), narrow_move(z_after[1], 0, 3)
    blocks_x = x_blocks(0, rest)
    blocks_z = z_blocks(0, pair, z_after, z_before, near, far)

    pair = after(pair_of(hid), z_before, z_after)
    z_before, z_after = narrow_move(pair, 0, 1), narrow_move(pair, 0, 3)
    rest_hid = narrow_move(after(far_blocks(hid), rest), 1, 0)
    hid_near, hid_far = narrow_move(z_before[0], 0, 1), narrow_move(z_after[1], 0, 3)
    hid_x = x_blocks(2, rest_hid)
    hid_z = z_blocks(2, pair, z_after, z_before, hid_near, hid_far)

    keep, send = back(after(at, z_before, z_after), blocks_x, blocks_z, weights)
    from_core = wide_move(send, 0, 0, 1)
    grad_input = scatter_tokens(keep, from_core)

    grad_gate, grad_up = grads("grads", 2, after(at, from_core, hid_near, hid_far), blocks_x, blocks_z, 0, halves)
    (grad_down,) = grads("down", 1, after(at, grad_gate), hid_x, hid_z, 1, halves)
    return grad_input, grad_gate.T, grad_up.T, grad_down


def solution(mesh):
    return jax.shard_map(
        body,
        mesh=mesh,
        in_specs=(
            P("wide", "narrow"),
            P("wide", "narrow"),
            P("narrow", "wide"),
            P("narrow", "wide"),
            P("wide", "narrow"),
        ),
        out_specs=(
            P("wide", "narrow"),
            P("narrow", "wide"),
            P("narrow", "wide"),
            P("wide", "narrow"),
        ),
        check_vma=False,
    )
```

time: 567 us -> 262 us (0.46)
  waiting for transfers between devices: 456 us -> 124 us
  Pallas kernels: 0 us -> 72 us
  matrix products: 64.7 us -> 0 us
  starting transfers between devices: 0.5 us -> 58.2 us
  local copies, waits for them, and re-layouts: 19.8 us -> 3.56 us
  between operations: 14.2 us -> 1.05 us
  other arithmetic: 8.97 us -> 3.03 us
    all_gather x5 -> x0, waiting for transfers between devices: 233 us -> none  [the longest x1 66.7 us: body(): lax.all_gather(gate_grad, 'narrow', axis=0, tiled=True)]
    unnamed x10 -> x0, waiting for transfers between devices: 168 us -> none
    ppermute x0 -> x39, waiting for transfers between devices: none -> 124 us  [the longest x25 106 us: narrow_move(): return lax.ppermute(value, 'narrow', pairs)]
    pallas_call x0 -> x13, Pallas kernels: none -> 72 us  [the longest x5 31 us: first(): pl.pallas_call(functools.partial(first_kernel, which, slots, layout, len(...]
    dot_general x8 -> x0, matrix products: 64.7 us -> none  [the longest x1 10.3 us: body(): lax.dot_general(up_all, w_up, last_contract, preferred_element_type=jnp.f...]
    ppermute x0 -> x39, starting transfers between devices: none -> 58.2 us  [the longest x25 35.8 us: narrow_move(): return lax.ppermute(value, 'narrow', pairs)]
    reduce_scatter x1 -> x0, waiting for transfers between devices: 54.9 us -> none  [body(): lax.psum_scatter((lax.dot_general(gate_all, w_gate, last_contract, prefer...]
    unnamed x14 -> x11, local copies, waits for them, and re-layouts: 19.8 us -> 3.04 us
  transfers between devices with their start and end apart: 8 -> 39, of which waited for: 8 -> 20; matrix products, arithmetic and copies ran while one was open for 16% -> 1% of each run, Pallas kernels for 0% -> 16%
where the time goes in v2:
time: 262 us; the launch traced here: 261 us
  waiting for transfers between devices  124 us (47%)
  Pallas kernels  72 us (27%)
  starting transfers between devices  58.2 us (22%)
  local copies, waits for them, and re-layouts  3.56 us (1%)
  other arithmetic  3.03 us (1%)
    ppermute x25, waiting for transfers between devices, narrow_move(): return lax.ppermute(value, 'narrow', pairs)  106 us
    ppermute x25, starting transfers between devices, narrow_move(): return lax.ppermute(value, 'narrow', pairs)  35.8 us
    pallas_call x5, Pallas kernels, first(): pl.pallas_call(functools.partial(first_kernel, which, slots, layout, len(...  31 us
    pallas_call x2, Pallas kernels, grads(): pl.pallas_call(functools.partial(grads_kernel, (places_x, places_z), coun...  23.7 us
    ppermute x14, starting transfers between devices, wide_move(): return lax.ppermute(value, 'wide', pairs)  22.4 us
    ppermute x14, waiting for transfers between devices, wide_move(): return lax.ppermute(value, 'wide', pairs)  17.2 us
    pallas_call x1, Pallas kernels, back(): pl.pallas_call(functools.partial(back_kernel, (places_x, places_z), count...  12.9 us
  transfers between devices with their start and end apart: 39, of which 20 were waited for; matrix products, arithmetic and copies ran while one was open for 1% of the time, Pallas kernels for 16%

profile of v2, /device:TPU:1, one launch (start us, length us, event | category | flops | bytes accessed | tf_op | source)
XLA Modules:
  0.0 261.5 jit_solution(1800008952702422842)
XLA Ops:
  0.6 2.1 collective-permute-start
  2.8 1.3 collective-permute-start.6
  4.0 2.6 %collective-permute-start.5 = (bf16[64,1024]{1,0:T(8,128)(2,1)}, bf16[64,1024]{1,0:T(8,128)(2,1)S(1)}, u32[]{:S(2)}, u32[]{:S(2)}) collective-permute-start(bf16[64,1024]{1,0:T(8,128)(2,1)} %param.6), channel_id=1, source_target_pairs={{0,64},{8,72},{16,80},{24,88},{32,96},{40,104},{48,112},{56,120},{... | collective-permute-start | bytes 393224 | tf_op jit(solution)/shard_map/ppermute | solution.py:59
  8.9 3.0 %collective-permute-done.5 = bf16[64,1024]{1,0:T(8,128)(2,1)S(1)} collective-permute-done((bf16[64,1024]{1,0:T(8,128)(2,1)}, bf16[64,1024]{1,0:T(8,128)(2,1)S(1)}, u32[]{:S(2)}, u32[]{:S(2)}) %collective-permute-start.5) | collective-permute-done | bytes 131104 | tf_op jit(solution)/shard_map/ppermute | solution.py:59
  13.5 2.1 collective-permute-start.2
  16.5 1.4 collective-permute-done.1
  18.0 2.4 collective-permute-done.2
  20.3 6.2 %collective-permute-done.3 = bf16[128,1024]{1,0:T(8,128)(2,1)S(1)} collective-permute-done((bf16[128,1024]{1,0:T(8,128)(2,1)S(1)}, bf16[128,1024]{1,0:T(8,128)(2,1)S(1)}, u32[]{:S(2)}, u32[]{:S(2)}) %collective-permute-start.3) | collective-permute-done | bytes 262176 | tf_op jit(solution)/shard_map/ppermute | solution.py:59
  27.0 2.9 %collective-permute-start.8 = (bf16[2,512,1024]{2,1,0:T(8,128)(2,1)S(1)}, bf16[2,512,1024]{2,1,0:T(8,128)(2,1)}, u32[]{:S(2)}, u32[]{:S(2)}) collective-permute-start(bf16[2,512,1024]{2,1,0:T(8,128)(2,1)S(1)} %pad_maximum_fusion.refs_0_.refs_11_), channel_id=1, source_target_pairs={{0,8},{8,0},{16,24},{24,16},{32,40},{40,32},{48,56},{56,48},{64,72... | collective-permute-start | bytes 6291464 | tf_op jit(solution)/shard_map/ppermute | solution.py:59
  29.9 3.8 %collective-permute-done.8.refs_1_.refs_12_ = bf16[2,512,1024]{2,1,0:T(8,128)(2,1)} collective-permute-done((bf16[2,512,1024]{2,1,0:T(8,128)(2,1)S(1)}, bf16[2,512,1024]{2,1,0:T(8,128)(2,1)}, u32[]{:S(2)}, u32[]{:S(2)}) %collective-permute-start.8) | collective-permute-done | bytes 2097184 | tf_op jit(solution)/shard_map/ppermute | solution.py:59
  33.7 12.7 %far.1 = (bf16[3,928,128]{2,1,0:T(8,128)(2,1)S(1)}, bf16[3,928,128]{2,1,0:T(8,128)(2,1)S(1)}, bf16[3,928,128]{2,1,0:T(8,128)(2,1)S(1)}, bf16[3,928,128]{2,1,0:T(8,128)(2,1)S(1)}) custom-call(s32[2]{0:T(128)S(1)} %pad_add_fusion.at, bf16[2,512,1024]{2,1,0:T(8,128)(2,1)S(1)} %pad_maximum_fusion.refs_0_.refs_11_, ...), custom_call_target="tpu_custom_call" | custom-call | flops 2919235584 | bytes 14254080 | tf_op jit(solution)/shard_map/far/pallas_call | solution.py:124
  46.4 1.9 collective-permute-start.15
  48.3 2.2 collective-permute-start.16
  50.5 2.7 %collective-permute-start.12 = (bf16[3,928,128]{2,1,0:T(8,128)(2,1)S(1)}, bf16[3,928,128]{2,1,0:T(8,128)(2,1)S(1)}, u32[]{:S(2)}, u32[]{:S(2)}) collective-permute-start(bf16[3,928,128]{2,1,0:T(8,128)(2,1)S(1)} %get-tuple-element.46), channel_id=1, source_target_pairs={{0,4},{1,5},{2,6},{3,7},{4,0},{5,1},{6,2},{7,3},{8,12},{9,13},{10,... | collective-permute-start | bytes 2138120 | tf_op jit(solution)/shard_map/ppermute | solution.py:49
  53.2 2.1 copy-done.2
  55.3 3.8 %send.1 = bf16[2,3,928,128]{3,2,1,0:T(8,128)(2,1)S(1)} custom-call(s32[2]{0:T(128)S(1)} %pad_add_fusion.at, bf16[2,512,1024]{2,1,0:T(8,128)(2,1)S(1)} %pad_maximum_fusion.refs_0_.refs_11_, bf16[2,512,1024]{2,1,0:T(8,128)(2,1)} %collective-permute-done.8.refs_1_.refs_12_, bf16[1848,1024]{1,0:T(8,128)(2,1)S(1)} %bitcast.36, bf16[1848,1024]{1,0:T(8,128)(2,1)S(1)} %bitcast.42, ...), custom_call_target="tpu_custom_call" | custom-call | flops 1459617792 | bytes 7127040 | tf_op jit(solution)/shard_map/send/pallas_call | solution.py:124
  59.3 5.5 %mid.1 = (bf16[2,3,928,128]{3,2,1,0:T(8,128)(2,1)S(1)}, bf16[2,3,928,128]{3,2,1,0:T(8,128)(2,1)S(1)}) custom-call(s32[2]{0:T(128)S(1)} %pad_add_fusion.at, bf16[2,512,1024]{2,1,0:T(8,128)(2,1)S(1)} %pad_maximum_fusion.refs_0_.refs_11_, bf16[2,512,1024]{2,1,0:T(8,128)(2,1)} %collective-permute-done.8.refs_1_.refs_12_, bf16[1848,1024]{1,0:T(8,128)(2,1)S(1)} %bitcast.37, ...), custom_call_target="tpu_custom_call" | custom-call | flops 2919235584 | bytes 8552448 | tf_op jit(solution)/shard_map/mid/pallas_call | solution.py:124
  64.8 1.7 collective-permute-done.15.refs_1_
  67.5 1.4 collective-permute-done.12.refs_1_
  68.9 2.7 %collective-permute-start.18 = (bf16[2,3,928,128]{3,2,1,0:T(8,128)(2,1)S(1)}, bf16[2,3,928,128]{3,2,1,0:T(8,128)(2,1)S(1)}, u32[]{:S(2)}, u32[]{:S(2)}) collective-permute-start(bf16[2,3,928,128]{3,2,1,0:T(8,128)(2,1)S(1)} %get-tuple-element.54), channel_id=1, source_target_pairs={{0,3},{1,0},{2,1},{3,2},{4,7},{5,4},{6,5},{7,6},{8,11},{9,8},{10,9... | collective-permute-start | bytes 4276232 | tf_op jit(solution)/shard_map/ppermute | solution.py:49
  71.6 5.3 %keep.1 = (bf16[3,928,128]{2,1,0:T(8,128)(2,1)S(1)}, bf16[3,3,928,128]{3,2,1,0:T(8,128)(2,1)S(1)}) custom-call(s32[2]{0:T(128)S(1)} %pad_add_fusion.at, bf16[2,512,1024]{2,1,0:T(8,128)(2,1)S(1)} %pad_maximum_fusion.refs_0_.refs_11_, bf16[2,512,1024]{2,1,0:T(8,128)(2,1)} %collective-permute-done.8.refs_1_.refs_12_, bf16[1848,1024]{1,0:T(8,128)(2,1)S(1)} %bitcast.38, ...), custom_call_target="tpu_custom_call" | custom-call | flops 2919235584 | bytes 8552448 | tf_op jit(solution)/shard_map/keep/pallas_call | solution.py:124
  76.9 3.3 %collective-permute-start.9 = (bf16[3,928,128]{2,1,0:T(8,128)(2,1)S(1)}, bf16[3,928,128]{2,1,0:T(8,128)(2,1)S(1)}, u32[]{:S(2)}, u32[]{:S(2)}) collective-permute-start(bf16[3,928,128]{2,1,0:T(8,128)(2,1)S(1)} %get-tuple-element.43), channel_id=1, source_target_pairs={{0,4},{1,5},{2,6},{3,7},{4,0},{5,1},{6,2},{7,3},{8,12},{9,13},{10,... | collective-permute-start | bytes 2138120 | tf_op jit(solution)/shard_map/ppermute | solution.py:49
  80.2 3.7 %own.1.refs_0_.refs_5_ = bf16[2,3,928,128]{3,2,1,0:T(8,128)(2,1)S(1)} custom-call(s32[2]{0:T(128)S(1)} %pad_add_fusion.at, bf16[2,512,1024]{2,1,0:T(8,128)(2,1)S(1)} %pad_maximum_fusion.refs_0_.refs_11_, bf16[2,512,1024]{2,1,0:T(8,128)(2,1)} %collective-permute-done.8.refs_1_.refs_12_, bf16[1848,1024]{1,0:T(8,128)(2,1)S(1)} %bitcast.39, ...), custom_call_target="tpu_custom_call" | custom-call | flops 1459617792 | bytes 7127040 | tf_op jit(solution)/shard_map/own/pallas_call | solution.py:124
  84.4 15.1 %collective-permute-done.10.refs_1_ = bf16[2,3,928,128]{3,2,1,0:T(8,128)(2,1)S(1)} collective-permute-done((bf16[2,3,928,128]{3,2,1,0:T(8,128)(2,1)S(1)}, bf16[2,3,928,128]{3,2,1,0:T(8,128)(2,1)S(1)}, u32[]{:S(2)}, u32[]{:S(2)}) %collective-permute-start.10) | collective-permute-done | bytes 1425440 | tf_op jit(solution)/shard_map/ppermute | solution.py:49
  101.3 1.6 collective-permute-start.14
  103.4 2.8 %collective-permute-start.19 = (bf16[3,928,128]{2,1,0:T(8,128)(2,1)S(1)}, bf16[3,928,128]{2,1,0:T(8,128)(2,1)S(1)}, u32[]{:S(2)}, u32[]{:S(2)}) collective-permute-start(bf16[3,928,128]{2,1,0:T(8,128)(2,1)S(1)} %z_far.1), channel_id=1, source_target_pairs={{0,4},{1,5},{2,6},{3,7},{4,0},{5,1},{6,2},{7,3},{8,12},{9,13},{10,... | collective-permute-start | bytes 2138120 | tf_op jit(solution)/shard_map/ppermute | solution.py:49
  106.2 8.5 %collective-permute-done.9.refs_1_ = bf16[3,928,128]{2,1,0:T(8,128)(2,1)S(1)} collective-permute-done((bf16[3,928,128]{2,1,0:T(8,128)(2,1)S(1)}, bf16[3,928,128]{2,1,0:T(8,128)(2,1)S(1)}, u32[]{:S(2)}, u32[]{:S(2)}) %collective-permute-start.9) | collective-permute-done | bytes 712736 | tf_op jit(solution)/shard_map/ppermute | solution.py:49
  114.7 17.6 %collective-permute-done.11.refs_2_ = bf16[3,928,128]{2,1,0:T(8,128)(2,1)S(1)} collective-permute-done((bf16[3,928,128]{2,1,0:T(8,128)(2,1)S(1)}, bf16[3,928,128]{2,1,0:T(8,128)(2,1)S(1)}, u32[]{:S(2)}, u32[]{:S(2)}) %collective-permute-start.11) | collective-permute-done | bytes 712736 | tf_op jit(solution)/shard_map/ppermute | solution.py:49
  132.3 1.8 swiglu.1
  134.1 2.7 %collective-permute-start.20 = (bf16[2,3,928,128]{3,2,1,0:T(8,128)(2,1)S(1)}, bf16[2,3,928,128]{3,2,1,0:T(8,128)(2,1)S(1)}, u32[]{:S(2)}, u32[]{:S(2)}) collective-permute-start(bf16[2,3,928,128]{3,2,1,0:T(8,128)(2,1)S(1)} %get-tuple-element.55), channel_id=1, source_target_pairs={{0,4},{1,5},{2,6},{3,7},{4,0},{5,1},{6,2},{7,3},{8,12},{9,13},{10,... | collective-permute-start | bytes 4276232 | tf_op jit(solution)/shard_map/ppermute | solution.py:49
  136.9 2.7 %collective-permute-start.22 = (bf16[3,928,128]{2,1,0:T(8,128)(2,1)S(1)}, bf16[3,928,128]{2,1,0:T(8,128)(2,1)S(1)}, u32[]{:S(2)}, u32[]{:S(2)}) collective-permute-start(bf16[3,928,128]{2,1,0:T(8,128)(2,1)S(1)} %get-tuple-element.56.refs_0_), channel_id=1, source_target_pairs={{0,3},{1,0},{2,1},{3,2},{4,7},{5,4},{6,5},{7,6},{8,11},{9,8},{10,9... | collective-permute-start | bytes 2138120 | tf_op jit(solution)/shard_map/ppermute | solution.py:49
  140.6 12.6 %collective-permute-done.21.refs_3_ = bf16[3,928,128]{2,1,0:T(8,128)(2,1)S(1)} collective-permute-done((bf16[3,928,128]{2,1,0:T(8,128)(2,1)S(1)}, bf16[3,928,128]{2,1,0:T(8,128)(2,1)S(1)}, u32[]{:S(2)}, u32[]{:S(2)}) %collective-permute-start.21) | collective-permute-done | bytes 712736 | tf_op jit(solution)/shard_map/ppermute | solution.py:49
  153.2 13.2 %collective-permute-done.20.refs_4_ = bf16[2,3,928,128]{3,2,1,0:T(8,128)(2,1)S(1)} collective-permute-done((bf16[2,3,928,128]{3,2,1,0:T(8,128)(2,1)S(1)}, bf16[2,3,928,128]{3,2,1,0:T(8,128)(2,1)S(1)}, u32[]{:S(2)}, u32[]{:S(2)}) %collective-permute-start.20) | collective-permute-done | bytes 1425440 | tf_op jit(solution)/shard_map/ppermute | solution.py:49
  166.6 2.7 %collective-permute-done.23.refs_2_ = bf16[3,928,128]{2,1,0:T(8,128)(2,1)S(1)} collective-permute-done((bf16[3,928,128]{2,1,0:T(8,128)(2,1)S(1)}, bf16[3,928,128]{2,1,0:T(8,128)(2,1)S(1)}, u32[]{:S(2)}, u32[]{:S(2)}) %collective-permute-start.23) | collective-permute-done | bytes 712736 | tf_op jit(solution)/shard_map/ppermute | solution.py:49
  169.8 2.1 collective-permute-start.25
  172.7 16.7 %collective-permute-done.24.refs_10_ = bf16[2,2,928,128]{3,2,1,0:T(8,128)(2,1)S(1)} collective-permute-done((bf16[2,2,928,128]{3,2,1,0:T(8,128)(2,1)S(1)}, bf16[2,2,928,128]{3,2,1,0:T(8,128)(2,1)S(1)}, u32[]{:S(2)}, u32[]{:S(2)}) %collective-permute-start.24) | collective-permute-done | bytes 950304 | tf_op jit(solution)/shard_map/ppermute | solution.py:49
  189.7 2.4 collective-permute-start.27
  192.3 2.9 %collective-permute-start.30 = (bf16[2,928,128]{2,1,0:T(8,128)(2,1)S(1)}, bf16[2,928,128]{2,1,0:T(8,128)(2,1)S(1)}, u32[]{:S(2)}, u32[]{:S(2)}) collective-permute-start(bf16[2,928,128]{2,1,0:T(8,128)(2,1)S(1)} %slice_bitcast_fusion), channel_id=1, source_target_pairs={{0,3},{1,0},{2,1},{3,2},{4,7},{5,4},{6,5},{7,6},{8,11},{9,8},{10,9... | collective-permute-start | bytes 1425416 | tf_op jit(solution)/shard_map/ppermute | solution.py:49
  195.2 3.5 %collective-permute-done.26.refs_10_ = bf16[2,1,928,128]{3,2,1,0:T(8,128)(2,1)S(1)} collective-permute-done((bf16[2,1,928,128]{3,2,1,0:T(8,128)(2,1)S(1)}, bf16[2,1,928,128]{3,2,1,0:T(8,128)(2,1)S(1)}, u32[]{:S(2)}, u32[]{:S(2)}) %collective-permute-start.26) | collective-permute-done | bytes 475168 | tf_op jit(solution)/shard_map/ppermute | solution.py:49
  198.8 3.6 %collective-permute-done.28.refs_5_ = bf16[3,2,928,128]{3,2,1,0:T(8,128)(2,1)S(1)} collective-permute-done((bf16[3,2,928,128]{3,2,1,0:T(8,128)(2,1)S(1)}, bf16[3,2,928,128]{3,2,1,0:T(8,128)(2,1)S(1)}, u32[]{:S(2)}, u32[]{:S(2)}) %collective-permute-start.28) | collective-permute-done | bytes 1425440 | tf_op jit(solution)/shard_map/ppermute | solution.py:49
  202.3 6.6 %collective-permute-done.29.refs_6_ = bf16[2,928,128]{2,1,0:T(8,128)(2,1)S(1)} collective-permute-done((bf16[2,928,128]{2,1,0:T(8,128)(2,1)S(1)}, bf16[2,928,128]{2,1,0:T(8,128)(2,1)S(1)}, u32[]{:S(2)}, u32[]{:S(2)}) %collective-permute-start.29) | collective-permute-done | bytes 475168 | tf_op jit(solution)/shard_map/ppermute | solution.py:49
  208.9 12.9 %back.1 = (bf16[512,1024]{1,0:T(8,128)(2,1)S(1)}, bf16[512,1024]{1,0:T(8,128)(2,1)S(1)}) custom-call(s32[2]{0:T(128)S(1)} %pad_add_fusion.at, bf16[3,928,128]{2,1,0:T(8,128)(2,1)S(1)} %get-tuple-element.56.refs_0_, bf16[3,928,128]{2,1,0:T(8,128)(2,1)S(1)} %collective-permute-done.22.refs_1_, bf16[3,928,128]{2,1,0:T(8,128)(2,1)S(1)} %collective-permute-done.23.refs_2_, ...), custom_call_target="tpu_custom_call" | custom-call | flops 7751073792 | bytes 17235968 | tf_op jit(solution)/shard_map/back/pallas_call | solution.py:299
  221.8 5.4 %collective-permute-start.31 = (bf16[512,1024]{1,0:T(8,128)(2,1)S(1)}, bf16[512,1024]{1,0:T(8,128)(2,1)S(1)}, u32[]{:S(2)}, u32[]{:S(2)}) collective-permute-start(bf16[512,1024]{1,0:T(8,128)(2,1)S(1)} %get-tuple-element.63), channel_id=1, source_target_pairs={{0,8},{8,0},{16,24},{24,16},{32,40},{40,32},{48,56},{56,48},{64,72... | collective-permute-start | bytes 3145736 | tf_op jit(solution)/shard_map/ppermute | solution.py:59
  227.9 2.4 collective-permute-start.37
  231.1 1.7 collective-permute-start.34
  233.9 2.1 collective-permute-done.36.refs_6_
  236.6 14.8 %grads.1 = (bf16[1848,1024]{1,0:T(8,128)(2,1)}, bf16[1848,1024]{1,0:T(8,128)(2,1)}) custom-call(s32[2]{0:T(128)S(1)} %pad_add_fusion.at, bf16[3,928,128]{2,1,0:T(8,128)(2,1)S(1)} %get-tuple-element.56.refs_0_, bf16[3,928,128]{2,1,0:T(8,128)(2,1)S(1)} %collective-permute-done.22.refs_1_, bf16[3,928,128]{2,1,0:T(8,128)(2,1)S(1)} %collective-permute-done.23.refs_2_, ...), custom_call_target="tpu_custom_call" | custom-call | flops 7751073792 | bytes 17235968 | tf_op jit(solution)/shard_map/grads/pallas_call | solution.py:351
  251.8 8.9 %down.1 = bf16[1848,1024]{1,0:T(8,128)(2,1)} custom-call(s32[2]{0:T(128)S(1)} %pad_add_fusion.at, bf16[3,928,128]{2,1,0:T(8,128)(2,1)S(1)} %get-tuple-element.56.refs_0_, bf16[3,928,128]{2,1,0:T(8,128)(2,1)S(1)} %collective-permute-done.22.refs_1_, bf16[3,928,128]{2,1,0:T(8,128)(2,1)S(1)} %collective-permute-done.23.refs_2_, ...), custom_call_target="tpu_custom_call" | custom-call | flops 3875536896 | bytes 9666560 | tf_op jit(solution)/shard_map/down/pallas_call | solution.py:351
  (84 shorter events, 16.1 us)
Async XLA Ops:
  0.6 8.0 %collective-permute-start = (bf16[64,1024]{1,0:T(8,128)(2,1)}, bf16[64,1024]{1,0:T(8,128)(2,1)S(1)}, u32[]{:S(2)}, u32[]{:S(2)}) collective-permute-start(bf16[64,1024]{1,0:T(8,128)(2,1)} %param.5), channel_id=1, source_target_pairs={{0,16},{8,24},{16,0},{24,8},{32,48},{40,56},{48,32},{56,40},{64,80... | collective-permute-start | bytes 393224 | tf_op jit(solution)/shard_map/ppermute | solution.py:59
  2.8 6.2 %collective-permute-start.6 = (bf16[64,1024]{1,0:T(8,128)(2,1)}, bf16[64,1024]{1,0:T(8,128)(2,1)S(1)}, u32[]{:S(2)}, u32[]{:S(2)}) collective-permute-start(bf16[64,1024]{1,0:T(8,128)(2,1)} %param.6), channel_id=1, source_target_pairs={{0,32},{8,40},{16,48},{24,56},{32,64},{40,72},{48,80},{56,88},{64,... | collective-permute-start | bytes 393224 | tf_op jit(solution)/shard_map/ppermute | solution.py:59
  4.0 7.9 %collective-permute-start.5 = (bf16[64,1024]{1,0:T(8,128)(2,1)}, bf16[64,1024]{1,0:T(8,128)(2,1)S(1)}, u32[]{:S(2)}, u32[]{:S(2)}) collective-permute-start(bf16[64,1024]{1,0:T(8,128)(2,1)} %param.6), channel_id=1, source_target_pairs={{0,64},{8,72},{16,80},{24,88},{32,96},{40,104},{48,112},{56,120},{... | collective-permute-start | bytes 393224 | tf_op jit(solution)/shard_map/ppermute | solution.py:59
  6.7 5.6 %collective-permute-start.4 = (bf16[64,1024]{1,0:T(8,128)(2,1)}, bf16[64,1024]{1,0:T(8,128)(2,1)S(1)}, u32[]{:S(2)}, u32[]{:S(2)}) collective-permute-start(bf16[64,1024]{1,0:T(8,128)(2,1)} %param.6), channel_id=1, source_target_pairs={{0,96},{8,104},{16,112},{24,120},{32,0},{40,8},{48,16},{56,24},{64... | collective-permute-start | bytes 393224 | tf_op jit(solution)/shard_map/ppermute | solution.py:59
  8.7 9.2 %collective-permute-start.1 = (bf16[128,1024]{1,0:T(8,128)(2,1)S(1)}, bf16[128,1024]{1,0:T(8,128)(2,1)S(1)}, u32[]{:S(2)}, u32[]{:S(2)}) collective-permute-start(bf16[128,1024]{1,0:T(8,128)(2,1)S(1)} %get-tuple-element.77), channel_id=1, source_target_pairs={{0,96},{8,104},{16,112},{24,120},{32,0},{40,8},{48,16},{56,24},{64... | collective-permute-start | bytes 786440 | tf_op jit(solution)/shard_map/ppermute | solution.py:59
  13.3 13.3 %collective-permute-start.7 = (bf16[4,64,1024]{2,1,0:T(8,128)(2,1)S(1)}, bf16[4,64,1024]{2,1,0:T(8,128)(2,1)S(1)}, u32[]{:S(2)}, u32[]{:S(2)}) collective-permute-start(bf16[4,64,1024]{2,1,0:T(8,128)(2,1)S(1)} %get-tuple-element.76), channel_id=1, source_target_pairs={{0,16},{8,24},{16,0},{24,8},{32,48},{40,56},{48,32},{56,40},{64,80... | collective-permute-start | bytes 1572872 | tf_op jit(solution)/shard_map/ppermute | solution.py:59
  13.5 6.9 %collective-permute-start.2 = (bf16[128,1024]{1,0:T(8,128)(2,1)S(1)}, bf16[128,1024]{1,0:T(8,128)(2,1)S(1)}, u32[]{:S(2)}, u32[]{:S(2)}) collective-permute-start(bf16[128,1024]{1,0:T(8,128)(2,1)S(1)} %get-tuple-element.77), channel_id=1, source_target_pairs={{0,64},{8,72},{16,80},{24,88},{32,96},{40,104},{48,112},{56,120},{... | collective-permute-start | bytes 786440 | tf_op jit(solution)/shard_map/ppermute | solution.py:59
  15.5 11.0 %collective-permute-start.3 = (bf16[128,1024]{1,0:T(8,128)(2,1)S(1)}, bf16[128,1024]{1,0:T(8,128)(2,1)S(1)}, u32[]{:S(2)}, u32[]{:S(2)}) collective-permute-start(bf16[128,1024]{1,0:T(8,128)(2,1)S(1)} %get-tuple-element.77), channel_id=1, source_target_pairs={{0,32},{8,40},{16,48},{24,56},{32,64},{40,72},{48,80},{56,88},{64,... | collective-permute-start | bytes 786440 | tf_op jit(solution)/shard_map/ppermute | solution.py:59
  27.0 6.8 %collective-permute-start.8 = (bf16[2,512,1024]{2,1,0:T(8,128)(2,1)S(1)}, bf16[2,512,1024]{2,1,0:T(8,128)(2,1)}, u32[]{:S(2)}, u32[]{:S(2)}) collective-permute-start(bf16[2,512,1024]{2,1,0:T(8,128)(2,1)S(1)} %pad_maximum_fusion.refs_0_.refs_11_), channel_id=1, source_target_pairs={{0,8},{8,0},{16,24},{24,16},{32,40},{40,32},{48,56},{56,48},{64,72... | collective-permute-start | bytes 6291464 | tf_op jit(solution)/shard_map/ppermute | solution.py:59
  33.7 19.5 %copy-start = (bf16[1848,1024]{1,0:T(8,128)(2,1)S(1)}, bf16[1848,1024]{1,0:T(8,128)(2,1)}, u32[]{:S(2)}) copy-start(bf16[1848,1024]{1,0:T(8,128)(2,1)} %refs_4_.9) | copy-start | bytes 11354116
  33.7 19.5 %copy-start.1 = (bf16[1024,1848]{0,1:T(8,128)(2,1)S(1)}, bf16[1024,1848]{0,1:T(8,128)(2,1)}, u32[]{:S(2)}) copy-start(bf16[1024,1848]{0,1:T(8,128)(2,1)} %param.7) | copy-start | bytes 11354116
  46.4 20.1 %collective-permute-start.15 = (bf16[3,928,128]{2,1,0:T(8,128)(2,1)S(1)}, bf16[3,928,128]{2,1,0:T(8,128)(2,1)S(1)}, u32[]{:S(2)}, u32[]{:S(2)}) collective-permute-start(bf16[3,928,128]{2,1,0:T(8,128)(2,1)S(1)} %get-tuple-element.37), channel_id=1, source_target_pairs={{0,1},{1,2},{2,3},{3,0},{4,5},{5,6},{6,7},{7,4},{8,9},{9,10},{10,1... | collective-permute-start | bytes 2138120 | tf_op jit(solution)/shard_map/ppermute | solution.py:49
  48.3 18.2 %collective-permute-start.16 = (bf16[3,928,128]{2,1,0:T(8,128)(2,1)S(1)}, bf16[3,928,128]{2,1,0:T(8,128)(2,1)S(1)}, u32[]{:S(2)}, u32[]{:S(2)}) collective-permute-start(bf16[3,928,128]{2,1,0:T(8,128)(2,1)S(1)} %get-tuple-element.50), channel_id=1, source_target_pairs={{0,3},{1,0},{2,1},{3,2},{4,7},{5,4},{6,5},{7,6},{8,11},{9,8},{10,9... | collective-permute-start | bytes 2138120 | tf_op jit(solution)/shard_map/ppermute | solution.py:49
  50.5 18.4 %collective-permute-start.12 = (bf16[3,928,128]{2,1,0:T(8,128)(2,1)S(1)}, bf16[3,928,128]{2,1,0:T(8,128)(2,1)S(1)}, u32[]{:S(2)}, u32[]{:S(2)}) collective-permute-start(bf16[3,928,128]{2,1,0:T(8,128)(2,1)S(1)} %get-tuple-element.46), channel_id=1, source_target_pairs={{0,4},{1,5},{2,6},{3,7},{4,0},{5,1},{6,2},{7,3},{8,12},{9,13},{10,... | collective-permute-start | bytes 2138120 | tf_op jit(solution)/shard_map/ppermute | solution.py:49
  53.2 2.1 copy-start.2
  59.2 40.3 %collective-permute-start.10 = (bf16[2,3,928,128]{3,2,1,0:T(8,128)(2,1)S(1)}, bf16[2,3,928,128]{3,2,1,0:T(8,128)(2,1)S(1)}, u32[]{:S(2)}, u32[]{:S(2)}) collective-permute-start(bf16[2,3,928,128]{3,2,1,0:T(8,128)(2,1)S(1)} %send.1), channel_id=1, source_target_pairs={{0,4},{1,5},{2,6},{3,7},{4,0},{5,1},{6,2},{7,3},{8,12},{9,13},{10,... | collective-permute-start | bytes 4276232 | tf_op jit(solution)/shard_map/ppermute | solution.py:49
  68.9 32.4 %collective-permute-start.17 = (bf16[2,3,928,128]{3,2,1,0:T(8,128)(2,1)S(1)}, bf16[2,3,928,128]{3,2,1,0:T(8,128)(2,1)S(1)}, u32[]{:S(2)}, u32[]{:S(2)}) collective-permute-start(bf16[2,3,928,128]{3,2,1,0:T(8,128)(2,1)S(1)} %get-tuple-element.52), channel_id=1, source_target_pairs={{0,1},{1,2},{2,3},{3,0},{4,5},{5,6},{6,7},{7,4},{8,9},{9,10},{10,1... | collective-permute-start | bytes 4276232 | tf_op jit(solution)/shard_map/ppermute | solution.py:49
  68.9 34.0 %collective-permute-start.18 = (bf16[2,3,928,128]{3,2,1,0:T(8,128)(2,1)S(1)}, bf16[2,3,928,128]{3,2,1,0:T(8,128)(2,1)S(1)}, u32[]{:S(2)}, u32[]{:S(2)}) collective-permute-start(bf16[2,3,928,128]{3,2,1,0:T(8,128)(2,1)S(1)} %get-tuple-element.54), channel_id=1, source_target_pairs={{0,3},{1,0},{2,1},{3,2},{4,7},{5,4},{6,5},{7,6},{8,11},{9,8},{10,9... | collective-permute-start | bytes 4276232 | tf_op jit(solution)/shard_map/ppermute | solution.py:49
  76.9 37.9 %collective-permute-start.9 = (bf16[3,928,128]{2,1,0:T(8,128)(2,1)S(1)}, bf16[3,928,128]{2,1,0:T(8,128)(2,1)S(1)}, u32[]{:S(2)}, u32[]{:S(2)}) collective-permute-start(bf16[3,928,128]{2,1,0:T(8,128)(2,1)S(1)} %get-tuple-element.43), channel_id=1, source_target_pairs={{0,4},{1,5},{2,6},{3,7},{4,0},{5,1},{6,2},{7,3},{8,12},{9,13},{10,... | collective-permute-start | bytes 2138120 | tf_op jit(solution)/shard_map/ppermute | solution.py:49
  84.3 30.4 %collective-permute-start.13 = (bf16[3,928,128]{2,1,0:T(8,128)(2,1)S(1)}, bf16[3,928,128]{2,1,0:T(8,128)(2,1)S(1)}, u32[]{:S(2)}, u32[]{:S(2)}) collective-permute-start(bf16[3,928,128]{2,1,0:T(8,128)(2,1)S(1)} %x_sum1.1), channel_id=1, source_target_pairs={{0,2},{1,3},{2,0},{3,1},{4,6},{5,7},{6,4},{7,5},{8,10},{9,11},{10,... | collective-permute-start | bytes 2138120 | tf_op jit(solution)/shard_map/ppermute | solution.py:49
  100.2 32.1 %collective-permute-start.11 = (bf16[3,928,128]{2,1,0:T(8,128)(2,1)S(1)}, bf16[3,928,128]{2,1,0:T(8,128)(2,1)S(1)}, u32[]{:S(2)}, u32[]{:S(2)}) collective-permute-start(bf16[3,928,128]{2,1,0:T(8,128)(2,1)S(1)} %get-tuple-element.44), channel_id=1, source_target_pairs={{0,1},{1,2},{2,3},{3,0},{4,5},{5,6},{6,7},{7,4},{8,9},{9,10},{10,1... | collective-permute-start | bytes 2138120 | tf_op jit(solution)/shard_map/ppermute | solution.py:49
  101.3 31.0 %collective-permute-start.14 = (bf16[3,928,128]{2,1,0:T(8,128)(2,1)S(1)}, bf16[3,928,128]{2,1,0:T(8,128)(2,1)S(1)}, u32[]{:S(2)}, u32[]{:S(2)}) collective-permute-start(bf16[3,928,128]{2,1,0:T(8,128)(2,1)S(1)} %get-tuple-element.47), channel_id=1, source_target_pairs={{0,3},{1,0},{2,1},{3,2},{4,7},{5,4},{6,5},{7,6},{8,11},{9,8},{10,9... | collective-permute-start | bytes 2138120 | tf_op jit(solution)/shard_map/ppermute | solution.py:49
  103.4 28.9 %collective-permute-start.19 = (bf16[3,928,128]{2,1,0:T(8,128)(2,1)S(1)}, bf16[3,928,128]{2,1,0:T(8,128)(2,1)S(1)}, u32[]{:S(2)}, u32[]{:S(2)}) collective-permute-start(bf16[3,928,128]{2,1,0:T(8,128)(2,1)S(1)} %z_far.1), channel_id=1, source_target_pairs={{0,4},{1,5},{2,6},{3,7},{4,0},{5,1},{6,2},{7,3},{8,12},{9,13},{10,... | collective-permute-start | bytes 2138120 | tf_op jit(solution)/shard_map/ppermute | solution.py:49
  134.1 32.3 %collective-permute-start.20 = (bf16[2,3,928,128]{3,2,1,0:T(8,128)(2,1)S(1)}, bf16[2,3,928,128]{3,2,1,0:T(8,128)(2,1)S(1)}, u32[]{:S(2)}, u32[]{:S(2)}) collective-permute-start(bf16[2,3,928,128]{3,2,1,0:T(8,128)(2,1)S(1)} %get-tuple-element.55), channel_id=1, source_target_pairs={{0,4},{1,5},{2,6},{3,7},{4,0},{5,1},{6,2},{7,3},{8,12},{9,13},{10,... | collective-permute-start | bytes 4276232 | tf_op jit(solution)/shard_map/ppermute | solution.py:49
  136.9 16.3 %collective-permute-start.21 = (bf16[3,928,128]{2,1,0:T(8,128)(2,1)S(1)}, bf16[3,928,128]{2,1,0:T(8,128)(2,1)S(1)}, u32[]{:S(2)}, u32[]{:S(2)}) collective-permute-start(bf16[3,928,128]{2,1,0:T(8,128)(2,1)S(1)} %get-tuple-element.56.refs_0_), channel_id=1, source_target_pairs={{0,1},{1,2},{2,3},{3,0},{4,5},{5,6},{6,7},{7,4},{8,9},{9,10},{10,1... | collective-permute-start | bytes 2138120 | tf_op jit(solution)/shard_map/ppermute | solution.py:49
  136.9 29.7 %collective-permute-start.22 = (bf16[3,928,128]{2,1,0:T(8,128)(2,1)S(1)}, bf16[3,928,128]{2,1,0:T(8,128)(2,1)S(1)}, u32[]{:S(2)}, u32[]{:S(2)}) collective-permute-start(bf16[3,928,128]{2,1,0:T(8,128)(2,1)S(1)} %get-tuple-element.56.refs_0_), channel_id=1, source_target_pairs={{0,3},{1,0},{2,1},{3,2},{4,7},{5,4},{6,5},{7,6},{8,11},{9,8},{10,9... | collective-permute-start | bytes 2138120 | tf_op jit(solution)/shard_map/ppermute | solution.py:49
  139.6 29.7 %collective-permute-start.23 = (bf16[3,928,128]{2,1,0:T(8,128)(2,1)S(1)}, bf16[3,928,128]{2,1,0:T(8,128)(2,1)S(1)}, u32[]{:S(2)}, u32[]{:S(2)}) collective-permute-start(bf16[3,928,128]{2,1,0:T(8,128)(2,1)S(1)} %get-tuple-element.56.refs_0_), channel_id=1, source_target_pairs={{0,2},{1,3},{2,0},{3,1},{4,6},{5,7},{6,4},{7,5},{8,10},{9,11},{10,... | collective-permute-start | bytes 2138120 | tf_op jit(solution)/shard_map/ppermute | solution.py:49
  169.3 20.2 %collective-permute-start.24 = (bf16[2,2,928,128]{3,2,1,0:T(8,128)(2,1)S(1)}, bf16[2,2,928,128]{3,2,1,0:T(8,128)(2,1)S(1)}, u32[]{:S(2)}, u32[]{:S(2)}) collective-permute-start(bf16[2,2,928,128]{3,2,1,0:T(8,128)(2,1)S(1)} %pad_maximum_fusion.3.refs_8_), channel_id=1, source_target_pairs={{0,1},{1,2},{2,3},{3,0},{4,5},{5,6},{6,7},{7,4},{8,9},{9,10},{10,1... | collective-permute-start | bytes 2850824 | tf_op jit(solution)/shard_map/ppermute | solution.py:49
  169.8 19.6 %collective-permute-start.25 = (bf16[2,2,928,128]{3,2,1,0:T(8,128)(2,1)S(1)}, bf16[2,2,928,128]{3,2,1,0:T(8,128)(2,1)S(1)}, u32[]{:S(2)}, u32[]{:S(2)}) collective-permute-start(bf16[2,2,928,128]{3,2,1,0:T(8,128)(2,1)S(1)} %pad_maximum_fusion.3.refs_8_), channel_id=1, source_target_pairs={{0,3},{1,0},{2,1},{3,2},{4,7},{5,4},{6,5},{7,6},{8,11},{9,8},{10,9... | collective-permute-start | bytes 2850824 | tf_op jit(solution)/shard_map/ppermute | solution.py:49
  172.2 30.2 %collective-permute-start.28 = (bf16[3,2,928,128]{3,2,1,0:T(8,128)(2,1)S(1)}, bf16[3,2,928,128]{3,2,1,0:T(8,128)(2,1)S(1)}, u32[]{:S(2)}, u32[]{:S(2)}) collective-permute-start(bf16[3,2,928,128]{3,2,1,0:T(8,128)(2,1)S(1)} %pad_maximum_fusion.1), channel_id=1, source_target_pairs={{0,4},{1,5},{2,6},{3,7},{4,0},{5,1},{6,2},{7,3},{8,12},{9,13},{10,... | collective-permute-start | bytes 4276232 | tf_op jit(solution)/shard_map/ppermute | solution.py:49
  172.6 36.3 %copy-start.3 = (bf16[1024,1848]{0,1:T(8,128)(2,1)S(1)}, bf16[1024,1848]{0,1:T(8,128)(2,1)}, u32[]{:S(2)}) copy-start(bf16[1024,1848]{0,1:T(8,128)(2,1)} %param.8) | copy-start | bytes 11354116
  189.4 9.3 %collective-permute-start.26 = (bf16[2,1,928,128]{3,2,1,0:T(8,128)(2,1)S(1)}, bf16[2,1,928,128]{3,2,1,0:T(8,128)(2,1)S(1)}, u32[]{:S(2)}, u32[]{:S(2)}) collective-permute-start(bf16[2,1,928,128]{3,2,1,0:T(8,128)(2,1)S(1)} %pad_maximum_fusion.6.refs_8_), channel_id=1, source_target_pairs={{0,1},{1,2},{2,3},{3,0},{4,5},{5,6},{6,7},{7,4},{8,9},{9,10},{10,1... | collective-permute-start | bytes 1425416 | tf_op jit(solution)/shard_map/ppermute | solution.py:49
  189.7 9.1 %collective-permute-start.27 = (bf16[2,1,928,128]{3,2,1,0:T(8,128)(2,1)S(1)}, bf16[2,1,928,128]{3,2,1,0:T(8,128)(2,1)S(1)}, u32[]{:S(2)}, u32[]{:S(2)}) collective-permute-start(bf16[2,1,928,128]{3,2,1,0:T(8,128)(2,1)S(1)} %pad_maximum_fusion.6.refs_8_), channel_id=1, source_target_pairs={{0,3},{1,0},{2,1},{3,2},{4,7},{5,4},{6,5},{7,6},{8,11},{9,8},{10,9... | collective-permute-start | bytes 1425416 | tf_op jit(solution)/shard_map/ppermute | solution.py:49
  192.2 16.8 %collective-permute-start.29 = (bf16[2,928,128]{2,1,0:T(8,128)(2,1)S(1)}, bf16[2,928,128]{2,1,0:T(8,128)(2,1)S(1)}, u32[]{:S(2)}, u32[]{:S(2)}) collective-permute-start(bf16[2,928,128]{2,1,0:T(8,128)(2,1)S(1)} %slice_bitcast_fusion.1), channel_id=1, source_target_pairs={{0,1},{1,2},{2,3},{3,0},{4,5},{5,6},{6,7},{7,4},{8,9},{9,10},{10,1... | collective-permute-start | bytes 1425416 | tf_op jit(solution)/shard_map/ppermute | solution.py:49
  192.3 16.7 %collective-permute-start.30 = (bf16[2,928,128]{2,1,0:T(8,128)(2,1)S(1)}, bf16[2,928,128]{2,1,0:T(8,128)(2,1)S(1)}, u32[]{:S(2)}, u32[]{:S(2)}) collective-permute-start(bf16[2,928,128]{2,1,0:T(8,128)(2,1)S(1)} %slice_bitcast_fusion), channel_id=1, source_target_pairs={{0,3},{1,0},{2,1},{3,2},{4,7},{5,4},{6,5},{7,6},{8,11},{9,8},{10,9... | collective-permute-start | bytes 1425416 | tf_op jit(solution)/shard_map/ppermute | solution.py:49
  221.8 8.8 %collective-permute-start.31 = (bf16[512,1024]{1,0:T(8,128)(2,1)S(1)}, bf16[512,1024]{1,0:T(8,128)(2,1)S(1)}, u32[]{:S(2)}, u32[]{:S(2)}) collective-permute-start(bf16[512,1024]{1,0:T(8,128)(2,1)S(1)} %get-tuple-element.63), channel_id=1, source_target_pairs={{0,8},{8,0},{16,24},{24,16},{32,40},{40,32},{48,56},{56,48},{64,72... | collective-permute-start | bytes 3145736 | tf_op jit(solution)/shard_map/ppermute | solution.py:59
  227.4 8.7 %collective-permute-start.36 = (bf16[1,928,128]{2,1,0:T(8,128)(2,1)S(1)}, bf16[1,928,128]{2,1,0:T(8,128)(2,1)S(1)}, u32[]{:S(2)}, u32[]{:S(2)}) collective-permute-start(bf16[1,928,128]{2,1,0:T(8,128)(2,1)S(1)} %slice_bitcast_fusion.9), channel_id=1, source_target_pairs={{0,1},{1,2},{2,3},{3,0},{4,5},{5,6},{6,7},{7,4},{8,9},{9,10},{10,1... | collective-permute-start | bytes 712712 | tf_op jit(solution)/shard_map/ppermute | solution.py:49
  227.9 8.7 %collective-permute-start.37 = (bf16[1,928,128]{2,1,0:T(8,128)(2,1)S(1)}, bf16[1,928,128]{2,1,0:T(8,128)(2,1)S(1)}, u32[]{:S(2)}, u32[]{:S(2)}) collective-permute-start(bf16[1,928,128]{2,1,0:T(8,128)(2,1)S(1)} %slice_bitcast_fusion.8), channel_id=1, source_target_pairs={{0,3},{1,0},{2,1},{3,2},{4,7},{5,4},{6,5},{7,6},{8,11},{9,8},{10,9... | collective-permute-start | bytes 712712 | tf_op jit(solution)/shard_map/ppermute | solution.py:49
  230.3 21.6 %collective-permute-start.38 = (bf16[3,1,928,128]{3,2,1,0:T(8,128)(2,1)S(1)}, bf16[3,1,928,128]{3,2,1,0:T(8,128)(2,1)S(1)}, u32[]{:S(2)}, u32[]{:S(2)}) collective-permute-start(bf16[3,1,928,128]{3,2,1,0:T(8,128)(2,1)S(1)} %pad_maximum_fusion.4), channel_id=1, source_target_pairs={{0,4},{1,5},{2,6},{3,7},{4,0},{5,1},{6,2},{7,3},{8,12},{9,13},{10,... | collective-permute-start | bytes 2138120 | tf_op jit(solution)/shard_map/ppermute | solution.py:49
  231.1 20.2 %collective-permute-start.34 = (bf16[128,1024]{1,0:T(8,128)(2,1)S(1)}, bf16[128,1024]{1,0:T(8,128)(2,1)S(1)}, u32[]{:S(2)}, u32[]{:S(2)}) collective-permute-start(bf16[128,1024]{1,0:T(8,128)(2,1)S(1)} %get-tuple-element.73), channel_id=1, source_target_pairs={{0,64},{8,72},{16,80},{24,88},{32,96},{40,104},{48,112},{56,120},{... | collective-permute-start | bytes 786440 | tf_op jit(solution)/shard_map/ppermute | solution.py:59
  232.8 18.5 %collective-permute-start.33 = (bf16[128,1024]{1,0:T(8,128)(2,1)S(1)}, bf16[128,1024]{1,0:T(8,128)(2,1)S(1)}, u32[]{:S(2)}, u32[]{:S(2)}) collective-permute-start(bf16[128,1024]{1,0:T(8,128)(2,1)S(1)} %get-tuple-element.74), channel_id=1, source_target_pairs={{0,96},{8,104},{16,112},{24,120},{32,0},{40,8},{48,16},{56,24},{64... | collective-permute-start | bytes 786440 | tf_op jit(solution)/shard_map/ppermute | solution.py:59
  236.1 15.3 %collective-permute-start.32 = (bf16[128,1024]{1,0:T(8,128)(2,1)S(1)}, bf16[128,1024]{1,0:T(8,128)(2,1)S(1)}, u32[]{:S(2)}, u32[]{:S(2)}) collective-permute-start(bf16[128,1024]{1,0:T(8,128)(2,1)S(1)} %get-tuple-element.72), channel_id=1, source_target_pairs={{0,32},{8,40},{16,48},{24,56},{32,64},{40,72},{48,80},{56,88},{64,... | collective-permute-start | bytes 786440 | tf_op jit(solution)/shard_map/ppermute | solution.py:59
  251.6 9.2 %collective-permute-start.35 = (bf16[64,1024]{1,0:T(8,128)(2,1)S(1)}, bf16[64,1024]{1,0:T(8,128)(2,1)S(1)}, u32[]{:S(2)}, u32[]{:S(2)}) collective-permute-start(bf16[64,1024]{1,0:T(8,128)(2,1)S(1)} %slice.121), channel_id=1, source_target_pairs={{0,16},{8,24},{16,0},{24,8},{32,48},{40,56},{48,32},{56,40},{64,80... | collective-permute-start | bytes 393224 | tf_op jit(solution)/shard_map/ppermute | solution.py:59

commit v3 on v2

--- a/solution.py
+++ b/solution.py
@@ -18,7 +18,7 @@
 R = RH // 2
 N_BLOCK = 512
 VMEM = 32 * 1024 * 1024
-VMEM_FAR = 44 * 1024 * 1024
+VMEM_FAR = 48 * 1024 * 1024
 VMEM_SUMS = 12 * 1024 * 1024
 
 NT = (((1,), (1,)), ((), ()))
@@ -83,21 +83,13 @@
 
     for i, w in enumerate(which):
         res = dot(weights[i][...], targets[sources.index(w // 2)][...], NT).astype(BF)
-
-        def store(outs):
-            for out, members in zip(outs, layout):
-                for k, s in enumerate(members):
-                    value = res[:, s * B : (s + 1) * B]
-                    if len(members) > 1:
-                        out[k, i] = value
-                    else:
-                        out[i] = value
-
-        if len(outs) == len(layout):
-            store(outs)
-        else:
-            pl.when(pl.program_id(0) < 2)(functools.partial(store, outs[: len(layout)]))
-            pl.when(pl.program_id(0) >= 2)(functools.partial(store, outs[len(layout) :]))
+        for out, members in zip(outs, layout):
+            for k, s in enumerate(members):
+                value = res[:, s * B : (s + 1) * B]
+                if len(members) > 1:
+                    out[k, i] = value
+                else:
+                    out[i] = value
 
 
 def rows_spec(array, lead=None, step=lambda r: r):
@@ -108,19 +100,14 @@
     return pl.BlockSpec((1, array.shape[1], R, B), lambda r, *_: (lead, 0, step(r), 0))
 
 
-def first(name, half, slots, layout, at, halves, weights):
+def first(name, half, slots, layout, at, halves, weights, limit=VMEM):
     which = (0, 1, 2)
     n = len(which)
-    base = 0 if half is None else 2 * half
-    weight = pl.BlockSpec((R, D), lambda r, at: (base + r, 0))
+    weight = pl.BlockSpec((R, D), lambda r, at: (2 * half + r, 0))
     out_shape = [shape(len(m), n, RH, B) if len(m) > 1 else shape(n, RH, B) for m in layout]
     out_specs = [rows_spec(o) for o in out_shape]
-    if half is None:
-        out_specs = [rows_spec(o, step=lambda r: jnp.minimum(r, 1)) for o in out_shape]
-        out_specs += [rows_spec(o, step=lambda r: jnp.maximum(r - 2, 0)) for o in out_shape]
-        out_shape = out_shape * 2
     width = len(slots) * B
-    steps = 4 if half is None else 2
+    steps = 2
     return pl.pallas_call(
         functools.partial(first_kernel, which, slots, layout, len(out_shape)),
         out_shape=out_shape,
@@ -134,7 +121,7 @@
                 pltpu.SemaphoreType.DMA((2, len(slots))),
             ],
         ),
-        compiler_params=params(VMEM_FAR if half is None else VMEM),
+        compiler_params=params(limit),
         cost_estimate=cost(n * 2 * steps * R * width * D, n * steps * R * (D + width) * 2),
         name=name,
     )(at, *halves, *[weights[w] for w in which])
@@ -396,10 +383,12 @@
     tokens = jnp.stack([jnp.concatenate(pairs), pairs_g])
     halves = (tokens, wide_move(tokens, 0, 0, 1))
 
-    keep2, send2, a2, b2 = first("far", None, ((0, 2), (1, 2)), ((0,), (1,)), at, halves, weights)
+    far_slots = ((0, 2), (1, 2))
+    a2, b2 = first("ring", 1, far_slots, ((0,), (1,)), at, halves, weights, VMEM_FAR)
+    keep2, send2 = first("far", 0, far_slots, ((0,), (1,)), after(at, a2), halves, weights, VMEM_FAR)
     recv2 = narrow_move(send2, 1, 0)
     ra, rb = narrow_move(a2, 0, 1), narrow_move(b2, 0, 3)
-    (send,) = first("send", 0, ((1, 1), (1, 3)), ((0, 1),), after(at, a2), halves, weights)
+    (send,) = first("send", 0, ((1, 1), (1, 3)), ((0, 1),), after(at, keep2), halves, weights)
     recv = narrow_move(send, 1, 0)
     mid_slots = ((0, 1), (1, 1), (0, 3), (1, 3))
     mid1, mid3 = first("mid", 1, mid_slots, ((0, 1), (2, 3)), after(at, send), halves, weights)

time: 262 us -> 262 us (level)
  waiting for transfers between devices: 124 us -> 121 us
    ppermute x25, waiting for transfers between devices: 106 us -> 103 us  [narrow_move(): return lax.ppermute(value, 'narrow', pairs)]
    pallas_call x5 -> x6, Pallas kernels: 31 us -> 31.8 us  [first(): pl.pallas_call(functools.partial(first_kernel, which, slots, layout, len(...]
  transfers between devices with their start and end apart: 39 -> 39, of which waited for: 20 -> 20; matrix products, arithmetic and copies ran while one was open for 1% -> 1% of each run, Pallas kernels for 16% -> 19%
where the time goes in v3:
time: 262 us
  waiting for transfers between devices  121 us (46%)
  Pallas kernels  74.3 us (28%)
  starting transfers between devices  59.2 us (23%)
  local copies, waits for them, and re-layouts  3.56 us (1%)
  other arithmetic  3.02 us (1%)
    ppermute x25, waiting for transfers between devices, narrow_move(): return lax.ppermute(value, 'narrow', pairs)  103 us
    ppermute x25, starting transfers between devices, narrow_move(): return lax.ppermute(value, 'narrow', pairs)  35.9 us
    pallas_call x6, Pallas kernels, first(): pl.pallas_call(functools.partial(first_kernel, which, slots, layout, len(...  31.8 us
    pallas_call x2, Pallas kernels, grads(): pl.pallas_call(functools.partial(grads_kernel, (places_x, places_z), coun...  23.7 us
    ppermute x14, starting transfers between devices, wide_move(): return lax.ppermute(value, 'wide', pairs)  23.2 us
    ppermute x14, waiting for transfers between devices, wide_move(): return lax.ppermute(value, 'wide', pairs)  17.2 us
    pallas_call x1, Pallas kernels, back(): pl.pallas_call(functools.partial(back_kernel, (places_x, places_z), count...  12.9 us
    pallas_call x5, Pallas kernels, on_groups(): pl.pallas_call(run, out_shape=out_shape, grid=(2,), in_specs=[rows_spec(a...  5.9 us
  transfers between devices with their start and end apart: 39, of which 20 were waited for; matrix products, arithmetic and copies ran while one was open for 1% of the time, Pallas kernels for 19%

profile of v3, /device:TPU:1, one launch (start us, length us, event | category | flops | bytes accessed | tf_op | source)
XLA Modules:
  0.0 261.7 jit_solution(8977145626875933673)
XLA Ops:
  0.6 2.1 collective-permute-start
  4.0 2.6 %collective-permute-start.5 = (bf16[64,1024]{1,0:T(8,128)(2,1)}, bf16[64,1024]{1,0:T(8,128)(2,1)S(1)}, u32[]{:S(2)}, u32[]{:S(2)}) collective-permute-start(bf16[64,1024]{1,0:T(8,128)(2,1)} %param.6), channel_id=1, source_target_pairs={{0,64},{8,72},{16,80},{24,88},{32,96},{40,104},{48,112},{56,120},{... | collective-permute-start | bytes 393224 | tf_op jit(solution)/shard_map/ppermute | solution.py:59
  8.9 3.0 %collective-permute-done.5 = bf16[64,1024]{1,0:T(8,128)(2,1)S(1)} collective-permute-done((bf16[64,1024]{1,0:T(8,128)(2,1)}, bf16[64,1024]{1,0:T(8,128)(2,1)S(1)}, u32[]{:S(2)}, u32[]{:S(2)}) %collective-permute-start.5) | collective-permute-done | bytes 131104 | tf_op jit(solution)/shard_map/ppermute | solution.py:59
  13.5 2.1 collective-permute-start.2
  16.5 1.4 collective-permute-done.1
  18.0 2.4 collective-permute-done.2
  20.3 6.2 %collective-permute-done.3 = bf16[128,1024]{1,0:T(8,128)(2,1)S(1)} collective-permute-done((bf16[128,1024]{1,0:T(8,128)(2,1)S(1)}, bf16[128,1024]{1,0:T(8,128)(2,1)S(1)}, u32[]{:S(2)}, u32[]{:S(2)}) %collective-permute-start.3) | collective-permute-done | bytes 262176 | tf_op jit(solution)/shard_map/ppermute | solution.py:59
  27.0 2.9 %collective-permute-start.8 = (bf16[2,512,1024]{2,1,0:T(8,128)(2,1)S(1)}, bf16[2,512,1024]{2,1,0:T(8,128)(2,1)}, u32[]{:S(2)}, u32[]{:S(2)}) collective-permute-start(bf16[2,512,1024]{2,1,0:T(8,128)(2,1)S(1)} %pad_maximum_fusion.refs_0_.refs_11_), channel_id=1, source_target_pairs={{0,8},{8,0},{16,24},{24,16},{32,40},{40,32},{48,56},{56,48},{64,72... | collective-permute-start | bytes 6291464 | tf_op jit(solution)/shard_map/ppermute | solution.py:59
  29.9 3.8 %collective-permute-done.8.refs_1_.refs_12_ = bf16[2,512,1024]{2,1,0:T(8,128)(2,1)} collective-permute-done((bf16[2,512,1024]{2,1,0:T(8,128)(2,1)S(1)}, bf16[2,512,1024]{2,1,0:T(8,128)(2,1)}, u32[]{:S(2)}, u32[]{:S(2)}) %collective-permute-start.8) | collective-permute-done | bytes 2097184 | tf_op jit(solution)/shard_map/ppermute | solution.py:59
  33.7 6.4 %ring.1 = (bf16[3,928,128]{2,1,0:T(8,128)(2,1)}, bf16[3,928,128]{2,1,0:T(8,128)(2,1)}) custom-call(s32[2]{0:T(128)S(1)} %pad_add_fusion.at, bf16[2,512,1024]{2,1,0:T(8,128)(2,1)S(1)} %pad_maximum_fusion.refs_0_.refs_11_, bf16[2,512,1024]{2,1,0:T(8,128)(2,1)} %collective-permute-done.8.refs_1_.refs_12_, bf16[1848,1024]{1,0:T(8,128)(2,1)} %bitcast.35, ...), custom_call_target="tpu_custom_call" | custom-call | flops 1459617792 | bytes 7127040 | tf_op jit(solution)/shard_map/ring/pallas_call | solution.py:111
  40.2 1.9 collective-permute-start.15
  42.0 2.2 collective-permute-start.16
  44.2 6.8 %far.1 = (bf16[3,928,128]{2,1,0:T(8,128)(2,1)S(1)}, bf16[3,928,128]{2,1,0:T(8,128)(2,1)S(1)}) custom-call(s32[2]{0:T(128)S(1)} %pad_add_fusion.at, bf16[2,512,1024]{2,1,0:T(8,128)(2,1)S(1)} %pad_maximum_fusion.refs_0_.refs_11_, bf16[2,512,1024]{2,1,0:T(8,128)(2,1)} %collective-permute-done.8.refs_1_.refs_12_, bf16[1848,1024]{1,0:T(8,128)(2,1)} %bitcast.36, ...), custom_call_target="tpu_custom_call" | custom-call | flops 1459617792 | bytes 7127040 | tf_op jit(solution)/shard_map/far/pallas_call | solution.py:111
  51.1 2.8 %collective-permute-start.12 = (bf16[3,928,128]{2,1,0:T(8,128)(2,1)S(1)}, bf16[3,928,128]{2,1,0:T(8,128)(2,1)S(1)}, u32[]{:S(2)}, u32[]{:S(2)}) collective-permute-start(bf16[3,928,128]{2,1,0:T(8,128)(2,1)S(1)} %get-tuple-element.48), channel_id=1, source_target_pairs={{0,4},{1,5},{2,6},{3,7},{4,0},{5,1},{6,2},{7,3},{8,12},{9,13},{10,... | collective-permute-start | bytes 2138120 | tf_op jit(solution)/shard_map/ppermute | solution.py:49
  53.8 2.1 copy-done.2
  55.9 4.1 %send.1 = bf16[2,3,928,128]{3,2,1,0:T(8,128)(2,1)S(1)} custom-call(s32[2]{0:T(128)S(1)} %pad_add_fusion.at, bf16[2,512,1024]{2,1,0:T(8,128)(2,1)S(1)} %pad_maximum_fusion.refs_0_.refs_11_, bf16[2,512,1024]{2,1,0:T(8,128)(2,1)} %collective-permute-done.8.refs_1_.refs_12_, bf16[1848,1024]{1,0:T(8,128)(2,1)S(1)} %bitcast.37, bf16[1848,1024]{1,0:T(8,128)(2,1)S(1)} %bitcast.44, ...), custom_call_target="tpu_custom_call" | custom-call | flops 1459617792 | bytes 7127040 | tf_op jit(solution)/shard_map/send/pallas_call | solution.py:111
  60.1 5.5 %mid.1 = (bf16[2,3,928,128]{3,2,1,0:T(8,128)(2,1)S(1)}, bf16[2,3,928,128]{3,2,1,0:T(8,128)(2,1)S(1)}) custom-call(s32[2]{0:T(128)S(1)} %pad_add_fusion.at, bf16[2,512,1024]{2,1,0:T(8,128)(2,1)S(1)} %pad_maximum_fusion.refs_0_.refs_11_, bf16[2,512,1024]{2,1,0:T(8,128)(2,1)} %collective-permute-done.8.refs_1_.refs_12_, bf16[1848,1024]{1,0:T(8,128)(2,1)S(1)} %bitcast.38, ...), custom_call_target="tpu_custom_call" | custom-call | flops 2919235584 | bytes 8552448 | tf_op jit(solution)/shard_map/mid/pallas_call | solution.py:111
  65.7 2.5 z_mid.1
  68.1 1.4 collective-permute-done.12.refs_1_
  69.5 2.7 %collective-permute-start.18 = (bf16[2,3,928,128]{3,2,1,0:T(8,128)(2,1)S(1)}, bf16[2,3,928,128]{3,2,1,0:T(8,128)(2,1)S(1)}, u32[]{:S(2)}, u32[]{:S(2)}) collective-permute-start(bf16[2,3,928,128]{3,2,1,0:T(8,128)(2,1)S(1)} %get-tuple-element.56), channel_id=1, source_target_pairs={{0,3},{1,0},{2,1},{3,2},{4,7},{5,4},{6,5},{7,6},{8,11},{9,8},{10,9... | collective-permute-start | bytes 4276232 | tf_op jit(solution)/shard_map/ppermute | solution.py:49
  72.2 5.3 %keep.1 = (bf16[3,928,128]{2,1,0:T(8,128)(2,1)S(1)}, bf16[3,3,928,128]{3,2,1,0:T(8,128)(2,1)S(1)}) custom-call(s32[2]{0:T(128)S(1)} %pad_add_fusion.at, bf16[2,512,1024]{2,1,0:T(8,128)(2,1)S(1)} %pad_maximum_fusion.refs_0_.refs_11_, bf16[2,512,1024]{2,1,0:T(8,128)(2,1)} %collective-permute-done.8.refs_1_.refs_12_, bf16[1848,1024]{1,0:T(8,128)(2,1)S(1)} %bitcast.39, ...), custom_call_target="tpu_custom_call" | custom-call | flops 2919235584 | bytes 8552448 | tf_op jit(solution)/shard_map/keep/pallas_call | solution.py:111
  77.5 3.3 %collective-permute-start.9 = (bf16[3,928,128]{2,1,0:T(8,128)(2,1)S(1)}, bf16[3,928,128]{2,1,0:T(8,128)(2,1)S(1)}, u32[]{:S(2)}, u32[]{:S(2)}) collective-permute-start(bf16[3,928,128]{2,1,0:T(8,128)(2,1)S(1)} %get-tuple-element.46), channel_id=1, source_target_pairs={{0,4},{1,5},{2,6},{3,7},{4,0},{5,1},{6,2},{7,3},{8,12},{9,13},{10,... | collective-permute-start | bytes 2138120 | tf_op jit(solution)/shard_map/ppermute | solution.py:49
  80.8 3.7 %own.1.refs_0_.refs_5_ = bf16[2,3,928,128]{3,2,1,0:T(8,128)(2,1)S(1)} custom-call(s32[2]{0:T(128)S(1)} %pad_add_fusion.at, bf16[2,512,1024]{2,1,0:T(8,128)(2,1)S(1)} %pad_maximum_fusion.refs_0_.refs_11_, bf16[2,512,1024]{2,1,0:T(8,128)(2,1)} %collective-permute-done.8.refs_1_.refs_12_, bf16[1848,1024]{1,0:T(8,128)(2,1)S(1)} %bitcast.40, ...), custom_call_target="tpu_custom_call" | custom-call | flops 1459617792 | bytes 7127040 | tf_op jit(solution)/shard_map/own/pallas_call | solution.py:111
  85.0 15.1 %collective-permute-done.10.refs_1_ = bf16[2,3,928,128]{3,2,1,0:T(8,128)(2,1)S(1)} collective-permute-done((bf16[2,3,928,128]{3,2,1,0:T(8,128)(2,1)S(1)}, bf16[2,3,928,128]{3,2,1,0:T(8,128)(2,1)S(1)}, u32[]{:S(2)}, u32[]{:S(2)}) %collective-permute-start.10) | collective-permute-done | bytes 1425440 | tf_op jit(solution)/shard_map/ppermute | solution.py:49
  102.0 1.5 collective-permute-start.14
  104.0 2.8 %collective-permute-start.19 = (bf16[3,928,128]{2,1,0:T(8,128)(2,1)S(1)}, bf16[3,928,128]{2,1,0:T(8,128)(2,1)S(1)}, u32[]{:S(2)}, u32[]{:S(2)}) collective-permute-start(bf16[3,928,128]{2,1,0:T(8,128)(2,1)S(1)} %z_far.1), channel_id=1, source_target_pairs={{0,4},{1,5},{2,6},{3,7},{4,0},{5,1},{6,2},{7,3},{8,12},{9,13},{10,... | collective-permute-start | bytes 2138120 | tf_op jit(solution)/shard_map/ppermute | solution.py:49
  106.8 8.5 %collective-permute-done.9.refs_1_ = bf16[3,928,128]{2,1,0:T(8,128)(2,1)S(1)} collective-permute-done((bf16[3,928,128]{2,1,0:T(8,128)(2,1)S(1)}, bf16[3,928,128]{2,1,0:T(8,128)(2,1)S(1)}, u32[]{:S(2)}, u32[]{:S(2)}) %collective-permute-start.9) | collective-permute-done | bytes 712736 | tf_op jit(solution)/shard_map/ppermute | solution.py:49
  115.4 17.6 %collective-permute-done.11.refs_2_ = bf16[3,928,128]{2,1,0:T(8,128)(2,1)S(1)} collective-permute-done((bf16[3,928,128]{2,1,0:T(8,128)(2,1)S(1)}, bf16[3,928,128]{2,1,0:T(8,128)(2,1)S(1)}, u32[]{:S(2)}, u32[]{:S(2)}) %collective-permute-start.11) | collective-permute-done | bytes 712736 | tf_op jit(solution)/shard_map/ppermute | solution.py:49
  133.0 1.8 swiglu.1
  134.9 2.7 %collective-permute-start.20 = (bf16[2,3,928,128]{3,2,1,0:T(8,128)(2,1)S(1)}, bf16[2,3,928,128]{3,2,1,0:T(8,128)(2,1)S(1)}, u32[]{:S(2)}, u32[]{:S(2)}) collective-permute-start(bf16[2,3,928,128]{3,2,1,0:T(8,128)(2,1)S(1)} %get-tuple-element.57), channel_id=1, source_target_pairs={{0,4},{1,5},{2,6},{3,7},{4,0},{5,1},{6,2},{7,3},{8,12},{9,13},{10,... | collective-permute-start | bytes 4276232 | tf_op jit(solution)/shard_map/ppermute | solution.py:49
  137.6 2.7 %collective-permute-start.22 = (bf16[3,928,128]{2,1,0:T(8,128)(2,1)S(1)}, bf16[3,928,128]{2,1,0:T(8,128)(2,1)S(1)}, u32[]{:S(2)}, u32[]{:S(2)}) collective-permute-start(bf16[3,928,128]{2,1,0:T(8,128)(2,1)S(1)} %get-tuple-element.58.refs_0_), channel_id=1, source_target_pairs={{0,3},{1,0},{2,1},{3,2},{4,7},{5,4},{6,5},{7,6},{8,11},{9,8},{10,9... | collective-permute-start | bytes 2138120 | tf_op jit(solution)/shard_map/ppermute | solution.py:49
  140.8 13.0 %collective-permute-done.21.refs_3_ = bf16[3,928,128]{2,1,0:T(8,128)(2,1)S(1)} collective-permute-done((bf16[3,928,128]{2,1,0:T(8,128)(2,1)S(1)}, bf16[3,928,128]{2,1,0:T(8,128)(2,1)S(1)}, u32[]{:S(2)}, u32[]{:S(2)}) %collective-permute-start.21) | collective-permute-done | bytes 712736 | tf_op jit(solution)/shard_map/ppermute | solution.py:49
  153.8 13.3 %collective-permute-done.20.refs_4_ = bf16[2,3,928,128]{3,2,1,0:T(8,128)(2,1)S(1)} collective-permute-done((bf16[2,3,928,128]{3,2,1,0:T(8,128)(2,1)S(1)}, bf16[2,3,928,128]{3,2,1,0:T(8,128)(2,1)S(1)}, u32[]{:S(2)}, u32[]{:S(2)}) %collective-permute-start.20) | collective-permute-done | bytes 1425440 | tf_op jit(solution)/shard_map/ppermute | solution.py:49
  167.2 1.9 collective-permute-done.23.refs_2_
  169.8 2.1 collective-permute-start.25
  173.0 16.2 %collective-permute-done.24.refs_10_ = bf16[2,2,928,128]{3,2,1,0:T(8,128)(2,1)S(1)} collective-permute-done((bf16[2,2,928,128]{3,2,1,0:T(8,128)(2,1)S(1)}, bf16[2,2,928,128]{3,2,1,0:T(8,128)(2,1)S(1)}, u32[]{:S(2)}, u32[]{:S(2)}) %collective-permute-start.24) | collective-permute-done | bytes 950304 | tf_op jit(solution)/shard_map/ppermute | solution.py:49
  189.5 2.3 collective-permute-start.27
  192.0 2.9 %collective-permute-start.30 = (bf16[2,928,128]{2,1,0:T(8,128)(2,1)S(1)}, bf16[2,928,128]{2,1,0:T(8,128)(2,1)S(1)}, u32[]{:S(2)}, u32[]{:S(2)}) collective-permute-start(bf16[2,928,128]{2,1,0:T(8,128)(2,1)S(1)} %slice_bitcast_fusion), channel_id=1, source_target_pairs={{0,3},{1,0},{2,1},{3,2},{4,7},{5,4},{6,5},{7,6},{8,11},{9,8},{10,9... | collective-permute-start | bytes 1425416 | tf_op jit(solution)/shard_map/ppermute | solution.py:49
  194.9 3.6 %collective-permute-done.26.refs_10_ = bf16[2,1,928,128]{3,2,1,0:T(8,128)(2,1)S(1)} collective-permute-done((bf16[2,1,928,128]{3,2,1,0:T(8,128)(2,1)S(1)}, bf16[2,1,928,128]{3,2,1,0:T(8,128)(2,1)S(1)}, u32[]{:S(2)}, u32[]{:S(2)}) %collective-permute-start.26) | collective-permute-done | bytes 475168 | tf_op jit(solution)/shard_map/ppermute | solution.py:49
  198.5 3.5 %collective-permute-done.28.refs_5_ = bf16[3,2,928,128]{3,2,1,0:T(8,128)(2,1)S(1)} collective-permute-done((bf16[3,2,928,128]{3,2,1,0:T(8,128)(2,1)S(1)}, bf16[3,2,928,128]{3,2,1,0:T(8,128)(2,1)S(1)}, u32[]{:S(2)}, u32[]{:S(2)}) %collective-permute-start.28) | collective-permute-done | bytes 1425440 | tf_op jit(solution)/shard_map/ppermute | solution.py:49
  202.0 6.6 %collective-permute-done.29.refs_6_ = bf16[2,928,128]{2,1,0:T(8,128)(2,1)S(1)} collective-permute-done((bf16[2,928,128]{2,1,0:T(8,128)(2,1)S(1)}, bf16[2,928,128]{2,1,0:T(8,128)(2,1)S(1)}, u32[]{:S(2)}, u32[]{:S(2)}) %collective-permute-start.29) | collective-permute-done | bytes 475168 | tf_op jit(solution)/shard_map/ppermute | solution.py:49
  208.6 12.9 %back.1 = (bf16[512,1024]{1,0:T(8,128)(2,1)S(1)}, bf16[512,1024]{1,0:T(8,128)(2,1)S(1)}) custom-call(s32[2]{0:T(128)S(1)} %pad_add_fusion.at, bf16[3,928,128]{2,1,0:T(8,128)(2,1)S(1)} %get-tuple-element.58.refs_0_, bf16[3,928,128]{2,1,0:T(8,128)(2,1)S(1)} %collective-permute-done.22.refs_1_, bf16[3,928,128]{2,1,0:T(8,128)(2,1)S(1)} %collective-permute-done.23.refs_2_, ...), custom_call_target="tpu_custom_call" | custom-call | flops 7751073792 | bytes 17235968 | tf_op jit(solution)/shard_map/back/pallas_call | solution.py:286
  221.5 5.7 %collective-permute-start.31 = (bf16[512,1024]{1,0:T(8,128)(2,1)S(1)}, bf16[512,1024]{1,0:T(8,128)(2,1)S(1)}, u32[]{:S(2)}, u32[]{:S(2)}) collective-permute-start(bf16[512,1024]{1,0:T(8,128)(2,1)S(1)} %get-tuple-element.65), channel_id=1, source_target_pairs={{0,8},{8,0},{16,24},{24,16},{32,40},{40,32},{48,56},{56,48},{64,72... | collective-permute-start | bytes 3145736 | tf_op jit(solution)/shard_map/ppermute | solution.py:59
  227.8 2.4 collective-permute-start.37
  231.4 1.9 collective-permute-start.34
  234.4 1.6 collective-permute-done.36.refs_6_
  236.5 14.8 %grads.1 = (bf16[1848,1024]{1,0:T(8,128)(2,1)}, bf16[1848,1024]{1,0:T(8,128)(2,1)}) custom-call(s32[2]{0:T(128)S(1)} %pad_add_fusion.at, bf16[3,928,128]{2,1,0:T(8,128)(2,1)S(1)} %get-tuple-element.58.refs_0_, bf16[3,928,128]{2,1,0:T(8,128)(2,1)S(1)} %collective-permute-done.22.refs_1_, bf16[3,928,128]{2,1,0:T(8,128)(2,1)S(1)} %collective-permute-done.23.refs_2_, ...), custom_call_target="tpu_custom_call" | custom-call | flops 7751073792 | bytes 17235968 | tf_op jit(solution)/shard_map/grads/pallas_call | solution.py:338
  252.1 8.9 %down.1 = bf16[1848,1024]{1,0:T(8,128)(2,1)} custom-call(s32[2]{0:T(128)S(1)} %pad_add_fusion.at, bf16[3,928,128]{2,1,0:T(8,128)(2,1)S(1)} %get-tuple-element.58.refs_0_, bf16[3,928,128]{2,1,0:T(8,128)(2,1)S(1)} %collective-permute-done.22.refs_1_, bf16[3,928,128]{2,1,0:T(8,128)(2,1)S(1)} %collective-permute-done.23.refs_2_, ...), custom_call_target="tpu_custom_call" | custom-call | flops 3875536896 | bytes 9666560 | tf_op jit(solution)/shard_map/down/pallas_call | solution.py:338
  (87 shorter events, 17.4 us)
Async XLA Ops:
  0.6 8.0 %collective-permute-start = (bf16[64,1024]{1,0:T(8,128)(2,1)}, bf16[64,1024]{1,0:T(8,128)(2,1)S(1)}, u32[]{:S(2)}, u32[]{:S(2)}) collective-permute-start(bf16[64,1024]{1,0:T(8,128)(2,1)} %param.5), channel_id=1, source_target_pairs={{0,16},{8,24},{16,0},{24,8},{32,48},{40,56},{48,32},{56,40},{64,80... | collective-permute-start | bytes 393224 | tf_op jit(solution)/shard_map/ppermute | solution.py:59
  2.8 6.2 %collective-permute-start.6 = (bf16[64,1024]{1,0:T(8,128)(2,1)}, bf16[64,1024]{1,0:T(8,128)(2,1)S(1)}, u32[]{:S(2)}, u32[]{:S(2)}) collective-permute-start(bf16[64,1024]{1,0:T(8,128)(2,1)} %param.6), channel_id=1, source_target_pairs={{0,32},{8,40},{16,48},{24,56},{32,64},{40,72},{48,80},{56,88},{64,... | collective-permute-start | bytes 393224 | tf_op jit(solution)/shard_map/ppermute | solution.py:59
  4.0 7.9 %collective-permute-start.5 = (bf16[64,1024]{1,0:T(8,128)(2,1)}, bf16[64,1024]{1,0:T(8,128)(2,1)S(1)}, u32[]{:S(2)}, u32[]{:S(2)}) collective-permute-start(bf16[64,1024]{1,0:T(8,128)(2,1)} %param.6), channel_id=1, source_target_pairs={{0,64},{8,72},{16,80},{24,88},{32,96},{40,104},{48,112},{56,120},{... | collective-permute-start | bytes 393224 | tf_op jit(solution)/shard_map/ppermute | solution.py:59
  6.7 5.6 %collective-permute-start.4 = (bf16[64,1024]{1,0:T(8,128)(2,1)}, bf16[64,1024]{1,0:T(8,128)(2,1)S(1)}, u32[]{:S(2)}, u32[]{:S(2)}) collective-permute-start(bf16[64,1024]{1,0:T(8,128)(2,1)} %param.6), channel_id=1, source_target_pairs={{0,96},{8,104},{16,112},{24,120},{32,0},{40,8},{48,16},{56,24},{64... | collective-permute-start | bytes 393224 | tf_op jit(solution)/shard_map/ppermute | solution.py:59
  8.7 9.2 %collective-permute-start.1 = (bf16[128,1024]{1,0:T(8,128)(2,1)S(1)}, bf16[128,1024]{1,0:T(8,128)(2,1)S(1)}, u32[]{:S(2)}, u32[]{:S(2)}) collective-permute-start(bf16[128,1024]{1,0:T(8,128)(2,1)S(1)} %get-tuple-element.79), channel_id=1, source_target_pairs={{0,96},{8,104},{16,112},{24,120},{32,0},{40,8},{48,16},{56,24},{64... | collective-permute-start | bytes 786440 | tf_op jit(solution)/shard_map/ppermute | solution.py:59
  13.3 13.3 %collective-permute-start.7 = (bf16[4,64,1024]{2,1,0:T(8,128)(2,1)S(1)}, bf16[4,64,1024]{2,1,0:T(8,128)(2,1)S(1)}, u32[]{:S(2)}, u32[]{:S(2)}) collective-permute-start(bf16[4,64,1024]{2,1,0:T(8,128)(2,1)S(1)} %get-tuple-element.78), channel_id=1, source_target_pairs={{0,16},{8,24},{16,0},{24,8},{32,48},{40,56},{48,32},{56,40},{64,80... | collective-permute-start | bytes 1572872 | tf_op jit(solution)/shard_map/ppermute | solution.py:59
  13.5 6.9 %collective-permute-start.2 = (bf16[128,1024]{1,0:T(8,128)(2,1)S(1)}, bf16[128,1024]{1,0:T(8,128)(2,1)S(1)}, u32[]{:S(2)}, u32[]{:S(2)}) collective-permute-start(bf16[128,1024]{1,0:T(8,128)(2,1)S(1)} %get-tuple-element.79), channel_id=1, source_target_pairs={{0,64},{8,72},{16,80},{24,88},{32,96},{40,104},{48,112},{56,120},{... | collective-permute-start | bytes 786440 | tf_op jit(solution)/shard_map/ppermute | solution.py:59
  15.5 11.0 %collective-permute-start.3 = (bf16[128,1024]{1,0:T(8,128)(2,1)S(1)}, bf16[128,1024]{1,0:T(8,128)(2,1)S(1)}, u32[]{:S(2)}, u32[]{:S(2)}) collective-permute-start(bf16[128,1024]{1,0:T(8,128)(2,1)S(1)} %get-tuple-element.79), channel_id=1, source_target_pairs={{0,32},{8,40},{16,48},{24,56},{32,64},{40,72},{48,80},{56,88},{64,... | collective-permute-start | bytes 786440 | tf_op jit(solution)/shard_map/ppermute | solution.py:59
  27.0 6.8 %collective-permute-start.8 = (bf16[2,512,1024]{2,1,0:T(8,128)(2,1)S(1)}, bf16[2,512,1024]{2,1,0:T(8,128)(2,1)}, u32[]{:S(2)}, u32[]{:S(2)}) collective-permute-start(bf16[2,512,1024]{2,1,0:T(8,128)(2,1)S(1)} %pad_maximum_fusion.refs_0_.refs_11_), channel_id=1, source_target_pairs={{0,8},{8,0},{16,24},{24,16},{32,40},{40,32},{48,56},{56,48},{64,72... | collective-permute-start | bytes 6291464 | tf_op jit(solution)/shard_map/ppermute | solution.py:59
  40.2 25.5 %collective-permute-start.15 = (bf16[3,928,128]{2,1,0:T(8,128)(2,1)}, bf16[3,928,128]{2,1,0:T(8,128)(2,1)S(1)}, u32[]{:S(2)}, u32[]{:S(2)}) collective-permute-start(bf16[3,928,128]{2,1,0:T(8,128)(2,1)} %get-tuple-element.38), channel_id=1, source_target_pairs={{0,1},{1,2},{2,3},{3,0},{4,5},{5,6},{6,7},{7,4},{8,9},{9,10},{10,1... | collective-permute-start | bytes 2138120 | tf_op jit(solution)/shard_map/ppermute | solution.py:49
  42.0 23.6 %collective-permute-start.16 = (bf16[3,928,128]{2,1,0:T(8,128)(2,1)}, bf16[3,928,128]{2,1,0:T(8,128)(2,1)}, u32[]{:S(2)}, u32[]{:S(2)}) collective-permute-start(bf16[3,928,128]{2,1,0:T(8,128)(2,1)} %get-tuple-element.52), channel_id=1, source_target_pairs={{0,3},{1,0},{2,1},{3,2},{4,7},{5,4},{6,5},{7,6},{8,11},{9,8},{10,9... | collective-permute-start | bytes 2138120 | tf_op jit(solution)/shard_map/ppermute | solution.py:49
  44.2 9.6 %copy-start = (bf16[1848,1024]{1,0:T(8,128)(2,1)S(1)}, bf16[1848,1024]{1,0:T(8,128)(2,1)}, u32[]{:S(2)}) copy-start(bf16[1848,1024]{1,0:T(8,128)(2,1)} %refs_4_.11) | copy-start | bytes 11354116
  44.2 9.6 %copy-start.1 = (bf16[1024,1848]{0,1:T(8,128)(2,1)S(1)}, bf16[1024,1848]{0,1:T(8,128)(2,1)}, u32[]{:S(2)}) copy-start(bf16[1024,1848]{0,1:T(8,128)(2,1)} %param.7) | copy-start | bytes 11354116
  51.1 18.4 %collective-permute-start.12 = (bf16[3,928,128]{2,1,0:T(8,128)(2,1)S(1)}, bf16[3,928,128]{2,1,0:T(8,128)(2,1)S(1)}, u32[]{:S(2)}, u32[]{:S(2)}) collective-permute-start(bf16[3,928,128]{2,1,0:T(8,128)(2,1)S(1)} %get-tuple-element.48), channel_id=1, source_target_pairs={{0,4},{1,5},{2,6},{3,7},{4,0},{5,1},{6,2},{7,3},{8,12},{9,13},{10,... | collective-permute-start | bytes 2138120 | tf_op jit(solution)/shard_map/ppermute | solution.py:49
  53.8 2.1 copy-start.2
  55.9 4.2 %copy-start.3 = (bf16[1024,1848]{0,1:T(8,128)(2,1)S(1)}, bf16[1024,1848]{0,1:T(8,128)(2,1)}, u32[]{:S(2)}) copy-start(bf16[1024,1848]{0,1:T(8,128)(2,1)} %param.8) | copy-start | bytes 11354116
  60.0 40.0 %collective-permute-start.10 = (bf16[2,3,928,128]{3,2,1,0:T(8,128)(2,1)S(1)}, bf16[2,3,928,128]{3,2,1,0:T(8,128)(2,1)S(1)}, u32[]{:S(2)}, u32[]{:S(2)}) collective-permute-start(bf16[2,3,928,128]{3,2,1,0:T(8,128)(2,1)S(1)} %send.1), channel_id=1, source_target_pairs={{0,4},{1,5},{2,6},{3,7},{4,0},{5,1},{6,2},{7,3},{8,12},{9,13},{10,... | collective-permute-start | bytes 4276232 | tf_op jit(solution)/shard_map/ppermute | solution.py:49
  69.5 32.5 %collective-permute-start.17 = (bf16[2,3,928,128]{3,2,1,0:T(8,128)(2,1)}, bf16[2,3,928,128]{3,2,1,0:T(8,128)(2,1)S(1)}, u32[]{:S(2)}, u32[]{:S(2)}) collective-permute-start(bf16[2,3,928,128]{3,2,1,0:T(8,128)(2,1)} %get-tuple-element.54), channel_id=1, source_target_pairs={{0,1},{1,2},{2,3},{3,0},{4,5},{5,6},{6,7},{7,4},{8,9},{9,10},{10,1... | collective-permute-start | bytes 4276232 | tf_op jit(solution)/shard_map/ppermute | solution.py:49
  69.5 34.0 %collective-permute-start.18 = (bf16[2,3,928,128]{3,2,1,0:T(8,128)(2,1)S(1)}, bf16[2,3,928,128]{3,2,1,0:T(8,128)(2,1)S(1)}, u32[]{:S(2)}, u32[]{:S(2)}) collective-permute-start(bf16[2,3,928,128]{3,2,1,0:T(8,128)(2,1)S(1)} %get-tuple-element.56), channel_id=1, source_target_pairs={{0,3},{1,0},{2,1},{3,2},{4,7},{5,4},{6,5},{7,6},{8,11},{9,8},{10,9... | collective-permute-start | bytes 4276232 | tf_op jit(solution)/shard_map/ppermute | solution.py:49
  77.5 37.9 %collective-permute-start.9 = (bf16[3,928,128]{2,1,0:T(8,128)(2,1)S(1)}, bf16[3,928,128]{2,1,0:T(8,128)(2,1)S(1)}, u32[]{:S(2)}, u32[]{:S(2)}) collective-permute-start(bf16[3,928,128]{2,1,0:T(8,128)(2,1)S(1)} %get-tuple-element.46), channel_id=1, source_target_pairs={{0,4},{1,5},{2,6},{3,7},{4,0},{5,1},{6,2},{7,3},{8,12},{9,13},{10,... | collective-permute-start | bytes 2138120 | tf_op jit(solution)/shard_map/ppermute | solution.py:49
  84.9 30.5 %collective-permute-start.13 = (bf16[3,928,128]{2,1,0:T(8,128)(2,1)S(1)}, bf16[3,928,128]{2,1,0:T(8,128)(2,1)S(1)}, u32[]{:S(2)}, u32[]{:S(2)}) collective-permute-start(bf16[3,928,128]{2,1,0:T(8,128)(2,1)S(1)} %x_sum1.1), channel_id=1, source_target_pairs={{0,2},{1,3},{2,0},{3,1},{4,6},{5,7},{6,4},{7,5},{8,10},{9,11},{10,... | collective-permute-start | bytes 2138120 | tf_op jit(solution)/shard_map/ppermute | solution.py:49
  100.8 32.3 %collective-permute-start.11 = (bf16[3,928,128]{2,1,0:T(8,128)(2,1)S(1)}, bf16[3,928,128]{2,1,0:T(8,128)(2,1)S(1)}, u32[]{:S(2)}, u32[]{:S(2)}) collective-permute-start(bf16[3,928,128]{2,1,0:T(8,128)(2,1)S(1)} %get-tuple-element.47), channel_id=1, source_target_pairs={{0,1},{1,2},{2,3},{3,0},{4,5},{5,6},{6,7},{7,4},{8,9},{9,10},{10,1... | collective-permute-start | bytes 2138120 | tf_op jit(solution)/shard_map/ppermute | solution.py:49
  102.0 31.0 %collective-permute-start.14 = (bf16[3,928,128]{2,1,0:T(8,128)(2,1)S(1)}, bf16[3,928,128]{2,1,0:T(8,128)(2,1)S(1)}, u32[]{:S(2)}, u32[]{:S(2)}) collective-permute-start(bf16[3,928,128]{2,1,0:T(8,128)(2,1)S(1)} %get-tuple-element.49), channel_id=1, source_target_pairs={{0,3},{1,0},{2,1},{3,2},{4,7},{5,4},{6,5},{7,6},{8,11},{9,8},{10,9... | collective-permute-start | bytes 2138120 | tf_op jit(solution)/shard_map/ppermute | solution.py:49
  104.0 29.0 %collective-permute-start.19 = (bf16[3,928,128]{2,1,0:T(8,128)(2,1)S(1)}, bf16[3,928,128]{2,1,0:T(8,128)(2,1)S(1)}, u32[]{:S(2)}, u32[]{:S(2)}) collective-permute-start(bf16[3,928,128]{2,1,0:T(8,128)(2,1)S(1)} %z_far.1), channel_id=1, source_target_pairs={{0,4},{1,5},{2,6},{3,7},{4,0},{5,1},{6,2},{7,3},{8,12},{9,13},{10,... | collective-permute-start | bytes 2138120 | tf_op jit(solution)/shard_map/ppermute | solution.py:49
  134.9 32.2 %collective-permute-start.20 = (bf16[2,3,928,128]{3,2,1,0:T(8,128)(2,1)S(1)}, bf16[2,3,928,128]{3,2,1,0:T(8,128)(2,1)S(1)}, u32[]{:S(2)}, u32[]{:S(2)}) collective-permute-start(bf16[2,3,928,128]{3,2,1,0:T(8,128)(2,1)S(1)} %get-tuple-element.57), channel_id=1, source_target_pairs={{0,4},{1,5},{2,6},{3,7},{4,0},{5,1},{6,2},{7,3},{8,12},{9,13},{10,... | collective-permute-start | bytes 4276232 | tf_op jit(solution)/shard_map/ppermute | solution.py:49
  137.6 16.2 %collective-permute-start.21 = (bf16[3,928,128]{2,1,0:T(8,128)(2,1)S(1)}, bf16[3,928,128]{2,1,0:T(8,128)(2,1)S(1)}, u32[]{:S(2)}, u32[]{:S(2)}) collective-permute-start(bf16[3,928,128]{2,1,0:T(8,128)(2,1)S(1)} %get-tuple-element.58.refs_0_), channel_id=1, source_target_pairs={{0,1},{1,2},{2,3},{3,0},{4,5},{5,6},{6,7},{7,4},{8,9},{9,10},{10,1... | collective-permute-start | bytes 2138120 | tf_op jit(solution)/shard_map/ppermute | solution.py:49
  137.6 29.7 %collective-permute-start.22 = (bf16[3,928,128]{2,1,0:T(8,128)(2,1)S(1)}, bf16[3,928,128]{2,1,0:T(8,128)(2,1)S(1)}, u32[]{:S(2)}, u32[]{:S(2)}) collective-permute-start(bf16[3,928,128]{2,1,0:T(8,128)(2,1)S(1)} %get-tuple-element.58.refs_0_), channel_id=1, source_target_pairs={{0,3},{1,0},{2,1},{3,2},{4,7},{5,4},{6,5},{7,6},{8,11},{9,8},{10,9... | collective-permute-start | bytes 2138120 | tf_op jit(solution)/shard_map/ppermute | solution.py:49
  140.2 28.9 %collective-permute-start.23 = (bf16[3,928,128]{2,1,0:T(8,128)(2,1)S(1)}, bf16[3,928,128]{2,1,0:T(8,128)(2,1)S(1)}, u32[]{:S(2)}, u32[]{:S(2)}) collective-permute-start(bf16[3,928,128]{2,1,0:T(8,128)(2,1)S(1)} %get-tuple-element.58.refs_0_), channel_id=1, source_target_pairs={{0,2},{1,3},{2,0},{3,1},{4,6},{5,7},{6,4},{7,5},{8,10},{9,11},{10,... | collective-permute-start | bytes 2138120 | tf_op jit(solution)/shard_map/ppermute | solution.py:49
  169.2 20.0 %collective-permute-start.24 = (bf16[2,2,928,128]{3,2,1,0:T(8,128)(2,1)S(1)}, bf16[2,2,928,128]{3,2,1,0:T(8,128)(2,1)S(1)}, u32[]{:S(2)}, u32[]{:S(2)}) collective-permute-start(bf16[2,2,928,128]{3,2,1,0:T(8,128)(2,1)S(1)} %pad_maximum_fusion.3.refs_8_), channel_id=1, source_target_pairs={{0,1},{1,2},{2,3},{3,0},{4,5},{5,6},{6,7},{7,4},{8,9},{9,10},{10,1... | collective-permute-start | bytes 2850824 | tf_op jit(solution)/shard_map/ppermute | solution.py:49
  169.8 19.4 %collective-permute-start.25 = (bf16[2,2,928,128]{3,2,1,0:T(8,128)(2,1)S(1)}, bf16[2,2,928,128]{3,2,1,0:T(8,128)(2,1)S(1)}, u32[]{:S(2)}, u32[]{:S(2)}) collective-permute-start(bf16[2,2,928,128]{3,2,1,0:T(8,128)(2,1)S(1)} %pad_maximum_fusion.3.refs_8_), channel_id=1, source_target_pairs={{0,3},{1,0},{2,1},{3,2},{4,7},{5,4},{6,5},{7,6},{8,11},{9,8},{10,9... | collective-permute-start | bytes 2850824 | tf_op jit(solution)/shard_map/ppermute | solution.py:49
  172.1 30.0 %collective-permute-start.28 = (bf16[3,2,928,128]{3,2,1,0:T(8,128)(2,1)S(1)}, bf16[3,2,928,128]{3,2,1,0:T(8,128)(2,1)S(1)}, u32[]{:S(2)}, u32[]{:S(2)}) collective-permute-start(bf16[3,2,928,128]{3,2,1,0:T(8,128)(2,1)S(1)} %pad_maximum_fusion.1), channel_id=1, source_target_pairs={{0,4},{1,5},{2,6},{3,7},{4,0},{5,1},{6,2},{7,3},{8,12},{9,13},{10,... | collective-permute-start | bytes 4276232 | tf_op jit(solution)/shard_map/ppermute | solution.py:49
  172.9 35.8 %copy-start.4 = (bf16[1024,1848]{0,1:T(8,128)(2,1)S(1)}, bf16[1024,1848]{0,1:T(8,128)(2,1)}, u32[]{:S(2)}) copy-start(bf16[1024,1848]{0,1:T(8,128)(2,1)} %param.8) | copy-start | bytes 11354116
  189.1 9.4 %collective-permute-start.26 = (bf16[2,1,928,128]{3,2,1,0:T(8,128)(2,1)S(1)}, bf16[2,1,928,128]{3,2,1,0:T(8,128)(2,1)S(1)}, u32[]{:S(2)}, u32[]{:S(2)}) collective-permute-start(bf16[2,1,928,128]{3,2,1,0:T(8,128)(2,1)S(1)} %pad_maximum_fusion.6.refs_8_), channel_id=1, source_target_pairs={{0,1},{1,2},{2,3},{3,0},{4,5},{5,6},{6,7},{7,4},{8,9},{9,10},{10,1... | collective-permute-start | bytes 1425416 | tf_op jit(solution)/shard_map/ppermute | solution.py:49
  189.5 9.1 %collective-permute-start.27 = (bf16[2,1,928,128]{3,2,1,0:T(8,128)(2,1)S(1)}, bf16[2,1,928,128]{3,2,1,0:T(8,128)(2,1)S(1)}, u32[]{:S(2)}, u32[]{:S(2)}) collective-permute-start(bf16[2,1,928,128]{3,2,1,0:T(8,128)(2,1)S(1)} %pad_maximum_fusion.6.refs_8_), channel_id=1, source_target_pairs={{0,3},{1,0},{2,1},{3,2},{4,7},{5,4},{6,5},{7,6},{8,11},{9,8},{10,9... | collective-permute-start | bytes 1425416 | tf_op jit(solution)/shard_map/ppermute | solution.py:49
  191.8 16.8 %collective-permute-start.29 = (bf16[2,928,128]{2,1,0:T(8,128)(2,1)S(1)}, bf16[2,928,128]{2,1,0:T(8,128)(2,1)S(1)}, u32[]{:S(2)}, u32[]{:S(2)}) collective-permute-start(bf16[2,928,128]{2,1,0:T(8,128)(2,1)S(1)} %slice_bitcast_fusion.1), channel_id=1, source_target_pairs={{0,1},{1,2},{2,3},{3,0},{4,5},{5,6},{6,7},{7,4},{8,9},{9,10},{10,1... | collective-permute-start | bytes 1425416 | tf_op jit(solution)/shard_map/ppermute | solution.py:49
  192.0 16.7 %collective-permute-start.30 = (bf16[2,928,128]{2,1,0:T(8,128)(2,1)S(1)}, bf16[2,928,128]{2,1,0:T(8,128)(2,1)S(1)}, u32[]{:S(2)}, u32[]{:S(2)}) collective-permute-start(bf16[2,928,128]{2,1,0:T(8,128)(2,1)S(1)} %slice_bitcast_fusion), channel_id=1, source_target_pairs={{0,3},{1,0},{2,1},{3,2},{4,7},{5,4},{6,5},{7,6},{8,11},{9,8},{10,9... | collective-permute-start | bytes 1425416 | tf_op jit(solution)/shard_map/ppermute | solution.py:49
  221.5 9.4 %collective-permute-start.31 = (bf16[512,1024]{1,0:T(8,128)(2,1)S(1)}, bf16[512,1024]{1,0:T(8,128)(2,1)S(1)}, u32[]{:S(2)}, u32[]{:S(2)}) collective-permute-start(bf16[512,1024]{1,0:T(8,128)(2,1)S(1)} %get-tuple-element.65), channel_id=1, source_target_pairs={{0,8},{8,0},{16,24},{24,16},{32,40},{40,32},{48,56},{56,48},{64,72... | collective-permute-start | bytes 3145736 | tf_op jit(solution)/shard_map/ppermute | solution.py:59
  227.3 8.7 %collective-permute-start.36 = (bf16[1,928,128]{2,1,0:T(8,128)(2,1)S(1)}, bf16[1,928,128]{2,1,0:T(8,128)(2,1)S(1)}, u32[]{:S(2)}, u32[]{:S(2)}) collective-permute-start(bf16[1,928,128]{2,1,0:T(8,128)(2,1)S(1)} %slice_bitcast_fusion.9), channel_id=1, source_target_pairs={{0,1},{1,2},{2,3},{3,0},{4,5},{5,6},{6,7},{7,4},{8,9},{9,10},{10,1... | collective-permute-start | bytes 712712 | tf_op jit(solution)/shard_map/ppermute | solution.py:49
  227.8 8.7 %collective-permute-start.37 = (bf16[1,928,128]{2,1,0:T(8,128)(2,1)S(1)}, bf16[1,928,128]{2,1,0:T(8,128)(2,1)S(1)}, u32[]{:S(2)}, u32[]{:S(2)}) collective-permute-start(bf16[1,928,128]{2,1,0:T(8,128)(2,1)S(1)} %slice_bitcast_fusion.8), channel_id=1, source_target_pairs={{0,3},{1,0},{2,1},{3,2},{4,7},{5,4},{6,5},{7,6},{8,11},{9,8},{10,9... | collective-permute-start | bytes 712712 | tf_op jit(solution)/shard_map/ppermute | solution.py:49
  230.2 21.9 %collective-permute-start.38 = (bf16[3,1,928,128]{3,2,1,0:T(8,128)(2,1)S(1)}, bf16[3,1,928,128]{3,2,1,0:T(8,128)(2,1)S(1)}, u32[]{:S(2)}, u32[]{:S(2)}) collective-permute-start(bf16[3,1,928,128]{3,2,1,0:T(8,128)(2,1)S(1)} %pad_maximum_fusion.4), channel_id=1, source_target_pairs={{0,4},{1,5},{2,6},{3,7},{4,0},{5,1},{6,2},{7,3},{8,12},{9,13},{10,... | collective-permute-start | bytes 2138120 | tf_op jit(solution)/shard_map/ppermute | solution.py:49
  231.4 19.9 %collective-permute-start.34 = (bf16[128,1024]{1,0:T(8,128)(2,1)S(1)}, bf16[128,1024]{1,0:T(8,128)(2,1)S(1)}, u32[]{:S(2)}, u32[]{:S(2)}) collective-permute-start(bf16[128,1024]{1,0:T(8,128)(2,1)S(1)} %get-tuple-element.75), channel_id=1, source_target_pairs={{0,64},{8,72},{16,80},{24,88},{32,96},{40,104},{48,112},{56,120},{... | collective-permute-start | bytes 786440 | tf_op jit(solution)/shard_map/ppermute | solution.py:59
  233.3 18.0 %collective-permute-start.33 = (bf16[128,1024]{1,0:T(8,128)(2,1)S(1)}, bf16[128,1024]{1,0:T(8,128)(2,1)S(1)}, u32[]{:S(2)}, u32[]{:S(2)}) collective-permute-start(bf16[128,1024]{1,0:T(8,128)(2,1)S(1)} %get-tuple-element.76), channel_id=1, source_target_pairs={{0,96},{8,104},{16,112},{24,120},{32,0},{40,8},{48,16},{56,24},{64... | collective-permute-start | bytes 786440 | tf_op jit(solution)/shard_map/ppermute | solution.py:59
  236.0 15.3 %collective-permute-start.32 = (bf16[128,1024]{1,0:T(8,128)(2,1)S(1)}, bf16[128,1024]{1,0:T(8,128)(2,1)S(1)}, u32[]{:S(2)}, u32[]{:S(2)}) collective-permute-start(bf16[128,1024]{1,0:T(8,128)(2,1)S(1)} %get-tuple-element.74), channel_id=1, source_target_pairs={{0,32},{8,40},{16,48},{24,56},{32,64},{40,72},{48,80},{56,88},{64,... | collective-permute-start | bytes 786440 | tf_op jit(solution)/shard_map/ppermute | solution.py:59
  251.5 9.6 %collective-permute-start.35 = (bf16[64,1024]{1,0:T(8,128)(2,1)S(1)}, bf16[64,1024]{1,0:T(8,128)(2,1)S(1)}, u32[]{:S(2)}, u32[]{:S(2)}) collective-permute-start(bf16[64,1024]{1,0:T(8,128)(2,1)S(1)} %slice.121), channel_id=1, source_target_pairs={{0,16},{8,24},{16,0},{24,8},{32,48},{40,56},{48,32},{56,40},{64,80... | collective-permute-start | bytes 393224 | tf_op jit(solution)/shard_map/ppermute | solution.py:59

commit v4 on v2

--- a/solution.py
+++ b/solution.py
@@ -16,6 +16,7 @@
 FF = 1848
 RH = 928
 R = RH // 2
+N_BACK = 256
 N_BLOCK = 512
 VMEM = 32 * 1024 * 1024
 VMEM_FAR = 44 * 1024 * 1024
@@ -281,9 +282,9 @@
         for act in acts:
             act[last, :] = jnp.where(rows, act[last, :], jnp.zeros((16, T), BF))
 
-    rows = lax.broadcasted_iota(jnp.int32, (2 * RH, N_BLOCK), 0) < FF
-    vg = jnp.where(rows, wg[...], jnp.zeros((2 * RH, N_BLOCK), BF))
-    vu = jnp.where(rows, wu[...], jnp.zeros((2 * RH, N_BLOCK), BF))
+    rows = lax.broadcasted_iota(jnp.int32, (2 * RH, N_BACK), 0) < FF
+    vg = jnp.where(rows, wg[...], jnp.zeros((2 * RH, N_BACK), BF))
+    vu = jnp.where(rows, wu[...], jnp.zeros((2 * RH, N_BACK), BF))
     for k, out in enumerate((out_o, out_t)):
         part = slice(k * HALF, (k + 1) * HALF)
         total = dot(acts[0][:, part], vg, TN) + dot(acts[1][:, part], vu, TN)
@@ -293,15 +294,15 @@
 def back(at, blocks_x, blocks_z, weights):
     (arrays_x, places_x), (arrays_z, places_z) = distinct(blocks_x), distinct(blocks_z)
     arrays = arrays_x + arrays_z
-    weight = pl.BlockSpec((2 * RH, N_BLOCK), lambda n, at: (0, n))
-    out = pl.BlockSpec((HALF, N_BLOCK), lambda n, at: (0, n))
+    weight = pl.BlockSpec((2 * RH, N_BACK), lambda n, at: (0, n))
+    out = pl.BlockSpec((HALF, N_BACK), lambda n, at: (0, n))
     counts = (len(arrays_x), len(arrays_z))
     return pl.pallas_call(
         functools.partial(back_kernel, (places_x, places_z), counts),
         out_shape=[shape(HALF, D)] * 2,
         grid_spec=pltpu.PrefetchScalarGridSpec(
             num_scalar_prefetch=1,
-            grid=(D // N_BLOCK,),
+            grid=(D // N_BACK,),
             in_specs=[pl.BlockSpec(memory_space=pl.ANY)] * len(arrays) + [weight] * 2,
             out_specs=[out] * 2,
             scratch_shapes=[pltpu.VMEM((2 * RH, T), BF)] * 2 + [pltpu.SemaphoreType.DMA((2, 2, 8))],
@@ -343,22 +344,23 @@
 
 
 def grads(name, n, at, blocks_x, blocks_z, k, halves):
+    width = N_BACK if n > 1 else N_BLOCK
     (arrays_x, places_x), (arrays_z, places_z) = distinct(blocks_x), distinct(blocks_z)
     arrays = arrays_x + arrays_z
-    token = pl.BlockSpec((1, HALF, N_BLOCK), lambda n, at: (k, 0, n))
-    out = pl.BlockSpec((2 * RH, N_BLOCK), lambda n, at: (0, n))
+    token = pl.BlockSpec((1, HALF, width), lambda n, at: (k, 0, n))
+    out = pl.BlockSpec((2 * RH, width), lambda n, at: (0, n))
     counts = (len(arrays_x), len(arrays_z))
     return pl.pallas_call(
         functools.partial(grads_kernel, (places_x, places_z), counts, n),
         out_shape=[shape(FF, D)] * n,
         grid_spec=pltpu.PrefetchScalarGridSpec(
             num_scalar_prefetch=1,
-            grid=(D // N_BLOCK,),
+            grid=(D // width,),
             in_specs=[pl.BlockSpec(memory_space=pl.ANY)] * len(arrays) + [token] * 2,
             out_specs=[out] * n,
             scratch_shapes=[
                 *[pltpu.VMEM((2 * RH, T), BF)] * n,
-                pltpu.VMEM((T, N_BLOCK), BF),
+                pltpu.VMEM((T, width), BF),
                 pltpu.SemaphoreType.DMA((2, n, 8)),
             ],
         ),

time: 262 us -> 263 us (level)
  no operation moved by 1% of the time
where the time goes in v4:
time: 263 us
  waiting for transfers between devices  124 us (47%)
  Pallas kernels  73.3 us (28%)
  starting transfers between devices  58.2 us (22%)
  local copies, waits for them, and re-layouts  3.56 us (1%)
  other arithmetic  3.03 us (1%)
    ppermute x25, waiting for transfers between devices, narrow_move(): return lax.ppermute(value, 'narrow', pairs)  106 us
    ppermute x25, starting transfers between devices, narrow_move(): return lax.ppermute(value, 'narrow', pairs)  35.8 us
    pallas_call x5, Pallas kernels, first(): pl.pallas_call(functools.partial(first_kernel, which, slots, layout, len(...  31 us
    pallas_call x2, Pallas kernels, grads(): pl.pallas_call(functools.partial(grads_kernel, (places_x, places_z), coun...  23.9 us
    ppermute x14, starting transfers between devices, wide_move(): return lax.ppermute(value, 'wide', pairs)  22.4 us
    ppermute x14, waiting for transfers between devices, wide_move(): return lax.ppermute(value, 'wide', pairs)  17.2 us
    pallas_call x1, Pallas kernels, back(): pl.pallas_call(functools.partial(back_kernel, (places_x, places_z), count...  14 us
  transfers between devices with their start and end apart: 39, of which 20 were waited for; matrix products, arithmetic and copies ran while one was open for 1% of the time, Pallas kernels for 16%

profile of v4, /device:TPU:1, one launch (start us, length us, event | category | flops | bytes accessed | tf_op | source)
XLA Modules:
  0.0 262.8 jit_solution(15173882547549985178)
XLA Ops:
  0.6 2.1 collective-permute-start
  2.8 1.3 collective-permute-start.6
  4.0 2.6 collective-permute-start.5
  8.9 3.0 %collective-permute-done.5 = bf16[64,1024]{1,0:T(8,128)(2,1)S(1)} collective-permute-done((bf16[64,1024]{1,0:T(8,128)(2,1)}, bf16[64,1024]{1,0:T(8,128)(2,1)S(1)}, u32[]{:S(2)}, u32[]{:S(2)}) %collective-permute-start.5) | collective-permute-done | bytes 131104 | tf_op jit(solution)/shard_map/ppermute | solution.py:60
  13.5 2.1 collective-permute-start.2
  16.5 1.4 collective-permute-done.1
  18.0 2.4 collective-permute-done.2
  20.3 6.2 %collective-permute-done.3 = bf16[128,1024]{1,0:T(8,128)(2,1)S(1)} collective-permute-done((bf16[128,1024]{1,0:T(8,128)(2,1)S(1)}, bf16[128,1024]{1,0:T(8,128)(2,1)S(1)}, u32[]{:S(2)}, u32[]{:S(2)}) %collective-permute-start.3) | collective-permute-done | bytes 262176 | tf_op jit(solution)/shard_map/ppermute | solution.py:60
  27.0 2.9 %collective-permute-start.8 = (bf16[2,512,1024]{2,1,0:T(8,128)(2,1)S(1)}, bf16[2,512,1024]{2,1,0:T(8,128)(2,1)}, u32[]{:S(2)}, u32[]{:S(2)}) collective-permute-start(bf16[2,512,1024]{2,1,0:T(8,128)(2,1)S(1)} %pad_maximum_fusion.refs_0_.refs_11_), channel_id=1, source_target_pairs={{0,8},{8,0},{16,24},{24,16},{32,40},{40,32},{48,56},{56,48},{64,72... | collective-permute-start | bytes 6291464 | tf_op jit(solution)/shard_map/ppermute | solution.py:60
  29.9 3.8 %collective-permute-done.8.refs_1_.refs_12_ = bf16[2,512,1024]{2,1,0:T(8,128)(2,1)} collective-permute-done((bf16[2,512,1024]{2,1,0:T(8,128)(2,1)S(1)}, bf16[2,512,1024]{2,1,0:T(8,128)(2,1)}, u32[]{:S(2)}, u32[]{:S(2)}) %collective-permute-start.8) | collective-permute-done | bytes 2097184 | tf_op jit(solution)/shard_map/ppermute | solution.py:60
  33.7 12.7 %far.1 = (bf16[3,928,128]{2,1,0:T(8,128)(2,1)S(1)}, bf16[3,928,128]{2,1,0:T(8,128)(2,1)S(1)}, bf16[3,928,128]{2,1,0:T(8,128)(2,1)S(1)}, bf16[3,928,128]{2,1,0:T(8,128)(2,1)S(1)}) custom-call(s32[2]{0:T(128)S(1)} %pad_add_fusion.at, bf16[2,512,1024]{2,1,0:T(8,128)(2,1)S(1)} %pad_maximum_fusion.refs_0_.refs_11_, ...), custom_call_target="tpu_custom_call" | custom-call | flops 2919235584 | bytes 14254080 | tf_op jit(solution)/shard_map/far/pallas_call | solution.py:125
  46.4 1.9 collective-permute-start.15
  48.3 2.2 collective-permute-start.16
  50.5 2.7 %collective-permute-start.12 = (bf16[3,928,128]{2,1,0:T(8,128)(2,1)S(1)}, bf16[3,928,128]{2,1,0:T(8,128)(2,1)S(1)}, u32[]{:S(2)}, u32[]{:S(2)}) collective-permute-start(bf16[3,928,128]{2,1,0:T(8,128)(2,1)S(1)} %get-tuple-element.46), channel_id=1, source_target_pairs={{0,4},{1,5},{2,6},{3,7},{4,0},{5,1},{6,2},{7,3},{8,12},{9,13},{10,... | collective-permute-start | bytes 2138120 | tf_op jit(solution)/shard_map/ppermute | solution.py:50
  53.2 2.1 copy-done.2
  55.3 3.8 %send.1 = bf16[2,3,928,128]{3,2,1,0:T(8,128)(2,1)S(1)} custom-call(s32[2]{0:T(128)S(1)} %pad_add_fusion.at, bf16[2,512,1024]{2,1,0:T(8,128)(2,1)S(1)} %pad_maximum_fusion.refs_0_.refs_11_, bf16[2,512,1024]{2,1,0:T(8,128)(2,1)} %collective-permute-done.8.refs_1_.refs_12_, bf16[1848,1024]{1,0:T(8,128)(2,1)S(1)} %bitcast.36, bf16[1848,1024]{1,0:T(8,128)(2,1)S(1)} %bitcast.42, ...), custom_call_target="tpu_custom_call" | custom-call | flops 1459617792 | bytes 7127040 | tf_op jit(solution)/shard_map/send/pallas_call | solution.py:125
  59.3 5.5 %mid.1 = (bf16[2,3,928,128]{3,2,1,0:T(8,128)(2,1)S(1)}, bf16[2,3,928,128]{3,2,1,0:T(8,128)(2,1)S(1)}) custom-call(s32[2]{0:T(128)S(1)} %pad_add_fusion.at, bf16[2,512,1024]{2,1,0:T(8,128)(2,1)S(1)} %pad_maximum_fusion.refs_0_.refs_11_, bf16[2,512,1024]{2,1,0:T(8,128)(2,1)} %collective-permute-done.8.refs_1_.refs_12_, bf16[1848,1024]{1,0:T(8,128)(2,1)S(1)} %bitcast.37, ...), custom_call_target="tpu_custom_call" | custom-call | flops 2919235584 | bytes 8552448 | tf_op jit(solution)/shard_map/mid/pallas_call | solution.py:125
  64.8 1.7 collective-permute-done.15.refs_1_
  67.5 1.4 collective-permute-done.12.refs_1_
  68.9 2.7 %collective-permute-start.18 = (bf16[2,3,928,128]{3,2,1,0:T(8,128)(2,1)S(1)}, bf16[2,3,928,128]{3,2,1,0:T(8,128)(2,1)S(1)}, u32[]{:S(2)}, u32[]{:S(2)}) collective-permute-start(bf16[2,3,928,128]{3,2,1,0:T(8,128)(2,1)S(1)} %get-tuple-element.54), channel_id=1, source_target_pairs={{0,3},{1,0},{2,1},{3,2},{4,7},{5,4},{6,5},{7,6},{8,11},{9,8},{10,9... | collective-permute-start | bytes 4276232 | tf_op jit(solution)/shard_map/ppermute | solution.py:50
  71.6 5.3 %keep.1 = (bf16[3,928,128]{2,1,0:T(8,128)(2,1)S(1)}, bf16[3,3,928,128]{3,2,1,0:T(8,128)(2,1)S(1)}) custom-call(s32[2]{0:T(128)S(1)} %pad_add_fusion.at, bf16[2,512,1024]{2,1,0:T(8,128)(2,1)S(1)} %pad_maximum_fusion.refs_0_.refs_11_, bf16[2,512,1024]{2,1,0:T(8,128)(2,1)} %collective-permute-done.8.refs_1_.refs_12_, bf16[1848,1024]{1,0:T(8,128)(2,1)S(1)} %bitcast.38, ...), custom_call_target="tpu_custom_call" | custom-call | flops 2919235584 | bytes 8552448 | tf_op jit(solution)/shard_map/keep/pallas_call | solution.py:125
  76.9 3.3 %collective-permute-start.9 = (bf16[3,928,128]{2,1,0:T(8,128)(2,1)S(1)}, bf16[3,928,128]{2,1,0:T(8,128)(2,1)S(1)}, u32[]{:S(2)}, u32[]{:S(2)}) collective-permute-start(bf16[3,928,128]{2,1,0:T(8,128)(2,1)S(1)} %get-tuple-element.43), channel_id=1, source_target_pairs={{0,4},{1,5},{2,6},{3,7},{4,0},{5,1},{6,2},{7,3},{8,12},{9,13},{10,... | collective-permute-start | bytes 2138120 | tf_op jit(solution)/shard_map/ppermute | solution.py:50
  80.2 3.7 %own.1.refs_0_.refs_5_ = bf16[2,3,928,128]{3,2,1,0:T(8,128)(2,1)S(1)} custom-call(s32[2]{0:T(128)S(1)} %pad_add_fusion.at, bf16[2,512,1024]{2,1,0:T(8,128)(2,1)S(1)} %pad_maximum_fusion.refs_0_.refs_11_, bf16[2,512,1024]{2,1,0:T(8,128)(2,1)} %collective-permute-done.8.refs_1_.refs_12_, bf16[1848,1024]{1,0:T(8,128)(2,1)S(1)} %bitcast.39, ...), custom_call_target="tpu_custom_call" | custom-call | flops 1459617792 | bytes 7127040 | tf_op jit(solution)/shard_map/own/pallas_call | solution.py:125
  84.4 15.1 %collective-permute-done.10.refs_1_ = bf16[2,3,928,128]{3,2,1,0:T(8,128)(2,1)S(1)} collective-permute-done((bf16[2,3,928,128]{3,2,1,0:T(8,128)(2,1)S(1)}, bf16[2,3,928,128]{3,2,1,0:T(8,128)(2,1)S(1)}, u32[]{:S(2)}, u32[]{:S(2)}) %collective-permute-start.10) | collective-permute-done | bytes 1425440 | tf_op jit(solution)/shard_map/ppermute | solution.py:50
  101.3 1.6 collective-permute-start.14
  103.4 2.8 %collective-permute-start.19 = (bf16[3,928,128]{2,1,0:T(8,128)(2,1)S(1)}, bf16[3,928,128]{2,1,0:T(8,128)(2,1)S(1)}, u32[]{:S(2)}, u32[]{:S(2)}) collective-permute-start(bf16[3,928,128]{2,1,0:T(8,128)(2,1)S(1)} %z_far.1), channel_id=1, source_target_pairs={{0,4},{1,5},{2,6},{3,7},{4,0},{5,1},{6,2},{7,3},{8,12},{9,13},{10,... | collective-permute-start | bytes 2138120 | tf_op jit(solution)/shard_map/ppermute | solution.py:50
  106.2 8.5 %collective-permute-done.9.refs_1_ = bf16[3,928,128]{2,1,0:T(8,128)(2,1)S(1)} collective-permute-done((bf16[3,928,128]{2,1,0:T(8,128)(2,1)S(1)}, bf16[3,928,128]{2,1,0:T(8,128)(2,1)S(1)}, u32[]{:S(2)}, u32[]{:S(2)}) %collective-permute-start.9) | collective-permute-done | bytes 712736 | tf_op jit(solution)/shard_map/ppermute | solution.py:50
  114.7 17.6 %collective-permute-done.11.refs_2_ = bf16[3,928,128]{2,1,0:T(8,128)(2,1)S(1)} collective-permute-done((bf16[3,928,128]{2,1,0:T(8,128)(2,1)S(1)}, bf16[3,928,128]{2,1,0:T(8,128)(2,1)S(1)}, u32[]{:S(2)}, u32[]{:S(2)}) %collective-permute-start.11) | collective-permute-done | bytes 712736 | tf_op jit(solution)/shard_map/ppermute | solution.py:50
  132.3 1.8 swiglu.1
  134.1 2.7 %collective-permute-start.20 = (bf16[2,3,928,128]{3,2,1,0:T(8,128)(2,1)S(1)}, bf16[2,3,928,128]{3,2,1,0:T(8,128)(2,1)S(1)}, u32[]{:S(2)}, u32[]{:S(2)}) collective-permute-start(bf16[2,3,928,128]{3,2,1,0:T(8,128)(2,1)S(1)} %get-tuple-element.55), channel_id=1, source_target_pairs={{0,4},{1,5},{2,6},{3,7},{4,0},{5,1},{6,2},{7,3},{8,12},{9,13},{10,... | collective-permute-start | bytes 4276232 | tf_op jit(solution)/shard_map/ppermute | solution.py:50
  136.9 2.7 %collective-permute-start.22 = (bf16[3,928,128]{2,1,0:T(8,128)(2,1)S(1)}, bf16[3,928,128]{2,1,0:T(8,128)(2,1)S(1)}, u32[]{:S(2)}, u32[]{:S(2)}) collective-permute-start(bf16[3,928,128]{2,1,0:T(8,128)(2,1)S(1)} %get-tuple-element.56.refs_0_), channel_id=1, source_target_pairs={{0,3},{1,0},{2,1},{3,2},{4,7},{5,4},{6,5},{7,6},{8,11},{9,8},{10,9... | collective-permute-start | bytes 2138120 | tf_op jit(solution)/shard_map/ppermute | solution.py:50
  140.6 12.6 %collective-permute-done.21.refs_3_ = bf16[3,928,128]{2,1,0:T(8,128)(2,1)S(1)} collective-permute-done((bf16[3,928,128]{2,1,0:T(8,128)(2,1)S(1)}, bf16[3,928,128]{2,1,0:T(8,128)(2,1)S(1)}, u32[]{:S(2)}, u32[]{:S(2)}) %collective-permute-start.21) | collective-permute-done | bytes 712736 | tf_op jit(solution)/shard_map/ppermute | solution.py:50
  153.2 13.2 %collective-permute-done.20.refs_4_ = bf16[2,3,928,128]{3,2,1,0:T(8,128)(2,1)S(1)} collective-permute-done((bf16[2,3,928,128]{3,2,1,0:T(8,128)(2,1)S(1)}, bf16[2,3,928,128]{3,2,1,0:T(8,128)(2,1)S(1)}, u32[]{:S(2)}, u32[]{:S(2)}) %collective-permute-start.20) | collective-permute-done | bytes 1425440 | tf_op jit(solution)/shard_map/ppermute | solution.py:50
  166.6 2.7 %collective-permute-done.23.refs_2_ = bf16[3,928,128]{2,1,0:T(8,128)(2,1)S(1)} collective-permute-done((bf16[3,928,128]{2,1,0:T(8,128)(2,1)S(1)}, bf16[3,928,128]{2,1,0:T(8,128)(2,1)S(1)}, u32[]{:S(2)}, u32[]{:S(2)}) %collective-permute-start.23) | collective-permute-done | bytes 712736 | tf_op jit(solution)/shard_map/ppermute | solution.py:50
  169.8 2.1 collective-permute-start.25
  172.7 16.7 %collective-permute-done.24.refs_10_ = bf16[2,2,928,128]{3,2,1,0:T(8,128)(2,1)S(1)} collective-permute-done((bf16[2,2,928,128]{3,2,1,0:T(8,128)(2,1)S(1)}, bf16[2,2,928,128]{3,2,1,0:T(8,128)(2,1)S(1)}, u32[]{:S(2)}, u32[]{:S(2)}) %collective-permute-start.24) | collective-permute-done | bytes 950304 | tf_op jit(solution)/shard_map/ppermute | solution.py:50
  189.7 2.4 collective-permute-start.27
  192.3 2.9 %collective-permute-start.30 = (bf16[2,928,128]{2,1,0:T(8,128)(2,1)S(1)}, bf16[2,928,128]{2,1,0:T(8,128)(2,1)S(1)}, u32[]{:S(2)}, u32[]{:S(2)}) collective-permute-start(bf16[2,928,128]{2,1,0:T(8,128)(2,1)S(1)} %slice_bitcast_fusion), channel_id=1, source_target_pairs={{0,3},{1,0},{2,1},{3,2},{4,7},{5,4},{6,5},{7,6},{8,11},{9,8},{10,9... | collective-permute-start | bytes 1425416 | tf_op jit(solution)/shard_map/ppermute | solution.py:50
  195.2 3.5 %collective-permute-done.26.refs_10_ = bf16[2,1,928,128]{3,2,1,0:T(8,128)(2,1)S(1)} collective-permute-done((bf16[2,1,928,128]{3,2,1,0:T(8,128)(2,1)S(1)}, bf16[2,1,928,128]{3,2,1,0:T(8,128)(2,1)S(1)}, u32[]{:S(2)}, u32[]{:S(2)}) %collective-permute-start.26) | collective-permute-done | bytes 475168 | tf_op jit(solution)/shard_map/ppermute | solution.py:50
  198.8 3.6 %collective-permute-done.28.refs_5_ = bf16[3,2,928,128]{3,2,1,0:T(8,128)(2,1)S(1)} collective-permute-done((bf16[3,2,928,128]{3,2,1,0:T(8,128)(2,1)S(1)}, bf16[3,2,928,128]{3,2,1,0:T(8,128)(2,1)S(1)}, u32[]{:S(2)}, u32[]{:S(2)}) %collective-permute-start.28) | collective-permute-done | bytes 1425440 | tf_op jit(solution)/shard_map/ppermute | solution.py:50
  202.3 6.6 %collective-permute-done.29.refs_6_ = bf16[2,928,128]{2,1,0:T(8,128)(2,1)S(1)} collective-permute-done((bf16[2,928,128]{2,1,0:T(8,128)(2,1)S(1)}, bf16[2,928,128]{2,1,0:T(8,128)(2,1)S(1)}, u32[]{:S(2)}, u32[]{:S(2)}) %collective-permute-start.29) | collective-permute-done | bytes 475168 | tf_op jit(solution)/shard_map/ppermute | solution.py:50
  208.9 14.0 %back.1 = (bf16[512,1024]{1,0:T(8,128)(2,1)S(1)}, bf16[512,1024]{1,0:T(8,128)(2,1)S(1)}) custom-call(s32[2]{0:T(128)S(1)} %pad_add_fusion.at, bf16[3,928,128]{2,1,0:T(8,128)(2,1)S(1)} %get-tuple-element.56.refs_0_, bf16[3,928,128]{2,1,0:T(8,128)(2,1)S(1)} %collective-permute-done.22.refs_1_, bf16[3,928,128]{2,1,0:T(8,128)(2,1)S(1)} %collective-permute-done.23.refs_2_, ...), custom_call_target="tpu_custom_call" | custom-call | flops 7751073792 | bytes 17235968 | tf_op jit(solution)/shard_map/back/pallas_call | solution.py:300
  223.0 5.5 %collective-permute-start.31 = (bf16[512,1024]{1,0:T(8,128)(2,1)S(1)}, bf16[512,1024]{1,0:T(8,128)(2,1)S(1)}, u32[]{:S(2)}, u32[]{:S(2)}) collective-permute-start(bf16[512,1024]{1,0:T(8,128)(2,1)S(1)} %get-tuple-element.63), channel_id=1, source_target_pairs={{0,8},{8,0},{16,24},{24,16},{32,40},{40,32},{48,56},{56,48},{64,72... | collective-permute-start | bytes 3145736 | tf_op jit(solution)/shard_map/ppermute | solution.py:60
  229.1 2.4 collective-permute-start.37
  232.3 1.7 collective-permute-start.34
  235.1 2.2 collective-permute-done.36.refs_6_
  237.8 15.0 %grads.1 = (bf16[1848,1024]{1,0:T(8,128)(2,1)}, bf16[1848,1024]{1,0:T(8,128)(2,1)}) custom-call(s32[2]{0:T(128)S(1)} %pad_add_fusion.at, bf16[3,928,128]{2,1,0:T(8,128)(2,1)S(1)} %get-tuple-element.56.refs_0_, bf16[3,928,128]{2,1,0:T(8,128)(2,1)S(1)} %collective-permute-done.22.refs_1_, bf16[3,928,128]{2,1,0:T(8,128)(2,1)S(1)} %collective-permute-done.23.refs_2_, ...), custom_call_target="tpu_custom_call" | custom-call | flops 7751073792 | bytes 17235968 | tf_op jit(solution)/shard_map/grads/pallas_call | solution.py:353
  253.2 8.9 %down.1 = bf16[1848,1024]{1,0:T(8,128)(2,1)} custom-call(s32[2]{0:T(128)S(1)} %pad_add_fusion.at, bf16[3,928,128]{2,1,0:T(8,128)(2,1)S(1)} %get-tuple-element.56.refs_0_, bf16[3,928,128]{2,1,0:T(8,128)(2,1)S(1)} %collective-permute-done.22.refs_1_, bf16[3,928,128]{2,1,0:T(8,128)(2,1)S(1)} %collective-permute-done.23.refs_2_, ...), custom_call_target="tpu_custom_call" | custom-call | flops 3875536896 | bytes 9666560 | tf_op jit(solution)/shard_map/down/pallas_call | solution.py:353
  (84 shorter events, 16.1 us)
Async XLA Ops:
  0.6 8.0 %collective-permute-start = (bf16[64,1024]{1,0:T(8,128)(2,1)}, bf16[64,1024]{1,0:T(8,128)(2,1)S(1)}, u32[]{:S(2)}, u32[]{:S(2)}) collective-permute-start(bf16[64,1024]{1,0:T(8,128)(2,1)} %param.5), channel_id=1, source_target_pairs={{0,16},{8,24},{16,0},{24,8},{32,48},{40,56},{48,32},{56,40},{64,80... | collective-permute-start | bytes 393224 | tf_op jit(solution)/shard_map/ppermute | solution.py:60
  2.8 6.2 %collective-permute-start.6 = (bf16[64,1024]{1,0:T(8,128)(2,1)}, bf16[64,1024]{1,0:T(8,128)(2,1)S(1)}, u32[]{:S(2)}, u32[]{:S(2)}) collective-permute-start(bf16[64,1024]{1,0:T(8,128)(2,1)} %param.6), channel_id=1, source_target_pairs={{0,32},{8,40},{16,48},{24,56},{32,64},{40,72},{48,80},{56,88},{64,... | collective-permute-start | bytes 393224 | tf_op jit(solution)/shard_map/ppermute | solution.py:60
  4.0 7.9 %collective-permute-start.5 = (bf16[64,1024]{1,0:T(8,128)(2,1)}, bf16[64,1024]{1,0:T(8,128)(2,1)S(1)}, u32[]{:S(2)}, u32[]{:S(2)}) collective-permute-start(bf16[64,1024]{1,0:T(8,128)(2,1)} %param.6), channel_id=1, source_target_pairs={{0,64},{8,72},{16,80},{24,88},{32,96},{40,104},{48,112},{56,120},{... | collective-permute-start | bytes 393224 | tf_op jit(solution)/shard_map/ppermute | solution.py:60
  6.7 5.6 %collective-permute-start.4 = (bf16[64,1024]{1,0:T(8,128)(2,1)}, bf16[64,1024]{1,0:T(8,128)(2,1)S(1)}, u32[]{:S(2)}, u32[]{:S(2)}) collective-permute-start(bf16[64,1024]{1,0:T(8,128)(2,1)} %param.6), channel_id=1, source_target_pairs={{0,96},{8,104},{16,112},{24,120},{32,0},{40,8},{48,16},{56,24},{64... | collective-permute-start | bytes 393224 | tf_op jit(solution)/shard_map/ppermute | solution.py:60
  8.7 9.2 %collective-permute-start.1 = (bf16[128,1024]{1,0:T(8,128)(2,1)S(1)}, bf16[128,1024]{1,0:T(8,128)(2,1)S(1)}, u32[]{:S(2)}, u32[]{:S(2)}) collective-permute-start(bf16[128,1024]{1,0:T(8,128)(2,1)S(1)} %get-tuple-element.77), channel_id=1, source_target_pairs={{0,96},{8,104},{16,112},{24,120},{32,0},{40,8},{48,16},{56,24},{64... | collective-permute-start | bytes 786440 | tf_op jit(solution)/shard_map/ppermute | solution.py:60
  13.3 13.3 %collective-permute-start.7 = (bf16[4,64,1024]{2,1,0:T(8,128)(2,1)S(1)}, bf16[4,64,1024]{2,1,0:T(8,128)(2,1)S(1)}, u32[]{:S(2)}, u32[]{:S(2)}) collective-permute-start(bf16[4,64,1024]{2,1,0:T(8,128)(2,1)S(1)} %get-tuple-element.76), channel_id=1, source_target_pairs={{0,16},{8,24},{16,0},{24,8},{32,48},{40,56},{48,32},{56,40},{64,80... | collective-permute-start | bytes 1572872 | tf_op jit(solution)/shard_map/ppermute | solution.py:60
  13.5 6.9 %collective-permute-start.2 = (bf16[128,1024]{1,0:T(8,128)(2,1)S(1)}, bf16[128,1024]{1,0:T(8,128)(2,1)S(1)}, u32[]{:S(2)}, u32[]{:S(2)}) collective-permute-start(bf16[128,1024]{1,0:T(8,128)(2,1)S(1)} %get-tuple-element.77), channel_id=1, source_target_pairs={{0,64},{8,72},{16,80},{24,88},{32,96},{40,104},{48,112},{56,120},{... | collective-permute-start | bytes 786440 | tf_op jit(solution)/shard_map/ppermute | solution.py:60
  15.5 11.0 %collective-permute-start.3 = (bf16[128,1024]{1,0:T(8,128)(2,1)S(1)}, bf16[128,1024]{1,0:T(8,128)(2,1)S(1)}, u32[]{:S(2)}, u32[]{:S(2)}) collective-permute-start(bf16[128,1024]{1,0:T(8,128)(2,1)S(1)} %get-tuple-element.77), channel_id=1, source_target_pairs={{0,32},{8,40},{16,48},{24,56},{32,64},{40,72},{48,80},{56,88},{64,... | collective-permute-start | bytes 786440 | tf_op jit(solution)/shard_map/ppermute | solution.py:60
  27.0 6.8 %collective-permute-start.8 = (bf16[2,512,1024]{2,1,0:T(8,128)(2,1)S(1)}, bf16[2,512,1024]{2,1,0:T(8,128)(2,1)}, u32[]{:S(2)}, u32[]{:S(2)}) collective-permute-start(bf16[2,512,1024]{2,1,0:T(8,128)(2,1)S(1)} %pad_maximum_fusion.refs_0_.refs_11_), channel_id=1, source_target_pairs={{0,8},{8,0},{16,24},{24,16},{32,40},{40,32},{48,56},{56,48},{64,72... | collective-permute-start | bytes 6291464 | tf_op jit(solution)/shard_map/ppermute | solution.py:60
  33.7 19.5 %copy-start = (bf16[1848,1024]{1,0:T(8,128)(2,1)S(1)}, bf16[1848,1024]{1,0:T(8,128)(2,1)}, u32[]{:S(2)}) copy-start(bf16[1848,1024]{1,0:T(8,128)(2,1)} %refs_4_.9) | copy-start | bytes 11354116
  33.7 19.5 %copy-start.1 = (bf16[1024,1848]{0,1:T(8,128)(2,1)S(1)}, bf16[1024,1848]{0,1:T(8,128)(2,1)}, u32[]{:S(2)}) copy-start(bf16[1024,1848]{0,1:T(8,128)(2,1)} %param.7) | copy-start | bytes 11354116
  46.4 20.1 %collective-permute-start.15 = (bf16[3,928,128]{2,1,0:T(8,128)(2,1)S(1)}, bf16[3,928,128]{2,1,0:T(8,128)(2,1)S(1)}, u32[]{:S(2)}, u32[]{:S(2)}) collective-permute-start(bf16[3,928,128]{2,1,0:T(8,128)(2,1)S(1)} %get-tuple-element.37), channel_id=1, source_target_pairs={{0,1},{1,2},{2,3},{3,0},{4,5},{5,6},{6,7},{7,4},{8,9},{9,10},{10,1... | collective-permute-start | bytes 2138120 | tf_op jit(solution)/shard_map/ppermute | solution.py:50
  48.3 18.2 %collective-permute-start.16 = (bf16[3,928,128]{2,1,0:T(8,128)(2,1)S(1)}, bf16[3,928,128]{2,1,0:T(8,128)(2,1)S(1)}, u32[]{:S(2)}, u32[]{:S(2)}) collective-permute-start(bf16[3,928,128]{2,1,0:T(8,128)(2,1)S(1)} %get-tuple-element.50), channel_id=1, source_target_pairs={{0,3},{1,0},{2,1},{3,2},{4,7},{5,4},{6,5},{7,6},{8,11},{9,8},{10,9... | collective-permute-start | bytes 2138120 | tf_op jit(solution)/shard_map/ppermute | solution.py:50
  50.5 18.4 %collective-permute-start.12 = (bf16[3,928,128]{2,1,0:T(8,128)(2,1)S(1)}, bf16[3,928,128]{2,1,0:T(8,128)(2,1)S(1)}, u32[]{:S(2)}, u32[]{:S(2)}) collective-permute-start(bf16[3,928,128]{2,1,0:T(8,128)(2,1)S(1)} %get-tuple-element.46), channel_id=1, source_target_pairs={{0,4},{1,5},{2,6},{3,7},{4,0},{5,1},{6,2},{7,3},{8,12},{9,13},{10,... | collective-permute-start | bytes 2138120 | tf_op jit(solution)/shard_map/ppermute | solution.py:50
  53.2 2.1 copy-start.2
  59.2 40.3 %collective-permute-start.10 = (bf16[2,3,928,128]{3,2,1,0:T(8,128)(2,1)S(1)}, bf16[2,3,928,128]{3,2,1,0:T(8,128)(2,1)S(1)}, u32[]{:S(2)}, u32[]{:S(2)}) collective-permute-start(bf16[2,3,928,128]{3,2,1,0:T(8,128)(2,1)S(1)} %send.1), channel_id=1, source_target_pairs={{0,4},{1,5},{2,6},{3,7},{4,0},{5,1},{6,2},{7,3},{8,12},{9,13},{10,... | collective-permute-start | bytes 4276232 | tf_op jit(solution)/shard_map/ppermute | solution.py:50
  68.9 32.4 %collective-permute-start.17 = (bf16[2,3,928,128]{3,2,1,0:T(8,128)(2,1)S(1)}, bf16[2,3,928,128]{3,2,1,0:T(8,128)(2,1)S(1)}, u32[]{:S(2)}, u32[]{:S(2)}) collective-permute-start(bf16[2,3,928,128]{3,2,1,0:T(8,128)(2,1)S(1)} %get-tuple-element.52), channel_id=1, source_target_pairs={{0,1},{1,2},{2,3},{3,0},{4,5},{5,6},{6,7},{7,4},{8,9},{9,10},{10,1... | collective-permute-start | bytes 4276232 | tf_op jit(solution)/shard_map/ppermute | solution.py:50
  68.9 34.0 %collective-permute-start.18 = (bf16[2,3,928,128]{3,2,1,0:T(8,128)(2,1)S(1)}, bf16[2,3,928,128]{3,2,1,0:T(8,128)(2,1)S(1)}, u32[]{:S(2)}, u32[]{:S(2)}) collective-permute-start(bf16[2,3,928,128]{3,2,1,0:T(8,128)(2,1)S(1)} %get-tuple-element.54), channel_id=1, source_target_pairs={{0,3},{1,0},{2,1},{3,2},{4,7},{5,4},{6,5},{7,6},{8,11},{9,8},{10,9... | collective-permute-start | bytes 4276232 | tf_op jit(solution)/shard_map/ppermute | solution.py:50
  76.9 37.9 %collective-permute-start.9 = (bf16[3,928,128]{2,1,0:T(8,128)(2,1)S(1)}, bf16[3,928,128]{2,1,0:T(8,128)(2,1)S(1)}, u32[]{:S(2)}, u32[]{:S(2)}) collective-permute-start(bf16[3,928,128]{2,1,0:T(8,128)(2,1)S(1)} %get-tuple-element.43), channel_id=1, source_target_pairs={{0,4},{1,5},{2,6},{3,7},{4,0},{5,1},{6,2},{7,3},{8,12},{9,13},{10,... | collective-permute-start | bytes 2138120 | tf_op jit(solution)/shard_map/ppermute | solution.py:50
  84.3 30.4 %collective-permute-start.13 = (bf16[3,928,128]{2,1,0:T(8,128)(2,1)S(1)}, bf16[3,928,128]{2,1,0:T(8,128)(2,1)S(1)}, u32[]{:S(2)}, u32[]{:S(2)}) collective-permute-start(bf16[3,928,128]{2,1,0:T(8,128)(2,1)S(1)} %x_sum1.1), channel_id=1, source_target_pairs={{0,2},{1,3},{2,0},{3,1},{4,6},{5,7},{6,4},{7,5},{8,10},{9,11},{10,... | collective-permute-start | bytes 2138120 | tf_op jit(solution)/shard_map/ppermute | solution.py:50
  100.2 32.1 %collective-permute-start.11 = (bf16[3,928,128]{2,1,0:T(8,128)(2,1)S(1)}, bf16[3,928,128]{2,1,0:T(8,128)(2,1)S(1)}, u32[]{:S(2)}, u32[]{:S(2)}) collective-permute-start(bf16[3,928,128]{2,1,0:T(8,128)(2,1)S(1)} %get-tuple-element.44), channel_id=1, source_target_pairs={{0,1},{1,2},{2,3},{3,0},{4,5},{5,6},{6,7},{7,4},{8,9},{9,10},{10,1... | collective-permute-start | bytes 2138120 | tf_op jit(solution)/shard_map/ppermute | solution.py:50
  101.3 31.0 %collective-permute-start.14 = (bf16[3,928,128]{2,1,0:T(8,128)(2,1)S(1)}, bf16[3,928,128]{2,1,0:T(8,128)(2,1)S(1)}, u32[]{:S(2)}, u32[]{:S(2)}) collective-permute-start(bf16[3,928,128]{2,1,0:T(8,128)(2,1)S(1)} %get-tuple-element.47), channel_id=1, source_target_pairs={{0,3},{1,0},{2,1},{3,2},{4,7},{5,4},{6,5},{7,6},{8,11},{9,8},{10,9... | collective-permute-start | bytes 2138120 | tf_op jit(solution)/shard_map/ppermute | solution.py:50
  103.4 28.9 %collective-permute-start.19 = (bf16[3,928,128]{2,1,0:T(8,128)(2,1)S(1)}, bf16[3,928,128]{2,1,0:T(8,128)(2,1)S(1)}, u32[]{:S(2)}, u32[]{:S(2)}) collective-permute-start(bf16[3,928,128]{2,1,0:T(8,128)(2,1)S(1)} %z_far.1), channel_id=1, source_target_pairs={{0,4},{1,5},{2,6},{3,7},{4,0},{5,1},{6,2},{7,3},{8,12},{9,13},{10,... | collective-permute-start | bytes 2138120 | tf_op jit(solution)/shard_map/ppermute | solution.py:50
  134.1 32.3 %collective-permute-start.20 = (bf16[2,3,928,128]{3,2,1,0:T(8,128)(2,1)S(1)}, bf16[2,3,928,128]{3,2,1,0:T(8,128)(2,1)S(1)}, u32[]{:S(2)}, u32[]{:S(2)}) collective-permute-start(bf16[2,3,928,128]{3,2,1,0:T(8,128)(2,1)S(1)} %get-tuple-element.55), channel_id=1, source_target_pairs={{0,4},{1,5},{2,6},{3,7},{4,0},{5,1},{6,2},{7,3},{8,12},{9,13},{10,... | collective-permute-start | bytes 4276232 | tf_op jit(solution)/shard_map/ppermute | solution.py:50
  136.9 16.3 %collective-permute-start.21 = (bf16[3,928,128]{2,1,0:T(8,128)(2,1)S(1)}, bf16[3,928,128]{2,1,0:T(8,128)(2,1)S(1)}, u32[]{:S(2)}, u32[]{:S(2)}) collective-permute-start(bf16[3,928,128]{2,1,0:T(8,128)(2,1)S(1)} %get-tuple-element.56.refs_0_), channel_id=1, source_target_pairs={{0,1},{1,2},{2,3},{3,0},{4,5},{5,6},{6,7},{7,4},{8,9},{9,10},{10,1... | collective-permute-start | bytes 2138120 | tf_op jit(solution)/shard_map/ppermute | solution.py:50
  136.9 29.7 %collective-permute-start.22 = (bf16[3,928,128]{2,1,0:T(8,128)(2,1)S(1)}, bf16[3,928,128]{2,1,0:T(8,128)(2,1)S(1)}, u32[]{:S(2)}, u32[]{:S(2)}) collective-permute-start(bf16[3,928,128]{2,1,0:T(8,128)(2,1)S(1)} %get-tuple-element.56.refs_0_), channel_id=1, source_target_pairs={{0,3},{1,0},{2,1},{3,2},{4,7},{5,4},{6,5},{7,6},{8,11},{9,8},{10,9... | collective-permute-start | bytes 2138120 | tf_op jit(solution)/shard_map/ppermute | solution.py:50
  139.6 29.7 %collective-permute-start.23 = (bf16[3,928,128]{2,1,0:T(8,128)(2,1)S(1)}, bf16[3,928,128]{2,1,0:T(8,128)(2,1)S(1)}, u32[]{:S(2)}, u32[]{:S(2)}) collective-permute-start(bf16[3,928,128]{2,1,0:T(8,128)(2,1)S(1)} %get-tuple-element.56.refs_0_), channel_id=1, source_target_pairs={{0,2},{1,3},{2,0},{3,1},{4,6},{5,7},{6,4},{7,5},{8,10},{9,11},{10,... | collective-permute-start | bytes 2138120 | tf_op jit(solution)/shard_map/ppermute | solution.py:50
  169.3 20.2 %collective-permute-start.24 = (bf16[2,2,928,128]{3,2,1,0:T(8,128)(2,1)S(1)}, bf16[2,2,928,128]{3,2,1,0:T(8,128)(2,1)S(1)}, u32[]{:S(2)}, u32[]{:S(2)}) collective-permute-start(bf16[2,2,928,128]{3,2,1,0:T(8,128)(2,1)S(1)} %pad_maximum_fusion.3.refs_8_), channel_id=1, source_target_pairs={{0,1},{1,2},{2,3},{3,0},{4,5},{5,6},{6,7},{7,4},{8,9},{9,10},{10,1... | collective-permute-start | bytes 2850824 | tf_op jit(solution)/shard_map/ppermute | solution.py:50
  169.8 19.6 %collective-permute-start.25 = (bf16[2,2,928,128]{3,2,1,0:T(8,128)(2,1)S(1)}, bf16[2,2,928,128]{3,2,1,0:T(8,128)(2,1)S(1)}, u32[]{:S(2)}, u32[]{:S(2)}) collective-permute-start(bf16[2,2,928,128]{3,2,1,0:T(8,128)(2,1)S(1)} %pad_maximum_fusion.3.refs_8_), channel_id=1, source_target_pairs={{0,3},{1,0},{2,1},{3,2},{4,7},{5,4},{6,5},{7,6},{8,11},{9,8},{10,9... | collective-permute-start | bytes 2850824 | tf_op jit(solution)/shard_map/ppermute | solution.py:50
  172.2 30.2 %collective-permute-start.28 = (bf16[3,2,928,128]{3,2,1,0:T(8,128)(2,1)S(1)}, bf16[3,2,928,128]{3,2,1,0:T(8,128)(2,1)S(1)}, u32[]{:S(2)}, u32[]{:S(2)}) collective-permute-start(bf16[3,2,928,128]{3,2,1,0:T(8,128)(2,1)S(1)} %pad_maximum_fusion.1), channel_id=1, source_target_pairs={{0,4},{1,5},{2,6},{3,7},{4,0},{5,1},{6,2},{7,3},{8,12},{9,13},{10,... | collective-permute-start | bytes 4276232 | tf_op jit(solution)/shard_map/ppermute | solution.py:50
  172.6 36.3 %copy-start.3 = (bf16[1024,1848]{0,1:T(8,128)(2,1)S(1)}, bf16[1024,1848]{0,1:T(8,128)(2,1)}, u32[]{:S(2)}) copy-start(bf16[1024,1848]{0,1:T(8,128)(2,1)} %param.8) | copy-start | bytes 11354116
  189.4 9.3 %collective-permute-start.26 = (bf16[2,1,928,128]{3,2,1,0:T(8,128)(2,1)S(1)}, bf16[2,1,928,128]{3,2,1,0:T(8,128)(2,1)S(1)}, u32[]{:S(2)}, u32[]{:S(2)}) collective-permute-start(bf16[2,1,928,128]{3,2,1,0:T(8,128)(2,1)S(1)} %pad_maximum_fusion.6.refs_8_), channel_id=1, source_target_pairs={{0,1},{1,2},{2,3},{3,0},{4,5},{5,6},{6,7},{7,4},{8,9},{9,10},{10,1... | collective-permute-start | bytes 1425416 | tf_op jit(solution)/shard_map/ppermute | solution.py:50
  189.7 9.1 %collective-permute-start.27 = (bf16[2,1,928,128]{3,2,1,0:T(8,128)(2,1)S(1)}, bf16[2,1,928,128]{3,2,1,0:T(8,128)(2,1)S(1)}, u32[]{:S(2)}, u32[]{:S(2)}) collective-permute-start(bf16[2,1,928,128]{3,2,1,0:T(8,128)(2,1)S(1)} %pad_maximum_fusion.6.refs_8_), channel_id=1, source_target_pairs={{0,3},{1,0},{2,1},{3,2},{4,7},{5,4},{6,5},{7,6},{8,11},{9,8},{10,9... | collective-permute-start | bytes 1425416 | tf_op jit(solution)/shard_map/ppermute | solution.py:50
  192.2 16.8 %collective-permute-start.29 = (bf16[2,928,128]{2,1,0:T(8,128)(2,1)S(1)}, bf16[2,928,128]{2,1,0:T(8,128)(2,1)S(1)}, u32[]{:S(2)}, u32[]{:S(2)}) collective-permute-start(bf16[2,928,128]{2,1,0:T(8,128)(2,1)S(1)} %slice_bitcast_fusion.1), channel_id=1, source_target_pairs={{0,1},{1,2},{2,3},{3,0},{4,5},{5,6},{6,7},{7,4},{8,9},{9,10},{10,1... | collective-permute-start | bytes 1425416 | tf_op jit(solution)/shard_map/ppermute | solution.py:50
  192.3 16.7 %collective-permute-start.30 = (bf16[2,928,128]{2,1,0:T(8,128)(2,1)S(1)}, bf16[2,928,128]{2,1,0:T(8,128)(2,1)S(1)}, u32[]{:S(2)}, u32[]{:S(2)}) collective-permute-start(bf16[2,928,128]{2,1,0:T(8,128)(2,1)S(1)} %slice_bitcast_fusion), channel_id=1, source_target_pairs={{0,3},{1,0},{2,1},{3,2},{4,7},{5,4},{6,5},{7,6},{8,11},{9,8},{10,9... | collective-permute-start | bytes 1425416 | tf_op jit(solution)/shard_map/ppermute | solution.py:50
  223.0 8.8 %collective-permute-start.31 = (bf16[512,1024]{1,0:T(8,128)(2,1)S(1)}, bf16[512,1024]{1,0:T(8,128)(2,1)S(1)}, u32[]{:S(2)}, u32[]{:S(2)}) collective-permute-start(bf16[512,1024]{1,0:T(8,128)(2,1)S(1)} %get-tuple-element.63), channel_id=1, source_target_pairs={{0,8},{8,0},{16,24},{24,16},{32,40},{40,32},{48,56},{56,48},{64,72... | collective-permute-start | bytes 3145736 | tf_op jit(solution)/shard_map/ppermute | solution.py:60
  228.6 8.7 %collective-permute-start.36 = (bf16[1,928,128]{2,1,0:T(8,128)(2,1)S(1)}, bf16[1,928,128]{2,1,0:T(8,128)(2,1)S(1)}, u32[]{:S(2)}, u32[]{:S(2)}) collective-permute-start(bf16[1,928,128]{2,1,0:T(8,128)(2,1)S(1)} %slice_bitcast_fusion.9), channel_id=1, source_target_pairs={{0,1},{1,2},{2,3},{3,0},{4,5},{5,6},{6,7},{7,4},{8,9},{9,10},{10,1... | collective-permute-start | bytes 712712 | tf_op jit(solution)/shard_map/ppermute | solution.py:50
  229.1 8.7 %collective-permute-start.37 = (bf16[1,928,128]{2,1,0:T(8,128)(2,1)S(1)}, bf16[1,928,128]{2,1,0:T(8,128)(2,1)S(1)}, u32[]{:S(2)}, u32[]{:S(2)}) collective-permute-start(bf16[1,928,128]{2,1,0:T(8,128)(2,1)S(1)} %slice_bitcast_fusion.8), channel_id=1, source_target_pairs={{0,3},{1,0},{2,1},{3,2},{4,7},{5,4},{6,5},{7,6},{8,11},{9,8},{10,9... | collective-permute-start | bytes 712712 | tf_op jit(solution)/shard_map/ppermute | solution.py:50
  231.4 21.8 %collective-permute-start.38 = (bf16[3,1,928,128]{3,2,1,0:T(8,128)(2,1)S(1)}, bf16[3,1,928,128]{3,2,1,0:T(8,128)(2,1)S(1)}, u32[]{:S(2)}, u32[]{:S(2)}) collective-permute-start(bf16[3,1,928,128]{3,2,1,0:T(8,128)(2,1)S(1)} %pad_maximum_fusion.4), channel_id=1, source_target_pairs={{0,4},{1,5},{2,6},{3,7},{4,0},{5,1},{6,2},{7,3},{8,12},{9,13},{10,... | collective-permute-start | bytes 2138120 | tf_op jit(solution)/shard_map/ppermute | solution.py:50
  232.3 20.4 %collective-permute-start.34 = (bf16[128,1024]{1,0:T(8,128)(2,1)S(1)}, bf16[128,1024]{1,0:T(8,128)(2,1)S(1)}, u32[]{:S(2)}, u32[]{:S(2)}) collective-permute-start(bf16[128,1024]{1,0:T(8,128)(2,1)S(1)} %get-tuple-element.73), channel_id=1, source_target_pairs={{0,64},{8,72},{16,80},{24,88},{32,96},{40,104},{48,112},{56,120},{... | collective-permute-start | bytes 786440 | tf_op jit(solution)/shard_map/ppermute | solution.py:60
  234.0 18.7 %collective-permute-start.33 = (bf16[128,1024]{1,0:T(8,128)(2,1)S(1)}, bf16[128,1024]{1,0:T(8,128)(2,1)S(1)}, u32[]{:S(2)}, u32[]{:S(2)}) collective-permute-start(bf16[128,1024]{1,0:T(8,128)(2,1)S(1)} %get-tuple-element.74), channel_id=1, source_target_pairs={{0,96},{8,104},{16,112},{24,120},{32,0},{40,8},{48,16},{56,24},{64... | collective-permute-start | bytes 786440 | tf_op jit(solution)/shard_map/ppermute | solution.py:60
  237.3 15.5 %collective-permute-start.32 = (bf16[128,1024]{1,0:T(8,128)(2,1)S(1)}, bf16[128,1024]{1,0:T(8,128)(2,1)S(1)}, u32[]{:S(2)}, u32[]{:S(2)}) collective-permute-start(bf16[128,1024]{1,0:T(8,128)(2,1)S(1)} %get-tuple-element.72), channel_id=1, source_target_pairs={{0,32},{8,40},{16,48},{24,56},{32,64},{40,72},{48,80},{56,88},{64,... | collective-permute-start | bytes 786440 | tf_op jit(solution)/shard_map/ppermute | solution.py:60
  252.9 9.2 %collective-permute-start.35 = (bf16[64,1024]{1,0:T(8,128)(2,1)S(1)}, bf16[64,1024]{1,0:T(8,128)(2,1)S(1)}, u32[]{:S(2)}, u32[]{:S(2)}) collective-permute-start(bf16[64,1024]{1,0:T(8,128)(2,1)S(1)} %slice.121), channel_id=1, source_target_pairs={{0,16},{8,24},{16,0},{24,8},{32,48},{40,56},{48,32},{56,40},{64,80... | collective-permute-start | bytes 393224 | tf_op jit(solution)/shard_map/ppermute | solution.py:60
